TPU v7x, 32 devices: a whole 2x2x4 slice. The times are simulated.
32 devices in a mesh: ty: 8 (over z, x), tx: 4 (over y, core).
Axes of the slice: x: 2, y: 2, z: 4, core: 2. Of those that a mesh axis runs over, the one named last changes fastest.
Arguments:
- stored_eastward_flow: float32 [30, 64, 512], P(None, 'ty', 'tx'), may hold values from -6 to 6
- stored_northward_flow: float32 [30, 64, 512], P(None, 'ty', 'tx'), may hold values from -6 to 6
- stored_heat_content: float32 [30, 64, 512], P(None, 'ty', 'tx'), may hold values from -6 to 6
- ocean_layer_tally: int32 [64, 512], P('ty', 'tx'), may hold values from 0 to 30, as said below
- eastward_flow_sensitivity: float32 [30, 64, 512], P(None, 'ty', 'tx'), may hold values from -6 to 6
- northward_flow_sensitivity: float32 [30, 64, 512], P(None, 'ty', 'tx'), may hold values from -6 to 6
- scalar_content_sensitivity: float32 [30, 64, 512], P(None, 'ty', 'tx'), may hold values from -6 to 6
- elevation_sensitivity: float32 [64, 512], P('ty', 'tx'), may hold values from -6 to 6
Outputs:
- u_gradient: float32 [30, 64, 512], P(None, 'ty', 'tx')
- v_gradient: float32 [30, 64, 512], P(None, 'ty', 'tx')
- t_gradient: float32 [30, 64, 512], P(None, 'ty', 'tx')
- eta_gradient: float32 [64, 512], P('ty', 'tx')
Inputs may be any that keep to these rules, and one draw needn't show every extreme that they name: `ocean_layer_tally`: the number of wet levels of each column; 0 marks land.
All inputs are finite; a program needn't handle non-finite values.
Results may differ from a plain program's by a relative error of at most 0.0001.
Values sent between devices are 32-bit elements; how exact they have to be, the bound alone decides.
No kernel may reach another device: no remote copies, remote signals or barrier semaphores. Data moves between devices by JAX's collectives and lax.ppermute only.
A program may use at most 64 MiB of HBM per device.

v0:
```python
import jax
import jax.numpy as jnp
from jax import lax
from jax.sharding import PartitionSpec as P

ITERS = 4


ADVECT = 0.1
GRAVITY_DT = 0.1
STEP_DT = 1.0


def padded(array, sides, width):
    for axis, dim in sides:
        size, length = (lax.axis_size(axis), array.shape[dim])
        up = [(i, (i + 1) % size) for i in range(size - 1)]
        down = [(j, i) for i, j in up]
        last = lax.slice_in_dim(array, length - width, length, axis=dim)
        first = lax.slice_in_dim(array, 0, width, axis=dim)
        before = lax.ppermute(last, axis, up)
        after = lax.ppermute(first, axis, down)
        array = jnp.concatenate([before, array, after], axis=dim)
    return array


def wet_cells(count_float, levels):
    level_index = jnp.arange(levels).astype(jnp.float32)
    return (level_index[:, None, None] < count_float[None]).astype(jnp.float32)


def tendencies(u_input, v_input, t_input, wet_cell, coriolis_u, coriolis_v):
    row_count = u_input.shape[1] - 4
    col_count = u_input.shape[2] - 4

    def offset_view(source, shift_row, shift_col):
        return source[
            :, 2 + shift_row : 2 + shift_row + row_count, 2 + shift_col : 2 + shift_col + col_count
        ]

    def mask_u(shift_row, shift_col):
        return offset_view(wet_cell, shift_row, shift_col) * offset_view(
            wet_cell, shift_row, shift_col - 1
        )

    def mask_v(shift_row, shift_col):
        return offset_view(wet_cell, shift_row, shift_col) * offset_view(
            wet_cell, shift_row - 1, shift_col
        )

    def flux_x(shift_col):
        face_value = (
            7.0 * (offset_view(t_input, 0, shift_col) + offset_view(t_input, 0, shift_col - 1))
            - (offset_view(t_input, 0, shift_col + 1) + offset_view(t_input, 0, shift_col - 2))
        ) / 12.0
        return mask_u(0, shift_col) * offset_view(u_input, 0, shift_col) * face_value

    def flux_y(shift_row):
        face_value = (
            7.0 * (offset_view(t_input, shift_row, 0) + offset_view(t_input, shift_row - 1, 0))
            - (offset_view(t_input, shift_row + 1, 0) + offset_view(t_input, shift_row - 2, 0))
        ) / 12.0
        return mask_v(shift_row, 0) * offset_view(v_input, shift_row, 0) * face_value

    t_new = offset_view(t_input, 0, 0) - ADVECT * offset_view(wet_cell, 0, 0) * (
        flux_x(1) - flux_x(0) + flux_y(1) - flux_y(0)
    )
    u_here = offset_view(u_input, 0, 0)
    v_here = offset_view(v_input, 0, 0)
    v_bar = 0.25 * (
        v_here
        + offset_view(v_input, 1, 0)
        + offset_view(v_input, 0, -1)
        + offset_view(v_input, 1, -1)
    )
    u_bar = 0.25 * (
        u_here
        + offset_view(u_input, 0, 1)
        + offset_view(u_input, -1, 0)
        + offset_view(u_input, -1, 1)
    )
    u_star = u_here + ADVECT * mask_u(0, 0) * (
        coriolis_u * v_bar
        - u_here * 0.5 * (offset_view(u_input, 0, 1) - offset_view(u_input, 0, -1))
        - v_bar * 0.5 * (offset_view(u_input, 1, 0) - offset_view(u_input, -1, 0))
    )
    v_star = v_here + ADVECT * mask_v(0, 0) * (
        -coriolis_v * u_bar
        - u_bar * 0.5 * (offset_view(v_input, 0, 1) - offset_view(v_input, 0, -1))
        - v_here * 0.5 * (offset_view(v_input, 1, 0) - offset_view(v_input, -1, 0))
    )
    return (u_star, v_star, t_new)


def surface_apply(rimmed, depth_u, depth_v):
    centre = rimmed[1:-1, 1:-1]
    east = rimmed[1:-1, 2:]
    west = rimmed[1:-1, :-2]
    north = rimmed[2:, 1:-1]
    south = rimmed[:-2, 1:-1]
    return centre - GRAVITY_DT * STEP_DT * (
        depth_u[1:-1, 2:] * (east - centre)
        - depth_u[1:-1, 1:-1] * (centre - west)
        + depth_v[2:, 1:-1] * (north - centre)
        - depth_v[1:-1, 1:-1] * (centre - south)
    )


def surface_rim(stacked_fields):
    return padded(stacked_fields, (("ty", 1), ("tx", 2)), 1)


def operate(direction, depth_u, depth_v):
    return surface_apply(surface_rim(direction[None])[0], depth_u, depth_v)


def two_products(residual, applied):
    return lax.psum((jnp.sum(residual * residual), jnp.sum(residual * applied)), ("ty", "tx"))


def solve_surface(surface_load, depth_u, depth_v):
    solution = jnp.zeros_like(surface_load)
    residual = surface_load
    applied = operate(residual, depth_u, depth_v)
    norm_now, product = two_products(residual, applied)
    step_length = norm_now / product
    direction = residual
    along = applied
    for iteration in range(ITERS):
        solution = solution + step_length * direction
        residual = residual - step_length * along
        if iteration + 1 < ITERS:
            applied = operate(residual, depth_u, depth_v)
            norm_next, product = two_products(residual, applied)
            beta_ratio = norm_next / norm_now
            step_length = norm_next / (product - beta_ratio * norm_next / step_length)
            direction = residual + beta_ratio * direction
            along = applied + beta_ratio * along
            norm_now = norm_next
    return solution


def on_device(
    stored_eastward_flow,
    stored_northward_flow,
    stored_heat_content,
    ocean_layer_tally,
    eastward_flow_sensitivity,
    northward_flow_sensitivity,
    scalar_content_sensitivity,
    elevation_sensitivity,
):
    levels, row_count, col_count = stored_eastward_flow.shape
    total_rows = row_count * lax.axis_size("ty")
    first_row = (lax.axis_index("ty") * row_count).astype(jnp.float32)
    thickness = (1.0 + jnp.arange(levels).astype(jnp.float32) / levels)[:, None, None]
    layer_number_map = ocean_layer_tally.astype(jnp.float32)[None]
    stacked_fields = jnp.concatenate(
        [stored_eastward_flow, stored_northward_flow, stored_heat_content, layer_number_map], axis=0
    )
    widened = padded(stacked_fields, (("ty", 1), ("tx", 2)), 4)
    u_wide = widened[0:levels]
    v_wide = widened[levels : 2 * levels]
    t_wide = widened[2 * levels : 3 * levels]
    wet_wide = wet_cells(widened[-1], levels)
    inner_wet = wet_wide[:, 3:-3, 3:-3]
    u_mask = inner_wet * wet_wide[:, 3:-3, 2:-4]
    v_mask = inner_wet * wet_wide[:, 2:-4, 3:-3]
    depth_u = jnp.sum(thickness * u_mask, axis=0)
    depth_v = jnp.sum(thickness * v_mask, axis=0)
    col_own = jnp.stack(
        [
            jnp.sum(u_mask[:, 1:-1, 1:-1] * eastward_flow_sensitivity, axis=0),
            jnp.sum(v_mask[:, 1:-1, 1:-1] * northward_flow_sensitivity, axis=0),
        ]
    )
    col_rimmed = surface_rim(col_own)
    col_u = col_rimmed[0]
    col_v = col_rimmed[1]
    surface_load = elevation_sensitivity + GRAVITY_DT * (
        col_u[1:-1, 2:] - col_u[1:-1, 1:-1] + col_v[2:, 1:-1] - col_v[1:-1, 1:-1]
    )
    solution = solve_surface(surface_load, depth_u, depth_v)
    solution_rimmed = surface_rim(solution[None])[0]
    u_own = (
        eastward_flow_sensitivity
        + STEP_DT
        * thickness
        * u_mask[:, 1:-1, 1:-1]
        * (solution - solution_rimmed[1:-1, :-2])[None]
    )
    v_own = (
        northward_flow_sensitivity
        + STEP_DT
        * thickness
        * v_mask[:, 1:-1, 1:-1]
        * (solution - solution_rimmed[:-2, 1:-1])[None]
    )
    cotangent_wide = padded(
        jnp.concatenate([u_own, v_own, scalar_content_sensitivity], axis=0),
        (("ty", 1), ("tx", 2)),
        2,
    )
    u_cotangent = cotangent_wide[0:levels]
    v_cotangent = cotangent_wide[levels : 2 * levels]
    t_cotangent = cotangent_wide[2 * levels : 3 * levels]
    row_global = first_row - 2.0 + jnp.arange(row_count + 4).astype(jnp.float32)
    coriolis_u = (0.5 + (row_global + 0.5) / total_rows)[:, None]
    coriolis_v = (0.5 + row_global / total_rows)[:, None]

    def advance_ocean_once(u_input, v_input, t_input):
        return tendencies(u_input, v_input, t_input, wet_wide, coriolis_u, coriolis_v)

    advance_results, backward_chain_rule = jax.vjp(advance_ocean_once, u_wide, v_wide, t_wide)
    gradients = backward_chain_rule((u_cotangent, v_cotangent, t_cotangent))
    return (
        gradients[0][:, 4:-4, 4:-4],
        gradients[1][:, 4:-4, 4:-4],
        gradients[2][:, 4:-4, 4:-4],
        solution,
    )


def solution(mesh):
    placed = (
        P(None, "ty", "tx"),
        P(None, "ty", "tx"),
        P(None, "ty", "tx"),
        P("ty", "tx"),
        P(None, "ty", "tx"),
        P(None, "ty", "tx"),
        P(None, "ty", "tx"),
        P("ty", "tx"),
    )
    return jax.shard_map(
        on_device,
        mesh=mesh,
        in_specs=placed,
        out_specs=(P(None, "ty", "tx"), P(None, "ty", "tx"), P(None, "ty", "tx"), P("ty", "tx")),
        check_vma=False,
    )
```

profile of v0, /device:TPU:11, one launch (start us, length us, event | category | flops | bytes accessed | tf_op | source)
XLA Modules:
  0.0 350.7 jit_solution(4662864517402132491)
XLA Ops:
  2.5 3.2 collective-permute-start
  5.7 2.1 collective-permute-start.1
  7.8 2.1 collective-permute-done
  10.0 4.0 %collective-permute-done.1 = f32[91,4,128]{2,1,0:T(4,128)S(1)} collective-permute-done((f32[91,4,128]{2,1,0:T(4,128)S(1)}, f32[91,4,128]{2,1,0:T(4,128)S(1)}, u32[]{:S(2)}, u32[]{:S(2)}) %collective-permute-start.1) | collective-permute-done | bytes 186400 | tf_op jit(solution)/shard_map/ppermute | solution.py:22
  15.4 3.5 %collective-permute-start.3 = (f32[91,16,4]{0,1,2:T(8,128)S(1)}, f32[91,16,4]{0,1,2:T(8,128)S(1)}, u32[]{:S(2)}, u32[]{:S(2)}) collective-permute-start(f32[91,16,4]{0,1,2:T(8,128)S(1)} %copy.27), channel_id=1, source_target_pairs={{1,0},{2,1},{3,2},{5,4},{6,5},{7,6},{9,8},{10,9},{11,10},{13,12},{... | collective-permute-start | bytes 69896 | tf_op jit(solution)/shard_map/ppermute | solution.py:22
  18.9 3.0 collective-permute-start.2
  23.9 2.1 pad_maximum_fusion
  27.6 4.1 %collective-permute-start.4 = (f32[2,1,128]{2,1,0:T(1,128)S(1)}, f32[2,1,128]{2,1,0:T(1,128)S(1)}, u32[]{:S(2)}, u32[]{:S(2)}) collective-permute-start(f32[2,1,128]{2,1,0:T(1,128)S(1)} %get-tuple-element.98), channel_id=1, source_target_pairs={{0,4},{4,8},{8,12},{12,16},{16,20},{20,24},{24,28},{1,5},{5,9},{9,... | collective-permute-start | bytes 3080 | tf_op jit(solution)/shard_map/ppermute | solution.py:21
  31.7 1.9 collective-permute-start.5
  33.6 3.4 collective-permute-done.5
  37.1 5.5 %collective-permute-start.6 = (f32[2,10,1]{2,1,0:T(8,128)S(1)}, f32[2,10,1]{2,1,0:T(8,128)S(1)}, u32[]{:S(2)}, u32[]{:S(2)}) collective-permute-start(f32[2,10,1]{2,1,0:T(8,128)S(1)} %get-tuple-element.86), channel_id=1, source_target_pairs={{0,1},{1,2},{2,3},{4,5},{5,6},{6,7},{8,9},{9,10},{10,11},{12,13},{... | collective-permute-start | bytes 248 | tf_op jit(solution)/shard_map/ppermute | solution.py:21
  42.6 1.9 collective-permute-start.7
  44.6 3.1 collective-permute-done.7
  47.9 1.9 collective-permute-start.8
  49.8 3.4 collective-permute-start.9
  53.2 1.9 collective-permute-done.9
  55.2 3.1 collective-permute-start.10
  58.3 1.9 collective-permute-start.11
  60.2 3.0 collective-permute-done.11
  64.0 37.4 %all-reduce.40 = (f32[]{:T(128)}, f32[]{:T(128)}) all-reduce(f32[]{:T(128)} %get-tuple-element.15, f32[]{:T(128)} %get-tuple-element.14), channel_id=1, replica_groups=mesh['ty'=8,'tx'=4] {'ty','tx'}, use_global_device_ids=true, to_apply=%region_3.0 | all-reduce | flops 2 | bytes 16 | tf_op jit(solution)/shard_map/psum | solution.py:118
  102.8 2.2 collective-permute-start.12
  105.0 3.1 collective-permute-start.13
  108.1 2.1 collective-permute-done.13
  110.3 6.7 %collective-permute-start.14 = (f32[1,10,1]{2,1,0:T(8,128)S(1)}, f32[1,10,1]{2,1,0:T(8,128)S(1)}, u32[]{:S(2)}, u32[]{:S(2)}) collective-permute-start(f32[1,10,1]{2,1,0:T(8,128)S(1)} %get-tuple-element.94), channel_id=1, source_target_pairs={{0,1},{1,2},{2,3},{4,5},{5,6},{6,7},{8,9},{9,10},{10,11},{12,13},{... | collective-permute-start | bytes 128 | tf_op jit(solution)/shard_map/ppermute | solution.py:21
  117.0 1.9 collective-permute-start.15
  118.9 3.0 collective-permute-done.15
  122.7 37.6 %all-reduce.39 = (f32[]{:T(128)}, f32[]{:T(128)}) all-reduce(f32[]{:T(128)} %get-tuple-element.13, f32[]{:T(128)} %get-tuple-element.12), channel_id=1, replica_groups=mesh['ty'=8,'tx'=4] {'ty','tx'}, use_global_device_ids=true, to_apply=%region_9.0 | all-reduce | flops 2 | bytes 16 | tf_op jit(solution)/shard_map/psum | solution.py:118
  164.9 2.7 collective-permute-start.16
  167.6 2.6 collective-permute-start.17
  170.2 2.6 collective-permute-done.17
  172.9 6.7 %collective-permute-start.18 = (f32[1,10,1]{2,1,0:T(8,128)S(1)}, f32[1,10,1]{2,1,0:T(8,128)S(1)}, u32[]{:S(2)}, u32[]{:S(2)}) collective-permute-start(f32[1,10,1]{2,1,0:T(8,128)S(1)} %get-tuple-element.92), channel_id=1, source_target_pairs={{0,1},{1,2},{2,3},{4,5},{5,6},{6,7},{8,9},{9,10},{10,11},{12,13},{... | collective-permute-start | bytes 128 | tf_op jit(solution)/shard_map/ppermute | solution.py:21
  179.6 1.9 collective-permute-start.19
  181.5 3.0 collective-permute-done.19
  185.3 37.1 %all-reduce.38 = (f32[]{:T(128)}, f32[]{:T(128)}) all-reduce(f32[]{:T(128)} %get-tuple-element.11, f32[]{:T(128)} %get-tuple-element.10), channel_id=1, replica_groups=mesh['ty'=8,'tx'=4] {'ty','tx'}, use_global_device_ids=true, to_apply=%region_13.0 | all-reduce | flops 2 | bytes 16 | tf_op jit(solution)/shard_map/psum | solution.py:118
  226.4 3.2 collective-permute-start.20
  229.6 2.1 collective-permute-start.21
  231.7 3.0 collective-permute-done.21
  234.8 6.7 %collective-permute-start.22 = (f32[1,10,1]{2,1,0:T(8,128)S(1)}, f32[1,10,1]{2,1,0:T(8,128)S(1)}, u32[]{:S(2)}, u32[]{:S(2)}) collective-permute-start(f32[1,10,1]{2,1,0:T(8,128)S(1)} %get-tuple-element.90), channel_id=1, source_target_pairs={{0,1},{1,2},{2,3},{4,5},{5,6},{6,7},{8,9},{9,10},{10,11},{12,13},{... | collective-permute-start | bytes 128 | tf_op jit(solution)/shard_map/ppermute | solution.py:21
  241.6 1.9 collective-permute-start.23
  243.5 3.0 collective-permute-done.23
  247.3 37.1 %all-reduce.37 = (f32[]{:T(128)}, f32[]{:T(128)}) all-reduce(f32[]{:T(128)} %get-tuple-element.9, f32[]{:T(128)} %get-tuple-element.8), channel_id=1, replica_groups=mesh['ty'=8,'tx'=4] {'ty','tx'}, use_global_device_ids=true, to_apply=%region_17.0 | all-reduce | flops 2 | bytes 16 | tf_op jit(solution)/shard_map/psum | solution.py:118
  288.4 3.2 collective-permute-start.24
  291.6 2.1 collective-permute-start.25
  293.7 3.0 collective-permute-done.25
  296.8 6.7 %collective-permute-start.26 = (f32[1,10,1]{2,1,0:T(8,128)S(1)}, f32[1,10,1]{2,1,0:T(8,128)S(1)}, u32[]{:S(2)}, u32[]{:S(2)}) collective-permute-start(f32[1,10,1]{2,1,0:T(8,128)S(1)} %get-tuple-element.88), channel_id=1, source_target_pairs={{0,1},{1,2},{2,3},{4,5},{5,6},{6,7},{8,9},{9,10},{10,11},{12,13},{... | collective-permute-start | bytes 128 | tf_op jit(solution)/shard_map/ppermute | solution.py:21
  303.5 1.9 collective-permute-start.27
  305.5 3.0 collective-permute-done.27
  308.7 1.5 multiply_add_fusion.1
  310.8 1.7 pad_maximum_fusion.19
  312.5 2.3 collective-permute-start.28
  314.8 3.0 collective-permute-start.29
  318.1 3.5 collective-permute-done.29
  321.5 1.2 pad_maximum_fusion.3
  322.8 1.3 fusion.90
  324.1 1.4 copy.30
  325.6 1.4 copy.31
  327.0 1.9 collective-permute-start.31
  328.9 3.8 %collective-permute-start.30 = (f32[90,12,2]{0,1,2:T(8,128)S(1)}, f32[90,12,2]{0,1,2:T(8,128)S(1)}, u32[]{:S(2)}, u32[]{:S(2)}) collective-permute-start(f32[90,12,2]{0,1,2:T(8,128)S(1)} %copy.30), channel_id=1, source_target_pairs={{0,1},{1,2},{2,3},{4,5},{5,6},{6,7},{8,9},{9,10},{10,11},{12,13},{... | collective-permute-start | bytes 25928 | tf_op jit(solution)/shard_map/ppermute | solution.py:21
  333.4 1.3 copy.32
  334.7 1.2 copy.33
  336.0 2.5 pad_maximum_fusion.1
  339.0 1.5 multiply_negate_fusion.2
  342.4 1.1 fusion.82
  344.4 1.4 pad_add_fusion
  (116 shorter events, 20.2 us)
Async XLA Ops:
  0.6 13.3 %copy-start = (f32[30,8,128]{2,1,0:T(8,128)S(1)}, f32[30,8,128]{2,1,0:T(8,128)}, u32[]{:S(2)}) copy-start(f32[30,8,128]{2,1,0:T(8,128)} %param.10) | copy-start | bytes 368644
  0.6 13.3 %copy-start.2 = (f32[30,8,128]{2,1,0:T(8,128)S(1)}, f32[30,8,128]{2,1,0:T(8,128)}, u32[]{:S(2)}) copy-start(f32[30,8,128]{2,1,0:T(8,128)} %param.9) | copy-start | bytes 368644
  0.7 13.3 %copy-start.4 = (f32[30,8,128]{2,1,0:T(8,128)S(1)}, f32[30,8,128]{2,1,0:T(8,128)}, u32[]{:S(2)}) copy-start(f32[30,8,128]{2,1,0:T(8,128)} %param.8) | copy-start | bytes 368644
  2.5 7.4 %collective-permute-start = (f32[91,4,128]{2,1,0:T(4,128)S(1)}, f32[91,4,128]{2,1,0:T(4,128)S(1)}, u32[]{:S(2)}, u32[]{:S(2)}) collective-permute-start(f32[91,4,128]{2,1,0:T(4,128)S(1)} %get-tuple-element.78), channel_id=1, source_target_pairs={{0,4},{4,8},{8,12},{12,16},{16,20},{20,24},{24,28},{1,5},{5,9},{9,... | collective-permute-start | bytes 559112 | tf_op jit(solution)/shard_map/ppermute | solution.py:21
  5.7 8.3 %collective-permute-start.1 = (f32[91,4,128]{2,1,0:T(4,128)S(1)}, f32[91,4,128]{2,1,0:T(4,128)S(1)}, u32[]{:S(2)}, u32[]{:S(2)}) collective-permute-start(f32[91,4,128]{2,1,0:T(4,128)S(1)} %get-tuple-element.79), channel_id=1, source_target_pairs={{4,0},{8,4},{12,8},{16,12},{20,16},{24,20},{28,24},{5,1},{9,5},{13... | collective-permute-start | bytes 559112 | tf_op jit(solution)/shard_map/ppermute | solution.py:22
  10.0 13.4 %copy-start.6 = (f32[91,4,128]{2,1,0:T(4,128)}, f32[91,4,128]{2,1,0:T(4,128)S(1)}, u32[]{:S(2)}) copy-start(f32[91,4,128]{2,1,0:T(4,128)S(1)} %collective-permute-done) | copy-start | bytes 559108
  14.0 0.7 copy-start.8
  15.4 8.0 %collective-permute-start.3 = (f32[91,16,4]{0,1,2:T(8,128)S(1)}, f32[91,16,4]{0,1,2:T(8,128)S(1)}, u32[]{:S(2)}, u32[]{:S(2)}) collective-permute-start(f32[91,16,4]{0,1,2:T(8,128)S(1)} %copy.27), channel_id=1, source_target_pairs={{1,0},{2,1},{3,2},{5,4},{6,5},{7,6},{9,8},{10,9},{11,10},{13,12},{... | collective-permute-start | bytes 69896 | tf_op jit(solution)/shard_map/ppermute | solution.py:22
  18.9 4.1 %collective-permute-start.2 = (f32[91,16,4]{0,1,2:T(8,128)S(1)}, f32[91,16,4]{0,1,2:T(8,128)S(1)}, u32[]{:S(2)}, u32[]{:S(2)}) collective-permute-start(f32[91,16,4]{0,1,2:T(8,128)S(1)} %copy.26), channel_id=1, source_target_pairs={{0,1},{1,2},{2,3},{4,5},{5,6},{6,7},{8,9},{9,10},{10,11},{12,13},{... | collective-permute-start | bytes 69896 | tf_op jit(solution)/shard_map/ppermute | solution.py:21
  26.0 1.4 copy-start.14
  26.0 1.4 copy-start.15
  26.1 21.7 %copy-start.17 = (f32[8,128]{1,0:T(8,128)S(1)}, f32[8,128]{1,0:T(8,128)}, u32[]{:S(2)}) copy-start(f32[8,128]{1,0:T(8,128)} %param.15) | copy-start | bytes 12292
  26.6 0.8 copy-start.12
  26.6 1.0 copy-start.13
  27.6 6.0 %collective-permute-start.4 = (f32[2,1,128]{2,1,0:T(1,128)S(1)}, f32[2,1,128]{2,1,0:T(1,128)S(1)}, u32[]{:S(2)}, u32[]{:S(2)}) collective-permute-start(f32[2,1,128]{2,1,0:T(1,128)S(1)} %get-tuple-element.98), channel_id=1, source_target_pairs={{0,4},{4,8},{8,12},{12,16},{16,20},{20,24},{24,28},{1,5},{5,9},{9,... | collective-permute-start | bytes 3080 | tf_op jit(solution)/shard_map/ppermute | solution.py:21
  31.7 5.3 %collective-permute-start.5 = (f32[2,1,128]{2,1,0:T(1,128)S(1)}, f32[2,1,128]{2,1,0:T(1,128)S(1)}, u32[]{:S(2)}, u32[]{:S(2)}) collective-permute-start(f32[2,1,128]{2,1,0:T(1,128)S(1)} %get-tuple-element.99), channel_id=1, source_target_pairs={{4,0},{8,4},{12,8},{16,12},{20,16},{24,20},{28,24},{5,1},{9,5},{13... | collective-permute-start | bytes 3080 | tf_op jit(solution)/shard_map/ppermute | solution.py:22
  37.1 7.5 %collective-permute-start.6 = (f32[2,10,1]{2,1,0:T(8,128)S(1)}, f32[2,10,1]{2,1,0:T(8,128)S(1)}, u32[]{:S(2)}, u32[]{:S(2)}) collective-permute-start(f32[2,10,1]{2,1,0:T(8,128)S(1)} %get-tuple-element.86), channel_id=1, source_target_pairs={{0,1},{1,2},{2,3},{4,5},{5,6},{6,7},{8,9},{9,10},{10,11},{12,13},{... | collective-permute-start | bytes 248 | tf_op jit(solution)/shard_map/ppermute | solution.py:21
  42.6 5.1 %collective-permute-start.7 = (f32[2,10,1]{2,1,0:T(8,128)S(1)}, f32[2,10,1]{2,1,0:T(8,128)S(1)}, u32[]{:S(2)}, u32[]{:S(2)}) collective-permute-start(f32[2,10,1]{2,1,0:T(8,128)S(1)} %get-tuple-element.87), channel_id=1, source_target_pairs={{1,0},{2,1},{3,2},{5,4},{6,5},{7,6},{9,8},{10,9},{11,10},{13,12},{... | collective-permute-start | bytes 248 | tf_op jit(solution)/shard_map/ppermute | solution.py:22
  47.9 5.3 %collective-permute-start.8 = (f32[1,1,128]{2,1,0:T(1,128)S(1)}, f32[1,1,128]{2,1,0:T(1,128)S(1)}, u32[]{:S(2)}, u32[]{:S(2)}) collective-permute-start(f32[1,1,128]{2,1,0:T(1,128)S(1)} %get-tuple-element.108), channel_id=1, source_target_pairs={{0,4},{4,8},{8,12},{12,16},{16,20},{20,24},{24,28},{1,5},{5,9},{9,... | collective-permute-start | bytes 1544 | tf_op jit(solution)/shard_map/ppermute | solution.py:21
  49.8 5.3 %collective-permute-start.9 = (f32[1,1,128]{2,1,0:T(1,128)S(1)}, f32[1,1,128]{2,1,0:T(1,128)S(1)}, u32[]{:S(2)}, u32[]{:S(2)}) collective-permute-start(f32[1,1,128]{2,1,0:T(1,128)S(1)} %get-tuple-element.109), channel_id=1, source_target_pairs={{4,0},{8,4},{12,8},{16,12},{20,16},{24,20},{28,24},{5,1},{9,5},{13... | collective-permute-start | bytes 1544 | tf_op jit(solution)/shard_map/ppermute | solution.py:22
  55.2 5.0 %collective-permute-start.10 = (f32[1,10,1]{2,1,0:T(8,128)S(1)}, f32[1,10,1]{2,1,0:T(8,128)S(1)}, u32[]{:S(2)}, u32[]{:S(2)}) collective-permute-start(f32[1,10,1]{2,1,0:T(8,128)S(1)} %get-tuple-element.96), channel_id=1, source_target_pairs={{0,1},{1,2},{2,3},{4,5},{5,6},{6,7},{8,9},{9,10},{10,11},{12,13},{... | collective-permute-start | bytes 128 | tf_op jit(solution)/shard_map/ppermute | solution.py:21
  58.3 5.0 %collective-permute-start.11 = (f32[1,10,1]{2,1,0:T(8,128)S(1)}, f32[1,10,1]{2,1,0:T(8,128)S(1)}, u32[]{:S(2)}, u32[]{:S(2)}) collective-permute-start(f32[1,10,1]{2,1,0:T(8,128)S(1)} %get-tuple-element.97), channel_id=1, source_target_pairs={{1,0},{2,1},{3,2},{5,4},{6,5},{7,6},{9,8},{10,9},{11,10},{13,12},{... | collective-permute-start | bytes 128 | tf_op jit(solution)/shard_map/ppermute | solution.py:22
  102.8 5.3 %collective-permute-start.12 = (f32[1,1,128]{2,1,0:T(1,128)S(1)}, f32[1,1,128]{2,1,0:T(1,128)S(1)}, u32[]{:S(2)}, u32[]{:S(2)}) collective-permute-start(f32[1,1,128]{2,1,0:T(1,128)S(1)} %get-tuple-element.106), channel_id=1, source_target_pairs={{0,4},{4,8},{8,12},{12,16},{16,20},{20,24},{24,28},{1,5},{5,9},{9,... | collective-permute-start | bytes 1544 | tf_op jit(solution)/shard_map/ppermute | solution.py:21
  105.0 5.2 %collective-permute-start.13 = (f32[1,1,128]{2,1,0:T(1,128)S(1)}, f32[1,1,128]{2,1,0:T(1,128)S(1)}, u32[]{:S(2)}, u32[]{:S(2)}) collective-permute-start(f32[1,1,128]{2,1,0:T(1,128)S(1)} %get-tuple-element.107), channel_id=1, source_target_pairs={{4,0},{8,4},{12,8},{16,12},{20,16},{24,20},{28,24},{5,1},{9,5},{13... | collective-permute-start | bytes 1544 | tf_op jit(solution)/shard_map/ppermute | solution.py:22
  110.3 8.6 %collective-permute-start.14 = (f32[1,10,1]{2,1,0:T(8,128)S(1)}, f32[1,10,1]{2,1,0:T(8,128)S(1)}, u32[]{:S(2)}, u32[]{:S(2)}) collective-permute-start(f32[1,10,1]{2,1,0:T(8,128)S(1)} %get-tuple-element.94), channel_id=1, source_target_pairs={{0,1},{1,2},{2,3},{4,5},{5,6},{6,7},{8,9},{9,10},{10,11},{12,13},{... | collective-permute-start | bytes 128 | tf_op jit(solution)/shard_map/ppermute | solution.py:21
  117.0 5.0 %collective-permute-start.15 = (f32[1,10,1]{2,1,0:T(8,128)S(1)}, f32[1,10,1]{2,1,0:T(8,128)S(1)}, u32[]{:S(2)}, u32[]{:S(2)}) collective-permute-start(f32[1,10,1]{2,1,0:T(8,128)S(1)} %get-tuple-element.95), channel_id=1, source_target_pairs={{1,0},{2,1},{3,2},{5,4},{6,5},{7,6},{9,8},{10,9},{11,10},{13,12},{... | collective-permute-start | bytes 128 | tf_op jit(solution)/shard_map/ppermute | solution.py:22
  164.9 5.3 %collective-permute-start.16 = (f32[1,1,128]{2,1,0:T(1,128)S(1)}, f32[1,1,128]{2,1,0:T(1,128)S(1)}, u32[]{:S(2)}, u32[]{:S(2)}) collective-permute-start(f32[1,1,128]{2,1,0:T(1,128)S(1)} %get-tuple-element.104), channel_id=1, source_target_pairs={{0,4},{4,8},{8,12},{12,16},{16,20},{20,24},{24,28},{1,5},{5,9},{9,... | collective-permute-start | bytes 1544 | tf_op jit(solution)/shard_map/ppermute | solution.py:21
  167.6 5.2 %collective-permute-start.17 = (f32[1,1,128]{2,1,0:T(1,128)S(1)}, f32[1,1,128]{2,1,0:T(1,128)S(1)}, u32[]{:S(2)}, u32[]{:S(2)}) collective-permute-start(f32[1,1,128]{2,1,0:T(1,128)S(1)} %get-tuple-element.105), channel_id=1, source_target_pairs={{4,0},{8,4},{12,8},{16,12},{20,16},{24,20},{28,24},{5,1},{9,5},{13... | collective-permute-start | bytes 1544 | tf_op jit(solution)/shard_map/ppermute | solution.py:22
  172.9 8.6 %collective-permute-start.18 = (f32[1,10,1]{2,1,0:T(8,128)S(1)}, f32[1,10,1]{2,1,0:T(8,128)S(1)}, u32[]{:S(2)}, u32[]{:S(2)}) collective-permute-start(f32[1,10,1]{2,1,0:T(8,128)S(1)} %get-tuple-element.92), channel_id=1, source_target_pairs={{0,1},{1,2},{2,3},{4,5},{5,6},{6,7},{8,9},{9,10},{10,11},{12,13},{... | collective-permute-start | bytes 128 | tf_op jit(solution)/shard_map/ppermute | solution.py:21
  179.6 5.0 %collective-permute-start.19 = (f32[1,10,1]{2,1,0:T(8,128)S(1)}, f32[1,10,1]{2,1,0:T(8,128)S(1)}, u32[]{:S(2)}, u32[]{:S(2)}) collective-permute-start(f32[1,10,1]{2,1,0:T(8,128)S(1)} %get-tuple-element.93), channel_id=1, source_target_pairs={{1,0},{2,1},{3,2},{5,4},{6,5},{7,6},{9,8},{10,9},{11,10},{13,12},{... | collective-permute-start | bytes 128 | tf_op jit(solution)/shard_map/ppermute | solution.py:22
  226.4 5.3 %collective-permute-start.20 = (f32[1,1,128]{2,1,0:T(1,128)S(1)}, f32[1,1,128]{2,1,0:T(1,128)S(1)}, u32[]{:S(2)}, u32[]{:S(2)}) collective-permute-start(f32[1,1,128]{2,1,0:T(1,128)S(1)} %get-tuple-element.102), channel_id=1, source_target_pairs={{0,4},{4,8},{8,12},{12,16},{16,20},{20,24},{24,28},{1,5},{5,9},{9,... | collective-permute-start | bytes 1544 | tf_op jit(solution)/shard_map/ppermute | solution.py:21
  229.6 5.2 %collective-permute-start.21 = (f32[1,1,128]{2,1,0:T(1,128)S(1)}, f32[1,1,128]{2,1,0:T(1,128)S(1)}, u32[]{:S(2)}, u32[]{:S(2)}) collective-permute-start(f32[1,1,128]{2,1,0:T(1,128)S(1)} %get-tuple-element.103), channel_id=1, source_target_pairs={{4,0},{8,4},{12,8},{16,12},{20,16},{24,20},{28,24},{5,1},{9,5},{13... | collective-permute-start | bytes 1544 | tf_op jit(solution)/shard_map/ppermute | solution.py:22
  234.8 8.6 %collective-permute-start.22 = (f32[1,10,1]{2,1,0:T(8,128)S(1)}, f32[1,10,1]{2,1,0:T(8,128)S(1)}, u32[]{:S(2)}, u32[]{:S(2)}) collective-permute-start(f32[1,10,1]{2,1,0:T(8,128)S(1)} %get-tuple-element.90), channel_id=1, source_target_pairs={{0,1},{1,2},{2,3},{4,5},{5,6},{6,7},{8,9},{9,10},{10,11},{12,13},{... | collective-permute-start | bytes 128 | tf_op jit(solution)/shard_map/ppermute | solution.py:21
  241.6 5.0 %collective-permute-start.23 = (f32[1,10,1]{2,1,0:T(8,128)S(1)}, f32[1,10,1]{2,1,0:T(8,128)S(1)}, u32[]{:S(2)}, u32[]{:S(2)}) collective-permute-start(f32[1,10,1]{2,1,0:T(8,128)S(1)} %get-tuple-element.91), channel_id=1, source_target_pairs={{1,0},{2,1},{3,2},{5,4},{6,5},{7,6},{9,8},{10,9},{11,10},{13,12},{... | collective-permute-start | bytes 128 | tf_op jit(solution)/shard_map/ppermute | solution.py:22
  288.4 35.7 %copy-start.16 = (f32[8,128]{1,0:T(8,128)}, f32[8,128]{1,0:T(8,128)S(1)}, u32[]{:S(2)}) copy-start(f32[8,128]{1,0:T(8,128)S(1)} %multiply_add_fusion.2) | copy-start | bytes 12292
  288.4 5.3 %collective-permute-start.24 = (f32[1,1,128]{2,1,0:T(1,128)S(1)}, f32[1,1,128]{2,1,0:T(1,128)S(1)}, u32[]{:S(2)}, u32[]{:S(2)}) collective-permute-start(f32[1,1,128]{2,1,0:T(1,128)S(1)} %get-tuple-element.100), channel_id=1, source_target_pairs={{0,4},{4,8},{8,12},{12,16},{16,20},{20,24},{24,28},{1,5},{5,9},{9,... | collective-permute-start | bytes 1544 | tf_op jit(solution)/shard_map/ppermute | solution.py:21
  291.6 5.2 %collective-permute-start.25 = (f32[1,1,128]{2,1,0:T(1,128)S(1)}, f32[1,1,128]{2,1,0:T(1,128)S(1)}, u32[]{:S(2)}, u32[]{:S(2)}) collective-permute-start(f32[1,1,128]{2,1,0:T(1,128)S(1)} %get-tuple-element.101), channel_id=1, source_target_pairs={{4,0},{8,4},{12,8},{16,12},{20,16},{24,20},{28,24},{5,1},{9,5},{13... | collective-permute-start | bytes 1544 | tf_op jit(solution)/shard_map/ppermute | solution.py:22
  296.8 8.6 %collective-permute-start.26 = (f32[1,10,1]{2,1,0:T(8,128)S(1)}, f32[1,10,1]{2,1,0:T(8,128)S(1)}, u32[]{:S(2)}, u32[]{:S(2)}) collective-permute-start(f32[1,10,1]{2,1,0:T(8,128)S(1)} %get-tuple-element.88), channel_id=1, source_target_pairs={{0,1},{1,2},{2,3},{4,5},{5,6},{6,7},{8,9},{9,10},{10,11},{12,13},{... | collective-permute-start | bytes 128 | tf_op jit(solution)/shard_map/ppermute | solution.py:21
  303.5 5.0 %collective-permute-start.27 = (f32[1,10,1]{2,1,0:T(8,128)S(1)}, f32[1,10,1]{2,1,0:T(8,128)S(1)}, u32[]{:S(2)}, u32[]{:S(2)}) collective-permute-start(f32[1,10,1]{2,1,0:T(8,128)S(1)} %get-tuple-element.89), channel_id=1, source_target_pairs={{1,0},{2,1},{3,2},{5,4},{6,5},{7,6},{9,8},{10,9},{11,10},{13,12},{... | collective-permute-start | bytes 128 | tf_op jit(solution)/shard_map/ppermute | solution.py:22
  310.1 0.7 copy-start.10
  310.1 2.3 copy-start.11
  312.5 5.6 %collective-permute-start.28 = (f32[90,2,128]{2,1,0:T(2,128)}, f32[90,2,128]{2,1,0:T(2,128)}, u32[]{:S(2)}, u32[]{:S(2)}) collective-permute-start(f32[90,2,128]{2,1,0:T(2,128)} %get-tuple-element.80), channel_id=1, source_target_pairs={{0,4},{4,8},{8,12},{12,16},{16,20},{20,24},{24,28},{1,5},{5,9},{9,... | collective-permute-start | bytes 276488 | tf_op jit(solution)/shard_map/ppermute | solution.py:21
  314.8 6.8 %collective-permute-start.29 = (f32[90,2,128]{2,1,0:T(2,128)}, f32[90,2,128]{2,1,0:T(2,128)}, u32[]{:S(2)}, u32[]{:S(2)}) collective-permute-start(f32[90,2,128]{2,1,0:T(2,128)} %get-tuple-element.81), channel_id=1, source_target_pairs={{4,0},{8,4},{12,8},{16,12},{20,16},{24,20},{28,24},{5,1},{9,5},{13... | collective-permute-start | bytes 276488 | tf_op jit(solution)/shard_map/ppermute | solution.py:22
  327.0 7.7 %collective-permute-start.31 = (f32[90,12,2]{0,1,2:T(8,128)S(1)}, f32[90,12,2]{0,1,2:T(8,128)S(1)}, u32[]{:S(2)}, u32[]{:S(2)}) collective-permute-start(f32[90,12,2]{0,1,2:T(8,128)S(1)} %copy.31), channel_id=1, source_target_pairs={{1,0},{2,1},{3,2},{5,4},{6,5},{7,6},{9,8},{10,9},{11,10},{13,12},{... | collective-permute-start | bytes 25928 | tf_op jit(solution)/shard_map/ppermute | solution.py:22
  328.9 4.5 %collective-permute-start.30 = (f32[90,12,2]{0,1,2:T(8,128)S(1)}, f32[90,12,2]{0,1,2:T(8,128)S(1)}, u32[]{:S(2)}, u32[]{:S(2)}) collective-permute-start(f32[90,12,2]{0,1,2:T(8,128)S(1)} %copy.30), channel_id=1, source_target_pairs={{0,1},{1,2},{2,3},{4,5},{5,6},{6,7},{8,9},{9,10},{10,11},{12,13},{... | collective-permute-start | bytes 25928 | tf_op jit(solution)/shard_map/ppermute | solution.py:21
  342.3 1.2 copy-start.1
  342.3 1.2 copy-start.3
  342.3 1.2 copy-start.5
  342.4 1.2 copy-start.7
  342.4 1.2 copy-start.9
where the time goes:
time: 354 us; the launch traced here: 351 us
  blocking collectives  149 us (42%)
  starting transfers between devices  102 us (29%)
  waiting for transfers between devices  45.9 us (13%)
  other arithmetic  27.1 us (8%)
  between operations  15.4 us (4%)
  local copies, waits for them, and re-layouts  10.9 us (3%)
    psum x4, blocking collectives, two_products(): lax.psum((jnp.sum(residual * residual), jnp.sum(residual * applied)), ('t...  149 us
    ppermute x16, starting transfers between devices, padded(): before = lax.ppermute(last, axis, up)  64.9 us
    ppermute x16, waiting for transfers between devices, padded(): after = lax.ppermute(first, axis, down)  41.8 us
    ppermute x16, starting transfers between devices, padded(): after = lax.ppermute(first, axis, down)  37.3 us
  transfers between devices with their start and end apart: 32, of which 18 were waited for; matrix products, arithmetic and copies ran while one was open for 0% of the time, Pallas kernels for 0%

commit v1 on v0

v1 whole, which is shorter than its diff:
```python
import functools

import jax
import jax.numpy as jnp
from jax import lax
from jax.experimental import pallas as pl
from jax.experimental.pallas import tpu as pltpu
from jax.sharding import Mesh, PartitionSpec as P

ITERS = 4
ADVECT = 0.1
GRAVITY_DT = 0.1

SUB = 8
LANES = 128
SEG = 32
FIELDS = ("u", "v", "t", "st", "su", "sv")
SLOTS = {"u": 0, "v": 2, "t": 4, "st": 6, "su": 8, "sv": 9}
N_SLOTS = 10
CHUNK_LOAD = SUB
CHUNK_EDGE = 2 * SUB
CHUNK_ROW = 3 * SUB
CORNER_LANE = 32
CORNER_STEP = 24


def lane_ids():
    return lax.broadcasted_iota(jnp.int32, (SUB, LANES), 1)


def row_ids():
    return lax.broadcasted_iota(jnp.int32, (SUB, LANES), 0)


def roll_lanes(value, amount):
    amount %= LANES
    return value if amount == 0 else pltpu.roll(value, amount, 1)


def roll_rows(value, amount):
    amount %= SUB
    return value if amount == 0 else pltpu.roll(value, amount, 0)


def at(value, shift):
    return roll_lanes(value, -shift)


def row_of(tile, row):
    return jnp.broadcast_to(tile[row : row + 1, :], (SUB, LANES))


def group_count(levels):
    return -(-levels // SUB)


def load_group(ref, row, q, levels):
    first = min(q * SUB, levels - SUB)
    value = ref[pl.ds(first * SUB + row, SUB, stride=SUB), :]
    return roll_rows(value, first - q * SUB)


def store_group(ref, row, q, levels, value):
    count = min(SUB, levels - q * SUB)
    ref[pl.ds(q * SUB * SUB + row, count, stride=SUB), :] = value[:count]


def level_numbers(groups):
    rows = row_ids()
    numbers = [(rows + q * SUB).astype(jnp.float32) for q in range(groups)]
    return numbers + [(rows + (lane_ids() // SEG) * SUB).astype(jnp.float32)]


def edge_of_groups(values):
    lanes = lane_ids()
    out = roll_lanes(values[0], 8)
    for q in range(1, len(values)):
        out = jnp.where(lanes >= SEG * q, roll_lanes(values[q], SEG * q + 8), out)
    return jnp.where(lanes % SEG >= 16, roll_lanes(out, 16), out)


def insert_sides(edge, west, east, field):
    place = lane_ids() % SEG
    edge = jnp.where((place == 6) | (place == 7), roll_lanes(west, 6 - 4 * field), edge)
    return jnp.where((place == 24) | (place == 25), roll_lanes(east, 22 - 4 * field), edge)


def edge_of_tile(west, centre, east):
    lanes = lane_ids()
    out = jnp.where(lanes < 8, roll_lanes(west, 8), roll_lanes(centre, 8))
    out = jnp.where(lanes >= 16, roll_lanes(centre, 24), out)
    out = jnp.where(lanes >= 24, roll_lanes(east, 24), out)
    out = jnp.where(lanes < SEG, out, roll_lanes(out, SEG))
    return jnp.where(lanes < 2 * SEG, out, roll_lanes(out, 2 * SEG))


def merge_edge(value, edge, q):
    lanes = lane_ids()
    value = jnp.where(lanes < 2, roll_lanes(edge, -(SEG * q + 8)), value)
    return jnp.where(lanes >= LANES - 2, roll_lanes(edge, 104 - SEG * q), value)


def pack_kernel(levels, peers, u_ref, v_ref, t_ref, su_ref, sv_ref, st_ref, count_ref, elev_ref, y1_ref, y2_ref, x_ref, chunk_ref):
    groups = group_count(levels)
    lanes, rows = lane_ids(), row_ids()
    even = lax.axis_index("ty") % 2 == 0
    refs = {"u": u_ref, "v": v_ref, "t": t_ref, "st": st_ref, "su": su_ref, "sv": sv_ref}
    count = count_ref[...].astype(jnp.float32)
    zero = jnp.zeros((SUB, LANES), jnp.float32)

    wet_u = jnp.where(lanes == 0, 0.0, jnp.minimum(count, roll_lanes(count, 1)))
    wet_v = jnp.where(rows == 0, 0.0, jnp.minimum(count, roll_rows(count, 1)))
    col_u, col_v, edge = zero, zero, zero
    for k in range(levels):
        su_level = su_ref[k * SUB : (k + 1) * SUB, :]
        col_u = col_u + jnp.where(wet_u > float(k), su_level, 0.0)
        col_v = col_v + jnp.where(wet_v > float(k), sv_ref[k * SUB : (k + 1) * SUB, :], 0.0)
        edge = jnp.where(lanes == k, roll_lanes(su_level, k), edge)
    load = elev_ref[...] + GRAVITY_DT * (at(col_u, 1) - col_u + roll_rows(col_v, -1) - col_v)

    loaded = {}
    for name in FIELDS:
        for row in range(SUB):
            for q in range(groups):
                loaded[name, row, q] = load_group(refs[name], row, q, levels)

    corners = (("u", 6, 0), ("u", 7, 0), ("u", 7, 1), ("su", 7, 0), ("v", 7, 127), ("u", 7, 127))
    corners += (("v", 0, 127), ("v", 1, 127), ("v", 0, 126), ("sv", 0, 127), ("v", 0, 0), ("u", 0, 0))
    for place, (name, row, column) in enumerate(corners):
        for q in range(groups):
            lane = CORNER_LANE + CORNER_STEP * q + place
            edge = jnp.where(lanes == lane, roll_lanes(loaded[name, row, q], lane - column), edge)

    for row in range(SUB):
        packet = zero
        for field, name in enumerate(FIELDS):
            for q in range(groups):
                lane = SEG * q + 4 * field
                packet = jnp.where((lanes >= lane) & (lanes < lane + 4), roll_lanes(loaded[name, row, q], lane + 2), packet)
        x_ref[row * SUB : (row + 1) * SUB, :] = packet
    x_ref[SUB * SUB :, :] = count

    for name in FIELDS:
        wide = name not in ("su", "sv")
        for offset in range(2 if wide else 1):
            for q in range(groups):
                upper = loaded[name, 6 + offset if wide else 7, q]
                lower = loaded[name, offset, q]
                place = pl.ds(((SLOTS[name] + offset) * groups + q) * SUB, SUB)
                y1_ref[place, :] = jnp.where(even, upper, lower)
                y2_ref[place, :] = jnp.where(even, lower, upper)
    y1_ref[N_SLOTS * groups * SUB :, :] = count
    y2_ref[N_SLOTS * groups * SUB :, :] = count

    south_row = [loaded["sv", 0, q] for q in range(groups)]

    def put(peer, carry):
        chunk_ref[peer, 0:SUB, :] = count
        chunk_ref[peer, CHUNK_LOAD : CHUNK_LOAD + SUB, :] = load
        chunk_ref[peer, CHUNK_EDGE : CHUNK_EDGE + SUB, :] = edge
        for q in range(groups):
            chunk_ref[peer, CHUNK_ROW + q * SUB : CHUNK_ROW + (q + 1) * SUB, :] = south_row[q]
        return carry

    lax.fori_loop(0, peers, put, 0)


def slot_reader(y1_ref, y2_ref, groups):
    even = lax.axis_index("ty") % 2 == 0

    def read(name, row, q):
        if name in ("su", "sv"):
            slot = SLOTS[name]
        else:
            slot = SLOTS[name] + (row + 2 if row < 0 else row - SUB)
        place = pl.ds((slot * groups + q) * SUB, SUB)
        north, south = jnp.where(even, y1_ref[place, :], y2_ref[place, :]), jnp.where(even, y2_ref[place, :], y1_ref[place, :])
        return south if row < 0 else north

    def counts():
        place = pl.ds(N_SLOTS * groups * SUB, SUB)
        one, two = y1_ref[place, :], y2_ref[place, :]
        return jnp.where(even, two, one), jnp.where(even, one, two)

    return read, counts


def side_reader(x1_ref, x2_ref):
    even = lax.axis_index("core") % 2 == 0

    def read(row):
        place = pl.ds(row * SUB, SUB)
        one, two = x1_ref[place, :], x2_ref[place, :]
        return jnp.where(even, two, one), jnp.where(even, one, two)

    return read


def face_value(t0, t_before, t_after, t_before2):
    return (7.0 * (t0 + t_before) - (t_after + t_before2)) * (1.0 / 12.0)


def tracer_kernel(levels, u_ref, v_ref, t_ref, st_ref, count_ref, y1_ref, y2_ref, x1_ref, x2_ref, dt_ref, du_ref, dv_ref):
    groups = group_count(levels)
    refs = {"u": u_ref, "v": v_ref, "t": t_ref, "st": st_ref}
    read_row, read_counts = slot_reader(y1_ref, y2_ref, groups)
    read_sides = side_reader(x1_ref, x2_ref)
    numbers = level_numbers(groups)

    count = count_ref[...].astype(jnp.float32)
    count_south, count_north = read_counts()
    count_west, count_east = read_sides(SUB)
    count_edge = edge_of_tile(count_west, count, count_east)
    wet_u_tile = (jnp.minimum(count, at(count, -1)), jnp.minimum(count_edge, at(count_edge, -1)))
    count_rows = {row: row_of(count, row) for row in range(SUB)}
    count_rows.update({row: row_of(count_south, row % SUB) for row in (-2, -1)})
    count_rows.update({row: row_of(count_north, row - SUB) for row in (8, 9)})
    wet_v_rows = {row: jnp.minimum(count_rows[row], count_rows[row - 1]) for row in range(-1, 10)}

    def along_columns(level, wet_count, wet_u_count, u, t, st):
        wet_u = wet_u_count > level
        cell = jnp.where(wet_count > level, -ADVECT * st, 0.0)
        flux = jnp.where(wet_u, at(cell, -1) - cell, 0.0)
        back = u * flux
        pair = back + at(back, 1)
        outer = at(back, -1) + at(back, 2)
        return (7.0 * pair - outer) * (1.0 / 12.0), flux * face_value(t, at(t, -1), at(t, 1), at(t, -2))

    sides = [read_sides(row) for row in range(SUB)]
    edge_t, edge_u = [], []
    for row in range(SUB):
        values = {}
        for name in ("u", "t", "st"):
            own = edge_of_groups([load_group(refs[name], row, q, levels) for q in range(groups)])
            values[name] = insert_sides(own, *sides[row], FIELDS.index(name))
        from_x, to_u = along_columns(
            numbers[groups], row_of(count_edge, row), row_of(wet_u_tile[1], row), values["u"], values["t"], values["st"]
        )
        edge_t.append(from_x)
        edge_u.append(to_u)

    for q in range(groups):
        level = numbers[q]

        def get(name, row):
            return load_group(refs[name], row, q, levels) if 0 <= row < SUB else read_row(name, row, q)

        t = {row: get("t", row) for row in range(-2, 9)}
        st = {row: get("st", row) for row in range(-2, 10)}
        v = {row: get("v", row) for row in range(-1, 10)}
        cell = {row: jnp.where(count_rows[row] > level, -ADVECT * st[row], 0.0) for row in range(-2, 10)}
        flux = {row: jnp.where(wet_v_rows[row] > level, cell[row - 1] - cell[row], 0.0) for row in range(-1, 10)}
        back = {row: v[row] * flux[row] for row in range(-1, 10)}
        for row in range(SUB):
            from_x, to_u = along_columns(
                level, count_rows[row], row_of(wet_u_tile[0], row), get("u", row), t[row], st[row]
            )
            from_x = merge_edge(from_x, edge_t[row], q)
            to_u = merge_edge(to_u, edge_u[row], q)
            from_y = (7.0 * (back[row] + back[row + 1]) - (back[row - 1] + back[row + 2])) * (1.0 / 12.0)
            to_v = flux[row] * face_value(t[row], t[row - 1], t[row + 1], t[row - 2])
            store_group(dt_ref, row, q, levels, st[row] + from_x + from_y)
            store_group(du_ref, row, q, levels, to_u)
            store_group(dv_ref, row, q, levels, to_v)


def total(value):
    return jnp.sum(value, axis=(0, 1), keepdims=True)


def surface_solve(levels, ny, nx, g_ref, count_ref, load_ref, face_ref, x_ref, r_ref, p_ref, q_ref):
    groups = group_count(levels)
    lanes, rows = lane_ids(), row_ids()
    numbers = level_numbers(groups)
    core = lax.axis_index("core")
    unroll = ny if ny <= 8 else 1

    def loop(body, init=0):
        return lax.fori_loop(0, ny, body, init, unroll=unroll)

    def block(ref, j, i):
        return ref[j, i]

    def west_of(ref, j, i):
        return roll_lanes(jnp.where(lanes == LANES - 1, ref[j, max(i - 1, 0)], ref[j, i]), 1)

    def east_of(ref, j, i):
        return roll_lanes(jnp.where(lanes == 0, ref[j, min(i + 1, nx - 1)], ref[j, i]), -1)

    def south_of(ref, j, i):
        return roll_rows(jnp.where(rows == SUB - 1, ref[jnp.maximum(j - 1, 0), i], ref[j, i]), 1)

    def north_of(ref, j, i):
        return roll_rows(jnp.where(rows == 0, ref[jnp.minimum(j + 1, ny - 1), i], ref[j, i]), -1)

    def chunk(j, i, first, size):
        half = jnp.where(core == i % 2, 0, 1)
        return g_ref[half][j * (nx // 2) + i // 2, first : first + size, :]

    def gather(j, carry):
        for i in range(nx):
            count_ref[j, i] = chunk(j, i, 0, SUB)
        return carry

    loop(gather)

    def depth(wet):
        return wet + wet * (wet - 1.0) * (0.5 / levels)

    def faces(j, carry):
        for i in range(nx):
            count = count_ref[j, i]
            wet_u = jnp.minimum(count, west_of(count_ref, j, i))
            wet_v = jnp.minimum(count, south_of(count_ref, j, i))
            if i == 0:
                wet_u = jnp.where(lanes == 0, 0.0, wet_u)
            wet_v = jnp.where((rows == 0) & (j == 0), 0.0, wet_v)
            face_ref[0, j, i] = GRAVITY_DT * depth(wet_u)
            face_ref[1, j, i] = GRAVITY_DT * depth(wet_v)
            edge = chunk(j, i, CHUNK_EDGE, SUB)
            wet_west = jnp.broadcast_to(wet_u[:, 0:1], (SUB, LANES))
            inside = (lanes < levels) & (wet_west > lanes.astype(jnp.float32))
            col_u = jnp.sum(jnp.where(inside, edge, 0.0), axis=1, keepdims=True)
            face_ref[2, j, i] = GRAVITY_DT * jnp.broadcast_to(col_u, (SUB, LANES))
            wet_south = row_of(wet_v, 0)
            col_v = jnp.zeros((SUB, LANES), jnp.float32)
            for q in range(groups):
                south = chunk(j, i, CHUNK_ROW + q * SUB, SUB)
                col_v = col_v + jnp.where(wet_south > numbers[q], south, 0.0)
            col_v = jnp.sum(col_v, axis=0, keepdims=True)
            face_ref[3, j, i] = GRAVITY_DT * jnp.broadcast_to(col_v, (SUB, LANES))
        return carry

    loop(faces)

    zero = jnp.zeros((SUB, LANES), jnp.float32)

    def start(j, norm):
        for i in range(nx):
            load = chunk(j, i, CHUNK_LOAD, SUB)
            load = load - jnp.where(lanes == 0, face_ref[2, j, i], 0.0)
            load = load - jnp.where(rows == 0, face_ref[3, j, i], 0.0)
            if i + 1 < nx:
                load = load + jnp.where(lanes == LANES - 1, face_ref[2, j, i + 1], 0.0)
            north = jnp.where(j + 1 < ny, face_ref[3, jnp.minimum(j + 1, ny - 1), i], 0.0)
            load = load + jnp.where(rows == SUB - 1, north, 0.0)
            r_ref[j, i] = load
            p_ref[j, i] = load
            x_ref[j, i] = zero
            norm = norm + load * load
        return norm

    norm = total(loop(start, zero))

    for iteration in range(ITERS):

        def apply(j, dot):
            for i in range(nx):
                p = p_ref[j, i]
                image = p + face_ref[0, j, i] * (p - west_of(p_ref, j, i))
                image = image + face_ref[1, j, i] * (p - south_of(p_ref, j, i))
                depth_east = east_of(face_ref.at[0], j, i)
                if i == nx - 1:
                    depth_east = jnp.where(lanes == LANES - 1, 0.0, depth_east)
                depth_north = north_of(face_ref.at[1], j, i)
                depth_north = jnp.where((rows == SUB - 1) & (j == ny - 1), 0.0, depth_north)
                image = image + depth_east * (p - east_of(p_ref, j, i))
                image = image + depth_north * (p - north_of(p_ref, j, i))
                q_ref[j, i] = image
                dot = dot + p * image
            return dot

        step = norm / total(loop(apply, zero))
        last = iteration + 1 == ITERS

        def advance(j, new):
            for i in range(nx):
                x_ref[j, i] = x_ref[j, i] + step * p_ref[j, i]
                if not last:
                    residual = r_ref[j, i] - step * q_ref[j, i]
                    r_ref[j, i] = residual
                    new = new + residual * residual
            return new

        new = loop(advance, zero)
        if not last:
            new = total(new)
            ratio = new / norm
            norm = new

            def turn(j, carry):
                for i in range(nx):
                    p_ref[j, i] = r_ref[j, i] + ratio * p_ref[j, i]
                return carry

            loop(turn)


def flow_kernel(
    levels, ny, nx, u_ref, v_ref, su_ref, sv_ref, ga_ref, gb_ref, y1_ref, y2_ref, x1_ref, x2_ref, dut_ref, dvt_ref,
    du_ref, dv_ref, eta_ref, count_s, face_s, x_s, r_s, p_s, q_s,
):
    groups = group_count(levels)
    lanes, rows = lane_ids(), row_ids()
    place = lanes % SEG
    core = lax.axis_index("core")
    my_j = lax.axis_index("ty")
    my_i = lax.axis_index("y") * 2 + core
    refs = {"u": u_ref, "v": v_ref, "su": su_ref, "sv": sv_ref}
    numbers = level_numbers(groups)
    thick = [1.0 + number * (1.0 / levels) for number in numbers]
    read_row, _ = slot_reader(y1_ref, y2_ref, groups)
    read_sides = side_reader(x1_ref, x2_ref)

    class Halves:
        def __getitem__(self, half):
            class Picked:
                def __getitem__(self, where):
                    return jnp.where(half == 0, ga_ref[where], gb_ref[where])

            return Picked()

    halves = Halves()
    surface_solve(levels, ny, nx, halves, count_s, None, face_s, x_s, r_s, p_s, q_s)
    eta_ref[...] = x_s[my_j, my_i]

    def around(ref):
        tiles = []
        for dj in (-1, 0, 1):
            j = jnp.clip(my_j + dj, 0, ny - 1)
            there = (my_j + dj >= 0) & (my_j + dj < ny)
            row = []
            for di in (-1, 0, 1):
                i = jnp.clip(my_i + di, 0, nx - 1)
                inside = there & (my_i + di >= 0) & (my_i + di < nx)
                row.append(jnp.where(inside, ref[j, i], 0.0))
            tiles.append((row[1], edge_of_tile(*row)))
        return tiles

    count_tiles, x_tiles = around(count_s), around(x_s)

    def rows_of(tiles, kind):
        out = {}
        for row in range(-2, 10):
            out[row] = row_of(tiles[row // SUB + 1][kind], row % SUB)
        return out

    def corner(dj, di):
        j, i = jnp.clip(my_j + dj, 0, ny - 1), jnp.clip(my_i + di, 0, nx - 1)
        inside = (my_j + dj >= 0) & (my_j + dj < ny) & (my_i + di >= 0) & (my_i + di < nx)
        half = jnp.where(core == i % 2, 0, 1)
        return jnp.where(inside, halves[half][j * (nx // 2) + i // 2, CHUNK_EDGE : CHUNK_EDGE + SUB, :], 0.0)

    corner_tiles = {"se": corner(-1, 1), "sw": corner(-1, -1), "nw": corner(1, -1), "ne": corner(1, 1)}
    corner_places = {
        ("u", -2): (("se", 0, 24),),
        ("u", -1): (("se", 1, 24), ("se", 2, 25), ("sw", 5, 7)),
        ("su", -1): (("se", 3, 24),),
        ("v", -1): (("sw", 4, 7),),
        ("v", 8): (("nw", 6, 7), ("nw", 8, 6), ("ne", 10, 24)),
        ("u", 8): (("ne", 11, 24),),
        ("v", 9): (("nw", 7, 7),),
        ("sv", 8): (("nw", 9, 7),),
    }

    def insert_corners(edge, name, row):
        for which, value, target in corner_places.get((name, row), ()):
            for q in range(groups):
                lane = SEG * q + target
                source = CORNER_LANE + CORNER_STEP * q + value
                edge = jnp.where(lanes == lane, roll_lanes(corner_tiles[which], lane - source), edge)
        return edge

    sides = [read_sides(row) for row in range(SUB)]
    wanted = {"u": range(-2, 9), "v": range(-1, 10), "su": range(-1, 9), "sv": range(-1, 9)}

    def get(name, row, q):
        return load_group(refs[name], row, q, levels) if 0 <= row < SUB else read_row(name, row, q)

    def get_edge(name, row):
        edge = edge_of_groups([get(name, row, q) for q in range(groups)])
        if 0 <= row < SUB:
            return insert_sides(edge, *sides[row], FIELDS.index(name))
        return insert_corners(edge, name, row)

    total_rows = ny * SUB
    first_row = (my_j * SUB).astype(jnp.float32)

    edge_u, edge_v = [], []
    for part in [groups] + list(range(groups)):
        is_edge = part == groups
        kind = 1 if is_edge else 0
        level = numbers[part]
        data = {
            name: {row: get_edge(name, row) if is_edge else get(name, row, part) for row in wanted[name]} for name in wanted
        }
        u, v, su, sv = data["u"], data["v"], data["su"], data["sv"]
        counts, x = rows_of(count_tiles, kind), rows_of(x_tiles, kind)
        u_cot, v_cot, a, b = {}, {}, {}, {}
        for row in range(-1, 9):
            wet_u = jnp.minimum(counts[row], at(counts[row], -1)) > level
            wet_v = jnp.minimum(counts[row], counts[row - 1]) > level
            u_cot[row] = su[row] + jnp.where(wet_u, thick[part] * (x[row] - at(x[row], -1)), 0.0)
            v_cot[row] = sv[row] + jnp.where(wet_v, thick[part] * (x[row] - x[row - 1]), 0.0)
            a[row] = jnp.where(wet_u, ADVECT * u_cot[row], 0.0)
            b[row] = jnp.where(wet_v, ADVECT * v_cot[row], 0.0)
        v_pair = {row: v[row] + v[row + 1] for row in range(-1, 9)}
        v_bar = {row: 0.25 * (v_pair[row] + at(v_pair[row], -1)) for row in range(-1, 9)}
        u_pair = {row: u[row] + u[row - 1] for row in range(SUB)}
        u_bar = {row: 0.25 * (u_pair[row] + at(u_pair[row], 1)) for row in range(SUB)}
        to_v_bar = {}
        for row in range(-1, 8):
            turn = 0.5 + (first_row + (row + 0.5)) * (1.0 / total_rows)
            to_v_bar[row] = a[row] * (turn - 0.5 * (u[row + 1] - u[row - 1]))
        to_u_bar = {}
        for row in range(0, 9):
            turn = 0.5 + (first_row + row) * (1.0 / total_rows)
            to_u_bar[row] = b[row] * (-turn - 0.5 * (at(v[row], 1) - at(v[row], -1)))
        for row in range(SUB):
            au, bu = a[row] * u[row], b[row] * u_bar[row]
            du = u_cot[row] + 0.5 * (
                at(au, 1) - at(au, -1) - a[row] * (at(u[row], 1) - at(u[row], -1))
                + a[row + 1] * v_bar[row + 1] - a[row - 1] * v_bar[row - 1]
            )
            pair = to_u_bar[row] + to_u_bar[row + 1]
            du = du + 0.25 * (pair + at(pair, -1))
            dv = v_cot[row] + 0.5 * (
                b[row + 1] * v[row + 1] - b[row - 1] * v[row - 1] - b[row] * (v[row + 1] - v[row - 1])
                + at(bu, 1) - at(bu, -1)
            )
            pair = to_v_bar[row] + to_v_bar[row - 1]
            dv = dv + 0.25 * (pair + at(pair, 1))
            if is_edge:
                edge_u.append(du)
                edge_v.append(dv)
            else:
                du = merge_edge(du, edge_u[row], part) + load_group(dut_ref, row, part, levels)
                dv = merge_edge(dv, edge_v[row], part) + load_group(dvt_ref, row, part, levels)
                store_group(du_ref, row, part, levels, du)
                store_group(dv_ref, row, part, levels, dv)


def swaps(mesh_shape, along, parity):
    ny, nx = mesh_shape
    pairs = []
    for j in range(ny):
        for i in range(nx):
            k, size = (j, ny) if along == "y" else (i, nx)
            other = k + 1 if k % 2 == parity else k - 1
            if 0 <= other < size:
                pairs.append((j * nx + i, other * nx + i if along == "y" else j * nx + other))
    return pairs


def call(kernel, outs, args, scratch=(), flops=0, size=0):
    vmem = pl.BlockSpec(memory_space=pltpu.VMEM)
    return pl.pallas_call(
        kernel,
        out_shape=[jax.ShapeDtypeStruct(shape, jnp.float32) for shape in outs],
        in_specs=[vmem] * len(args),
        out_specs=[vmem] * len(outs),
        scratch_shapes=list(scratch),
        compiler_params=pltpu.CompilerParams(vmem_limit_bytes=48 * 1024 * 1024),
        cost_estimate=pl.CostEstimate(flops=flops, bytes_accessed=size, transcendentals=0),
    )(*args)


def on_device(shape, u, v, t, count, su, sv, st, elev):
    ny, nx = shape
    levels = u.shape[0]
    groups = group_count(levels)
    flat = (levels * SUB, LANES)
    u, v, t, su, sv, st = (field.reshape(flat) for field in (u, v, t, su, sv, st))
    peers = ny * nx // 2
    row_packet = ((N_SLOTS * groups + 1) * SUB, LANES)
    column_packet = ((SUB + 1) * SUB, LANES)
    chunk = (peers, CHUNK_ROW + groups * SUB, LANES)
    y1, y2, xp, chunks = call(
        functools.partial(pack_kernel, levels, peers),
        [row_packet, row_packet, column_packet, chunk],
        (u, v, t, su, sv, st, count, elev),
        flops=1 << 20,
        size=1 << 21,
    )
    axes = ("ty", "y", "core")
    ga = lax.all_to_all(chunks, ("ty", "y"), 0, 0)
    x1 = lax.ppermute(xp, axes, swaps(shape, "x", 0))
    x2 = lax.ppermute(xp, axes, swaps(shape, "x", 1))
    y1 = lax.ppermute(y1, axes, swaps(shape, "y", 0))
    y2 = lax.ppermute(y2, axes, swaps(shape, "y", 1))
    gb = lax.ppermute(ga, axes, swaps(shape, "x", 0))
    dt, du_t, dv_t = call(
        functools.partial(tracer_kernel, levels),
        [flat] * 3,
        (u, v, t, st, count, y1, y2, x1, x2),
        flops=1 << 22,
        size=1 << 21,
    )
    grid = pltpu.VMEM((ny, nx, SUB, LANES), jnp.float32)
    faces = pltpu.VMEM((4, ny, nx, SUB, LANES), jnp.float32)
    du, dv, eta = call(
        functools.partial(flow_kernel, levels, ny, nx),
        [flat, flat, (SUB, LANES)],
        (u, v, su, sv, ga, gb, y1, y2, x1, x2, du_t, dv_t),
        scratch=(grid, faces, grid, grid, grid, grid),
        flops=1 << 23,
        size=1 << 22,
    )
    whole = (levels, SUB, LANES)
    return du.reshape(whole), dv.reshape(whole), dt.reshape(whole), eta


def solution(mesh):
    ny, nx = mesh.shape["ty"], mesh.shape["tx"]
    split = Mesh(mesh.devices.reshape(ny, nx // 2, 2), ("ty", "y", "core"))
    deep, flat = P(None, "ty", ("y", "core")), P("ty", ("y", "core"))
    return jax.shard_map(
        functools.partial(on_device, (ny, nx)),
        mesh=split,
        in_specs=(deep, deep, deep, flat, deep, deep, deep, flat),
        out_specs=(deep, deep, deep, flat),
        check_vma=False,
    )
```

time: 354 us -> 50.3 us (0.14)
  the two profiles are of different devices: /device:TPU:11 before, /device:TPU:3 now
where the time goes in v1:
time: 50.3 us; the launch traced here: 50 us
  blocking collectives  17.5 us (35%)
  Pallas kernels  12.6 us (25%)
  starting transfers between devices  10.2 us (20%)
  local copies, waits for them, and re-layouts  6.11 us (12%)
  waiting for transfers between devices  2.86 us (6%)
  between operations  0.71 us (1%)
    all_to_all x1, blocking collectives, on_device(): ga = lax.all_to_all(chunks, ('ty', 'y'), 0, 0)  17.5 us
    pallas_call x3, Pallas kernels, call(): pl.pallas_call(kernel, out_shape=[jax.ShapeDtypeStruct(shape, jnp.float32...  12.6 us
    unnamed x20, local copies, waits for them, and re-layouts  6.11 us
    ppermute x1, starting transfers between devices, on_device(): y2 = lax.ppermute(y2, axes, swaps(shape, 'y', 1))  3.41 us
    ppermute x1, starting transfers between devices, on_device(): gb = lax.ppermute(ga, axes, swaps(shape, 'x', 0))  3.35 us
    ppermute x1, waiting for transfers between devices, on_device(): x2 = lax.ppermute(xp, axes, swaps(shape, 'x', 1))  2.85 us
    ppermute x1, starting transfers between devices, on_device(): x2 = lax.ppermute(xp, axes, swaps(shape, 'x', 1))  2.77 us
  transfers between devices with their start and end apart: 5, of which 1 were waited for; matrix products, arithmetic and copies ran while one was open for 0% of the time, Pallas kernels for 8%

profile of v1, /device:TPU:3, one launch (start us, length us, event | category | flops | bytes accessed | tf_op | source)
XLA Modules:
  0.0 50.0 jit_solution(688619271104853780)
XLA Ops:
  0.6 0.0 copy-start.9
  0.6 0.0 copy-start.8
  0.7 0.7 %copy-done.9 = f32[8,128]{1,0:T(8,128)S(1)} copy-done((f32[8,128]{1,0:T(8,128)S(1)}, f32[8,128]{1,0:T(8,128)}, u32[]{:S(2)}) %copy-start.9) | copy-done | bytes 4120
  1.3 0.0 copy-done.8
  1.3 0.0 copy-start
  1.3 0.9 %copy-done = f32[30,8,128]{2,1,0:T(8,128)S(1)} copy-done((f32[30,8,128]{2,1,0:T(8,128)S(1)}, f32[30,8,128]{2,1,0:T(8,128)}, u32[]{:S(2)}) %copy-start) | copy-done | bytes 122904
  2.2 0.0 copy-start.1
  2.2 0.9 %copy-done.1 = f32[30,8,128]{2,1,0:T(8,128)S(1)} copy-done((f32[30,8,128]{2,1,0:T(8,128)S(1)}, f32[30,8,128]{2,1,0:T(8,128)}, u32[]{:S(2)}) %copy-start.1) | copy-done | bytes 122904
  3.1 0.0 copy-start.2
  3.1 0.9 %copy-done.2 = f32[30,8,128]{2,1,0:T(8,128)S(1)} copy-done((f32[30,8,128]{2,1,0:T(8,128)S(1)}, f32[30,8,128]{2,1,0:T(8,128)}, u32[]{:S(2)}) %copy-start.2) | copy-done | bytes 122904
  4.0 0.0 copy-start.3
  4.0 0.9 %copy-done.3 = f32[30,8,128]{2,1,0:T(8,128)S(1)} copy-done((f32[30,8,128]{2,1,0:T(8,128)S(1)}, f32[30,8,128]{2,1,0:T(8,128)}, u32[]{:S(2)}) %copy-start.3) | copy-done | bytes 122904
  4.9 0.0 copy-start.4
  4.9 0.9 %copy-done.4 = f32[30,8,128]{2,1,0:T(8,128)S(1)} copy-done((f32[30,8,128]{2,1,0:T(8,128)S(1)}, f32[30,8,128]{2,1,0:T(8,128)}, u32[]{:S(2)}) %copy-start.4) | copy-done | bytes 122904
  5.8 0.0 copy-start.6
  5.8 0.9 %copy-done.6 = f32[30,8,128]{2,1,0:T(8,128)S(1)} copy-done((f32[30,8,128]{2,1,0:T(8,128)S(1)}, f32[30,8,128]{2,1,0:T(8,128)}, u32[]{:S(2)}) %copy-start.6) | copy-done | bytes 122904
  6.7 0.4 shard_map.111
  7.2 17.5 %all_to_all.5.ga_ref = f32[16,56,128]{2,1,0:T(8,128)S(1)} all-to-all(f32[16,56,128]{2,1,0:T(8,128)S(1)} %get-tuple-element.14), channel_id=1, replica_groups=mesh['ty'=8,'y'=2,'core'=2] {'ty','y'}, dimensions={0} | all-to-all | bytes 917504 | tf_op jit(solution)/shard_map/all_to_all | solution.py:586
  24.7 3.4 %collective-permute-start = (f32[16,56,128]{2,1,0:T(8,128)S(1)}, f32[16,56,128]{2,1,0:T(8,128)S(1)}, u32[]{:S(2)}, u32[]{:S(2)}) collective-permute-start(f32[16,56,128]{2,1,0:T(8,128)S(1)} %all_to_all.5.ga_ref), channel_id=1, source_target_pairs={{0,1},{1,0},{2,3},{3,2},{4,5},{5,4},{6,7},{7,6},{8,9},{9,8},{10,11... | collective-permute-start | bytes 1376264 | tf_op jit(solution)/shard_map/ppermute | solution.py:591
  28.1 0.6 %collective-permute-start.1 = (f32[328,128]{1,0:T(8,128)S(1)}, f32[328,128]{1,0:T(8,128)S(1)}, u32[]{:S(2)}, u32[]{:S(2)}) collective-permute-start(f32[328,128]{1,0:T(8,128)S(1)} %get-tuple-element.15), channel_id=1, source_target_pairs={{0,4},{1,5},{2,6},{3,7},{4,0},{5,1},{6,2},{7,3},{8,12},{9,13},{10,... | collective-permute-start | bytes 503816 | tf_op jit(solution)/shard_map/ppermute | solution.py:589
  28.7 3.4 %collective-permute-start.2 = (f32[328,128]{1,0:T(8,128)S(1)}, f32[328,128]{1,0:T(8,128)S(1)}, u32[]{:S(2)}, u32[]{:S(2)}) collective-permute-start(f32[328,128]{1,0:T(8,128)S(1)} %get-tuple-element.16), channel_id=1, source_target_pairs={{4,8},{5,9},{6,10},{7,11},{8,4},{9,5},{10,6},{11,7},{12,16},{13,17... | collective-permute-start | bytes 503816 | tf_op jit(solution)/shard_map/ppermute | solution.py:590
  32.1 0.0 copy-start.5
  32.1 0.0 copy-start.7
  32.1 2.8 %collective-permute-start.4 = (f32[72,128]{1,0:T(8,128)S(1)}, f32[72,128]{1,0:T(8,128)S(1)}, u32[]{:S(2)}, u32[]{:S(2)}) collective-permute-start(f32[72,128]{1,0:T(8,128)S(1)} %get-tuple-element.17), channel_id=1, source_target_pairs={{1,2},{2,1},{5,6},{6,5},{9,10},{10,9},{13,14},{14,13},{17,18},{18,... | collective-permute-start | bytes 110600 | tf_op jit(solution)/shard_map/ppermute | solution.py:588
  34.9 0.1 collective-permute-start.3
  35.0 2.8 %collective-permute-done.4.x2_ref = f32[72,128]{1,0:T(8,128)S(1)} collective-permute-done((f32[72,128]{1,0:T(8,128)S(1)}, f32[72,128]{1,0:T(8,128)S(1)}, u32[]{:S(2)}, u32[]{:S(2)}) %collective-permute-start.4) | collective-permute-done | bytes 36896 | tf_op jit(solution)/shard_map/ppermute | solution.py:588
  37.8 0.0 collective-permute-done.3.x1_ref
  37.8 0.0 collective-permute-done.1.y1_ref
  37.8 0.0 collective-permute-done.2.y2_ref
  37.8 4.2 %shard_map.112 = (f32[240,128]{1,0:T(8,128)}, f32[240,128]{1,0:T(8,128)S(1)}, f32[240,128]{1,0:T(8,128)S(1)}) custom-call(f32[240,128]{1,0:T(8,128)S(1)} %bitcast.10, f32[240,128]{1,0:T(8,128)S(1)} %bitcast.13, f32[240,128]{1,0:T(8,128)S(1)} %bitcast.16, f32[240,128]{1,0:T(8,128)S(1)} %bitcast.18, s32[8,128]{1,0:T(8,128)S(1)} %copy-done.8, ...), custom_call_target="tpu_custom_call" | custom-call | flops 4194304 | bytes 2097152 | tf_op jit(solution)/shard_map/pallas_call | solution.py:557
  42.0 0.0 collective-permute-done.gb_ref
  42.0 0.0 copy-done.5
  42.1 0.0 copy-done.7
  42.1 7.9 %shard_map.113 = (f32[240,128]{1,0:T(8,128)}, f32[240,128]{1,0:T(8,128)}, f32[8,128]{1,0:T(8,128)}) custom-call(f32[240,128]{1,0:T(8,128)S(1)} %bitcast.11, f32[240,128]{1,0:T(8,128)S(1)} %bitcast.14, f32[240,128]{1,0:T(8,128)S(1)} %bitcast.20, f32[240,128]{1,0:T(8,128)S(1)} %bitcast.22, f32[16,56,128]{2,1,0:T(8,128)S(1)} %all_to_all.5.ga_ref, ...), custom_call_target="tpu_custom_call" | custom-call | flops 8388608 | bytes 4194304 | tf_op jit(solution)/shard_map/pallas_call | solution.py:557
Async XLA Ops:
  0.6 0.7 %copy-start.9 = (f32[8,128]{1,0:T(8,128)S(1)}, f32[8,128]{1,0:T(8,128)}, u32[]{:S(2)}) copy-start(f32[8,128]{1,0:T(8,128)} %elev_ref.1) | copy-start | bytes 12292
  0.6 0.7 %copy-start.8 = (s32[8,128]{1,0:T(8,128)S(1)}, s32[8,128]{1,0:T(8,128)}, u32[]{:S(2)}) copy-start(s32[8,128]{1,0:T(8,128)} %count_ref.3) | copy-start | bytes 12292
  1.3 0.9 %copy-start = (f32[30,8,128]{2,1,0:T(8,128)S(1)}, f32[30,8,128]{2,1,0:T(8,128)}, u32[]{:S(2)}) copy-start(f32[30,8,128]{2,1,0:T(8,128)} %param.8) | copy-start | bytes 368644
  2.2 0.9 %copy-start.1 = (f32[30,8,128]{2,1,0:T(8,128)S(1)}, f32[30,8,128]{2,1,0:T(8,128)}, u32[]{:S(2)}) copy-start(f32[30,8,128]{2,1,0:T(8,128)} %param.9) | copy-start | bytes 368644
  3.1 0.9 %copy-start.2 = (f32[30,8,128]{2,1,0:T(8,128)S(1)}, f32[30,8,128]{2,1,0:T(8,128)}, u32[]{:S(2)}) copy-start(f32[30,8,128]{2,1,0:T(8,128)} %param.10) | copy-start | bytes 368644
  4.0 0.9 %copy-start.3 = (f32[30,8,128]{2,1,0:T(8,128)S(1)}, f32[30,8,128]{2,1,0:T(8,128)}, u32[]{:S(2)}) copy-start(f32[30,8,128]{2,1,0:T(8,128)} %param.14) | copy-start | bytes 368644
  4.9 0.9 %copy-start.4 = (f32[30,8,128]{2,1,0:T(8,128)S(1)}, f32[30,8,128]{2,1,0:T(8,128)}, u32[]{:S(2)}) copy-start(f32[30,8,128]{2,1,0:T(8,128)} %param.12) | copy-start | bytes 368644
  5.8 0.9 %copy-start.6 = (f32[30,8,128]{2,1,0:T(8,128)S(1)}, f32[30,8,128]{2,1,0:T(8,128)}, u32[]{:S(2)}) copy-start(f32[30,8,128]{2,1,0:T(8,128)} %param.13) | copy-start | bytes 368644
  24.7 17.3 %collective-permute-start = (f32[16,56,128]{2,1,0:T(8,128)S(1)}, f32[16,56,128]{2,1,0:T(8,128)S(1)}, u32[]{:S(2)}, u32[]{:S(2)}) collective-permute-start(f32[16,56,128]{2,1,0:T(8,128)S(1)} %all_to_all.5.ga_ref), channel_id=1, source_target_pairs={{0,1},{1,0},{2,3},{3,2},{4,5},{5,4},{6,7},{7,6},{8,9},{9,8},{10,11... | collective-permute-start | bytes 1376264 | tf_op jit(solution)/shard_map/ppermute | solution.py:591
  28.1 9.7 %collective-permute-start.1 = (f32[328,128]{1,0:T(8,128)S(1)}, f32[328,128]{1,0:T(8,128)S(1)}, u32[]{:S(2)}, u32[]{:S(2)}) collective-permute-start(f32[328,128]{1,0:T(8,128)S(1)} %get-tuple-element.15), channel_id=1, source_target_pairs={{0,4},{1,5},{2,6},{3,7},{4,0},{5,1},{6,2},{7,3},{8,12},{9,13},{10,... | collective-permute-start | bytes 503816 | tf_op jit(solution)/shard_map/ppermute | solution.py:589
  28.7 9.2 %collective-permute-start.2 = (f32[328,128]{1,0:T(8,128)S(1)}, f32[328,128]{1,0:T(8,128)S(1)}, u32[]{:S(2)}, u32[]{:S(2)}) collective-permute-start(f32[328,128]{1,0:T(8,128)S(1)} %get-tuple-element.16), channel_id=1, source_target_pairs={{4,8},{5,9},{6,10},{7,11},{8,4},{9,5},{10,6},{11,7},{12,16},{13,17... | collective-permute-start | bytes 503816 | tf_op jit(solution)/shard_map/ppermute | solution.py:590
  32.1 10.0 %copy-start.5 = (f32[30,8,128]{2,1,0:T(8,128)S(1)}, f32[30,8,128]{2,1,0:T(8,128)}, u32[]{:S(2)}) copy-start(f32[30,8,128]{2,1,0:T(8,128)} %param.12) | copy-start | bytes 368644
  32.1 10.0 %copy-start.7 = (f32[30,8,128]{2,1,0:T(8,128)S(1)}, f32[30,8,128]{2,1,0:T(8,128)}, u32[]{:S(2)}) copy-start(f32[30,8,128]{2,1,0:T(8,128)} %param.13) | copy-start | bytes 368644
  32.1 5.7 %collective-permute-start.4 = (f32[72,128]{1,0:T(8,128)S(1)}, f32[72,128]{1,0:T(8,128)S(1)}, u32[]{:S(2)}, u32[]{:S(2)}) collective-permute-start(f32[72,128]{1,0:T(8,128)S(1)} %get-tuple-element.17), channel_id=1, source_target_pairs={{1,2},{2,1},{5,6},{6,5},{9,10},{10,9},{13,14},{14,13},{17,18},{18,... | collective-permute-start | bytes 110600 | tf_op jit(solution)/shard_map/ppermute | solution.py:588
  34.9 2.9 %collective-permute-start.3 = (f32[72,128]{1,0:T(8,128)S(1)}, f32[72,128]{1,0:T(8,128)S(1)}, u32[]{:S(2)}, u32[]{:S(2)}) collective-permute-start(f32[72,128]{1,0:T(8,128)S(1)} %get-tuple-element.17), channel_id=1, source_target_pairs={{0,1},{1,0},{2,3},{3,2},{4,5},{5,4},{6,7},{7,6},{8,9},{9,8},{10,11... | collective-permute-start | bytes 110600 | tf_op jit(solution)/shard_map/ppermute | solution.py:587

commit v2 on v1

v2 whole, which is shorter than its diff:
```python
import functools

import jax
import jax.numpy as jnp
from jax import lax
from jax.experimental import pallas as pl
from jax.experimental.pallas import tpu as pltpu
from jax.sharding import Mesh, PartitionSpec as P

ITERS = 4
ADVECT = 0.1
GRAVITY_DT = 0.1

SUB = 8
LANES = 128
SEG = 32
FIELDS = ("u", "v", "t", "st", "su", "sv")
SOUTH_SLOTS = {("u", -2): 0, ("u", -1): 1, ("v", -1): 2, ("t", -2): 3, ("t", -1): 4, ("st", -2): 5, ("st", -1): 6}
SOUTH_SLOTS.update({("su", -1): 7, ("sv", -1): 8})
NORTH_SLOTS = {("u", 8): 0, ("v", 8): 1, ("v", 9): 2, ("t", 8): 3, ("st", 8): 5, ("st", 9): 6, ("su", 8): 7, ("sv", 8): 8}
N_SLOTS = 9
CHUNK_LOAD = SUB
CHUNK_EDGE = 2 * SUB
CHUNK_ROW = 3 * SUB
CORNER_LANE = 32
CORNER_STEP = 24
CORNERS = (("u", 6, 0), ("u", 7, 0), ("u", 7, 1), ("su", 7, 0), ("v", 7, 127), ("u", 7, 127))
CORNERS += (("v", 0, 127), ("v", 1, 127), ("v", 0, 126), ("sv", 0, 127), ("v", 0, 0), ("u", 0, 0))
CORNER_PLACES = {
    ("u", -2): (("se", 0, 24),),
    ("u", -1): (("se", 1, 24), ("se", 2, 25), ("sw", 5, 7)),
    ("su", -1): (("se", 3, 24),),
    ("v", -1): (("sw", 4, 7),),
    ("v", 8): (("nw", 6, 7), ("nw", 8, 6), ("ne", 10, 24)),
    ("u", 8): (("ne", 11, 24),),
    ("v", 9): (("nw", 7, 7),),
    ("sv", 8): (("nw", 9, 7),),
}


def lane_ids():
    return lax.broadcasted_iota(jnp.int32, (SUB, LANES), 1)


def row_ids():
    return lax.broadcasted_iota(jnp.int32, (SUB, LANES), 0)


def roll_lanes(value, amount):
    amount %= LANES
    return value if amount == 0 else pltpu.roll(value, amount, 1)


def roll_rows(value, amount):
    amount %= SUB
    return value if amount == 0 else pltpu.roll(value, amount, 0)


def at(value, shift):
    return roll_lanes(value, -shift)


def row_of(tile, row):
    return jnp.broadcast_to(tile[row : row + 1, :], (SUB, LANES))


def group_count(levels):
    return -(-levels // SUB)


def load_group(ref, row, q, levels):
    first = min(q * SUB, levels - SUB)
    value = ref[pl.ds(first * SUB + row, SUB, stride=SUB), :]
    return roll_rows(value, first - q * SUB)


def store_group(ref, row, q, levels, value):
    count = min(SUB, levels - q * SUB)
    ref[pl.ds(q * SUB * SUB + row, count, stride=SUB), :] = value[:count]


def level_numbers(groups):
    rows = row_ids()
    numbers = [(rows + q * SUB).astype(jnp.float32) for q in range(groups)]
    return numbers + [(rows + (lane_ids() >> 5) * SUB).astype(jnp.float32)]


def edge_of_tile(west, centre, east):
    lanes = lane_ids()
    out = jnp.where(lanes < 8, roll_lanes(west, 8), roll_lanes(centre, 8))
    out = jnp.where(lanes >= 16, roll_lanes(centre, 24), out)
    out = jnp.where(lanes >= 24, roll_lanes(east, 24), out)
    out = jnp.where(lanes < SEG, out, roll_lanes(out, SEG))
    return jnp.where(lanes < 2 * SEG, out, roll_lanes(out, 2 * SEG))


def pack_kernel(
    levels, peers, u_hbm, v_hbm, t_hbm, su_hbm, sv_hbm, st_hbm, count_hbm, elev_hbm,
    y1_hbm, y2_hbm, x_hbm, chunk_hbm,
    u_ref, v_ref, t_ref, su_ref, sv_ref, st_ref, count_ref, elev_ref, y1_ref, y2_ref, x_ref, chunk_ref, sems,
):
    pairs = (
        (count_hbm, count_ref), (su_hbm, su_ref), (sv_hbm, sv_ref), (elev_hbm, elev_ref),
        (u_hbm, u_ref), (v_hbm, v_ref), (t_hbm, t_ref), (st_hbm, st_ref),
    )
    copies = [pltpu.make_async_copy(source, target, sems.at[n]) for n, (source, target) in enumerate(pairs)]
    for copy in copies:
        copy.start()
    for copy in copies:
        copy.wait()
    groups = group_count(levels)
    lanes, rows = lane_ids(), row_ids()
    even = lax.axis_index("ty") % 2 == 0
    refs = {"u": u_ref, "v": v_ref, "t": t_ref, "st": st_ref, "su": su_ref, "sv": sv_ref}
    count = count_ref[...].astype(jnp.float32)
    zero = jnp.zeros((SUB, LANES), jnp.float32)

    wet_u = jnp.where(lanes == 0, 0.0, jnp.minimum(count, roll_lanes(count, 1)))
    wet_v = jnp.where(rows == 0, 0.0, jnp.minimum(count, roll_rows(count, 1)))
    col_u, col_v, edge = zero, zero, zero
    for k in range(levels):
        su_level = su_ref[k * SUB : (k + 1) * SUB, :]
        col_u = col_u + jnp.where(wet_u > float(k), su_level, 0.0)
        col_v = col_v + jnp.where(wet_v > float(k), sv_ref[k * SUB : (k + 1) * SUB, :], 0.0)
        edge = jnp.where(lanes == k, roll_lanes(su_level, k), edge)
    load = elev_ref[...] + GRAVITY_DT * (at(col_u, 1) - col_u + roll_rows(col_v, -1) - col_v)

    loaded = {}
    for name in FIELDS:
        for row in range(SUB):
            for q in range(groups):
                loaded[name, row, q] = load_group(refs[name], row, q, levels)

    for place, (name, row, column) in enumerate(CORNERS):
        for q in range(groups):
            lane = CORNER_LANE + CORNER_STEP * q + place
            edge = jnp.where(lanes == lane, roll_lanes(loaded[name, row, q], lane - column), edge)

    chunk_ref[0:SUB, :] = count
    chunk_ref[CHUNK_LOAD : CHUNK_LOAD + SUB, :] = load
    chunk_ref[CHUNK_EDGE : CHUNK_EDGE + SUB, :] = edge
    for q in range(groups):
        chunk_ref[CHUNK_ROW + q * SUB : CHUNK_ROW + (q + 1) * SUB, :] = loaded["sv", 0, q]

    def put(peer, carry):
        pltpu.make_async_copy(chunk_ref, chunk_hbm.at[peer], sems.at[len(pairs)]).start()
        return carry

    lax.fori_loop(0, peers, put, 0, unroll=peers <= 32)

    for slot in range(N_SLOTS):
        upper = [(name, row + SUB) for (name, row), place in SOUTH_SLOTS.items() if place == slot]
        lower = [(name, row - SUB) for (name, row), place in NORTH_SLOTS.items() if place == slot]
        for q in range(groups):
            to_north = loaded[(*upper[0], q)]
            to_south = loaded[(*lower[0], q)] if lower else zero
            place = pl.ds((slot * groups + q) * SUB, SUB)
            y1_ref[place, :] = jnp.where(even, to_north, to_south)
            y2_ref[place, :] = jnp.where(even, to_south, to_north)
    y1_ref[N_SLOTS * groups * SUB :, :] = count
    y2_ref[N_SLOTS * groups * SUB :, :] = count
    out = [pltpu.make_async_copy(y1_ref, y1_hbm, sems.at[0]), pltpu.make_async_copy(y2_ref, y2_hbm, sems.at[1])]
    out[0].start()
    out[1].start()

    for row in range(SUB):
        packet = zero
        for field, name in enumerate(FIELDS):
            for q in range(groups):
                lane = SEG * q + 4 * field
                packet = jnp.where((lanes >= lane) & (lanes < lane + 4), roll_lanes(loaded[name, row, q], lane + 2), packet)
        x_ref[row * SUB : (row + 1) * SUB, :] = packet
    x_ref[SUB * SUB :, :] = count
    out.append(pltpu.make_async_copy(x_ref, x_hbm, sems.at[2]))
    out[2].start()
    for copy in out:
        copy.wait()
    pltpu.make_async_copy(chunk_hbm, chunk_hbm, sems.at[len(pairs)]).wait()


class Many:
    def __init__(self, items):
        self.items = list(items)

    def __getitem__(self, where):
        return Many(self.items[where]) if isinstance(where, slice) else self.items[where]

    def __len__(self):
        return len(self.items)

    def apply(self, operation, *others):
        others = [other.items if isinstance(other, Many) else [other] * len(self) for other in others]
        assert all(len(other) == len(self) for other in others)
        return Many(operation(*parts) for parts in zip(self.items, *others))

    def __add__(self, other):
        return self.apply(lambda a, b: a + b, other)

    def __sub__(self, other):
        return self.apply(lambda a, b: a - b, other)

    def __mul__(self, other):
        return self.apply(lambda a, b: a * b, other)

    def __gt__(self, other):
        return self.apply(lambda a, b: a > b, other)

    def at(self, shift):
        return self.apply(lambda a: at(a, shift))

    def rolled(self, amount):
        return self.apply(lambda a: roll_lanes(a, amount))

    def minimum(self, other):
        return self.apply(jnp.minimum, other)

    def where(self, mask, other):
        return self.apply(lambda a, m, b: jnp.where(m, a, b), mask, other)


def edges_of_groups(parts):
    lanes = lane_ids()
    out = parts[0].rolled(8)
    for q in range(1, len(parts)):
        out = parts[q].rolled(SEG * q + 8).where(lanes >= SEG * q, out)
    return out.rolled(16).where((lanes & (SEG - 1)) >= 16, out)


def insert_sides(edge, west, east, field):
    place = lane_ids() & (SEG - 1)
    edge = west.rolled(6 - 4 * field).where((place == 6) | (place == 7), edge)
    return east.rolled(22 - 4 * field).where((place == 24) | (place == 25), edge)


def merge_edges(values, edge, q):
    lanes = lane_ids()
    values = edge.rolled(-(SEG * q + 8)).where(lanes < 2, values)
    return edge.rolled(104 - SEG * q).where(lanes >= LANES - 2, values)


def load_rows(ref, q, levels):
    return Many(load_group(ref, row, q, levels) for row in range(SUB))


def store_rows(ref, q, levels, values):
    for row in range(SUB):
        store_group(ref, row, q, levels, values[row])


def rows_of(tiles, first, last):
    return Many(row_of(tiles[row // SUB + 1], row % SUB) for row in range(first, last + 1))


def slot_reader(y1_ref, y2_ref, groups):
    even = lax.axis_index("ty") % 2 == 0

    def read(name, row, q):
        slot = (SOUTH_SLOTS if row < 0 else NORTH_SLOTS)[name, row]
        place = pl.ds((slot * groups + q) * SUB, SUB)
        one, two = y1_ref[place, :], y2_ref[place, :]
        return jnp.where(even, two, one) if row < 0 else jnp.where(even, one, two)

    def counts():
        place = pl.ds(N_SLOTS * groups * SUB, SUB)
        one, two = y1_ref[place, :], y2_ref[place, :]
        return jnp.where(even, two, one), jnp.where(even, one, two)

    return read, counts


def side_reader(x1_ref, x2_ref):
    even = lax.axis_index("core") % 2 == 0

    def read(row):
        place = pl.ds(row * SUB, SUB)
        one, two = x1_ref[place, :], x2_ref[place, :]
        return jnp.where(even, two, one), jnp.where(even, one, two)

    return read


def face_values(t0, t_before, t_after, t_before2):
    return ((t0 + t_before) * 7.0 - (t_after + t_before2)) * (1.0 / 12.0)


def tracer_kernel(levels, u_ref, v_ref, t_ref, st_ref, count_ref, y1_ref, y2_ref, x1_ref, x2_ref, dt_ref, du_ref, dv_ref):
    groups = group_count(levels)
    read_row, read_counts = slot_reader(y1_ref, y2_ref, groups)
    read_sides = side_reader(x1_ref, x2_ref)
    numbers = level_numbers(groups)
    zero = jnp.zeros((SUB, LANES), jnp.float32)

    count = count_ref[...].astype(jnp.float32)
    count_south, count_north = read_counts()
    count_west, count_east = read_sides(SUB)
    count_edge = edge_of_tile(count_west, count, count_east)
    counts = rows_of((count_south, count, count_north), -2, 9)
    counts_v = counts[1:].minimum(counts[:-1])
    own = (None, count, None)
    counts_u = rows_of((None, jnp.minimum(count, at(count, -1)), None), 0, 7)
    edge_counts = rows_of((None, count_edge, None), 0, 7)
    edge_counts_u = rows_of((None, jnp.minimum(count_edge, at(count_edge, -1)), None), 0, 7)
    del own

    def along_columns(level, wet, wet_u, u, t, st):
        cell = (st * -ADVECT).where(wet > level, zero)
        flux = (cell.at(-1) - cell).where(wet_u > level, zero)
        back = u * flux
        face = face_values(t, t.at(-1), t.at(1), t.at(-2))
        return ((back + back.at(1)) * 7.0 - (back.at(-1) + back.at(2))) * (1.0 / 12.0), flux * face

    sides = [read_sides(row) for row in range(SUB)]
    west, east = Many(side[0] for side in sides), Many(side[1] for side in sides)
    u, t, st = (
        insert_sides(
            edges_of_groups([load_rows(ref, q, levels) for q in range(groups)]), west, east, FIELDS.index(name)
        )
        for name, ref in (("u", u_ref), ("t", t_ref), ("st", st_ref))
    )
    edge_t, edge_u = along_columns(numbers[groups], edge_counts, edge_counts_u, u, t, st)

    for q in range(groups):
        level = numbers[q]

        def rows(name, ref, first, last):
            south = [read_row(name, row, q) for row in range(first, 0)]
            north = [read_row(name, row, q) for row in range(SUB, last + 1)]
            return Many(south + load_rows(ref, q, levels).items + north)

        t, st, v = rows("t", t_ref, -2, 8), rows("st", st_ref, -2, 9), rows("v", v_ref, -1, 9)
        from_x, to_u = along_columns(level, counts[2:10], counts_u, load_rows(u_ref, q, levels), t[2:10], st[2:10])
        cell = (st * -ADVECT).where(counts > level, zero)
        flux = (cell[:-1] - cell[1:]).where(counts_v > level, zero)
        back = v * flux
        from_y = ((back[1:9] + back[2:10]) * 7.0 - (back[0:8] + back[3:11])) * (1.0 / 12.0)
        to_v = flux[1:9] * face_values(t[2:10], t[1:9], t[3:11], t[0:8])
        store_rows(dt_ref, q, levels, st[2:10] + merge_edges(from_x, edge_t, q) + from_y)
        store_rows(du_ref, q, levels, merge_edges(to_u, edge_u, q))
        store_rows(dv_ref, q, levels, to_v)


def total(value):
    return jnp.sum(value, axis=(0, 1), keepdims=True)


def surface_solve(levels, ny, nx, read, count_ref, face_ref, x_ref, r_ref, p_ref):
    groups = group_count(levels)
    lanes, rows = lane_ids(), row_ids()
    numbers = level_numbers(groups)
    zero = jnp.zeros((SUB, LANES), jnp.float32)
    band = max(1, min(ny, 32 // nx))
    while ny % band:
        band -= 1
    cells = [(dj, i) for dj in range(band) for i in range(nx)]

    def loop(body, init=0):
        if band == ny:
            return body(0, init)
        return lax.fori_loop(0, ny // band, lambda step, carry: body(step * band, carry), init)

    def get(ref, j):
        return Many(ref[j + dj, i] for dj, i in cells)

    def put(ref, j, values):
        for (dj, i), value in zip(cells, values.items):
            ref[j + dj, i] = value

    def beside(values, step):
        return Many(values[dj * nx + min(max(i + step, 0), nx - 1)] for dj, i in cells)

    def below(ref, j, values):
        outside = [ref[jnp.maximum(j - 1, 0), i] for i in range(nx)] if band < ny else values.items[:nx]
        return Many(outside + values.items[:-nx])

    def above(ref, j, values):
        outside = [ref[jnp.minimum(j + band, ny - 1), i] for i in range(nx)] if band < ny else values.items[-nx:]
        return Many(values.items[nx:] + outside)

    def west_of(values):
        return beside(values, -1).where(lanes == LANES - 1, values).rolled(1)

    def east_of(values):
        return beside(values, 1).where(lanes == 0, values).rolled(-1)

    def south_of(ref, j, values):
        return below(ref, j, values).where(rows == SUB - 1, values).apply(lambda a: roll_rows(a, 1))

    def north_of(ref, j, values):
        return above(ref, j, values).where(rows == 0, values).apply(lambda a: roll_rows(a, -1))

    def depth(wet):
        return wet.apply(lambda m: GRAVITY_DT * (m + m * (m - 1.0) * (0.5 / levels)))

    def gather(j, carry):
        put(count_ref, j, Many(read(j + dj, i, 0) for dj, i in cells))
        return carry

    loop(gather)

    def faces(j, carry):
        count = get(count_ref, j)
        wet_u, wet_v = count.minimum(west_of(count)), count.minimum(south_of(count_ref, j, count))
        first_column = [(lanes == 0) if i == 0 else (lanes < 0) for dj, i in cells]
        first_row = [(rows == 0) & (j + dj == 0) for dj, i in cells]
        wet_u = Many([zero] * len(cells)).where(Many(first_column), wet_u)
        wet_v = Many([zero] * len(cells)).where(Many(first_row), wet_v)
        put(face_ref.at[0], j, depth(wet_u))
        put(face_ref.at[1], j, depth(wet_v))
        edge = Many(read(j + dj, i, CHUNK_EDGE) for dj, i in cells)
        wet_west = wet_u.apply(lambda a: jnp.broadcast_to(a[:, 0:1], (SUB, LANES)))
        reach = jnp.where(lanes < levels, lanes.astype(jnp.float32), float(levels))
        inside = edge.where(wet_west > reach, zero)
        col_u = inside.apply(lambda a: jnp.broadcast_to(jnp.sum(a, axis=1, keepdims=True), (SUB, LANES)))
        put(face_ref.at[4], j, col_u * GRAVITY_DT)
        wet_south = wet_v.apply(lambda a: row_of(a, 0))
        col_v = Many([zero] * len(cells))
        for q in range(groups):
            south = Many(read(j + dj, i, CHUNK_ROW + q * SUB) for dj, i in cells)
            col_v = col_v + south.where(wet_south > numbers[q], zero)
        col_v = col_v.apply(lambda a: jnp.broadcast_to(jnp.sum(a, axis=0, keepdims=True), (SUB, LANES)))
        put(face_ref.at[5], j, col_v * GRAVITY_DT)
        return carry

    loop(faces)

    def start(j, norm):
        load = Many(read(j + dj, i, CHUNK_LOAD) for dj, i in cells)
        col_u, col_v = get(face_ref.at[4], j), get(face_ref.at[5], j)
        depth_u, depth_v = get(face_ref.at[0], j), get(face_ref.at[1], j)
        last_column = Many((lanes == LANES - 1) if i + 1 < nx else (lanes < 0) for dj, i in cells)
        at_end = Many((lanes == LANES - 1) if i + 1 == nx else (lanes < 0) for dj, i in cells)
        last_row = Many((rows == SUB - 1) & (j + dj + 1 < ny) for dj, i in cells)
        at_top = Many((rows == SUB - 1) & (j + dj + 1 == ny) for dj, i in cells)
        none = Many([zero] * len(cells))
        load = load - col_u.where(lanes == 0, zero) - col_v.where(rows == 0, zero)
        load = load + beside(col_u, 1).where(last_column, none) + above(face_ref.at[5], j, col_v).where(last_row, none)
        put(face_ref.at[2], j, none.where(at_end, east_of(depth_u)))
        put(face_ref.at[3], j, none.where(at_top, north_of(face_ref.at[1], j, depth_v)))
        put(r_ref, j, load)
        put(p_ref, j, load)
        put(x_ref, j, none)
        return gathered(norm, load * load)

    def gathered(partial, values):
        items = list(values.items)
        while len(items) > 1:
            items = [a + b for a, b in zip(items[::2], items[1::2])] + items[len(items) // 2 * 2 :]
        return partial + items[0]

    norm = total(loop(start, zero))

    for iteration in range(ITERS):
        last = iteration + 1 == ITERS

        def image_of(j):
            p = get(p_ref, j)
            image = p + get(face_ref.at[0], j) * (p - west_of(p)) + get(face_ref.at[2], j) * (p - east_of(p))
            image = image + get(face_ref.at[1], j) * (p - south_of(p_ref, j, p))
            return p, image + get(face_ref.at[3], j) * (p - north_of(p_ref, j, p))

        def product(j, dot):
            p, image = image_of(j)
            put(face_ref.at[4], j, image)
            return gathered(dot, p * image)

        step = norm / total(loop(product, zero))

        def advance(j, new):
            put(x_ref, j, get(x_ref, j) + get(p_ref, j) * step)
            if last:
                return new
            residual = get(r_ref, j) - get(face_ref.at[4], j) * step
            put(r_ref, j, residual)
            return gathered(new, residual * residual)

        new = loop(advance, zero)
        if not last:
            new = total(new)
            ratio = new / norm
            norm = new

            def turn(j, carry):
                put(p_ref, j, get(r_ref, j) + get(p_ref, j) * ratio)
                return carry

            loop(turn)


def flow_kernel(
    levels, ny, nx, u_ref, v_ref, su_ref, sv_ref, ga_ref, gb_ref, y1_ref, y2_ref, x1_ref, x2_ref, dut_ref, dvt_ref,
    du_ref, dv_ref, eta_ref, count_s, face_s, x_s, r_s, p_s,
):
    groups = group_count(levels)
    lanes = lane_ids()
    core = lax.axis_index("core")
    my_j = lax.axis_index("ty")
    my_i = lax.axis_index("y") * 2 + core
    numbers = level_numbers(groups)
    thick = [1.0 + number * (1.0 / levels) for number in numbers]
    read_row, _ = slot_reader(y1_ref, y2_ref, groups)
    read_sides = side_reader(x1_ref, x2_ref)
    zero = jnp.zeros((SUB, LANES), jnp.float32)

    def read(j, i, first):
        where = (j * (nx // 2) + i // 2, pl.ds(first, SUB), slice(None))
        return jnp.where(core == i % 2, ga_ref[where], gb_ref[where])

    surface_solve(levels, ny, nx, read, count_s, face_s, x_s, r_s, p_s)
    eta_ref[...] = x_s[my_j, my_i]

    def near(dj, di, get):
        j, i = jnp.clip(my_j + dj, 0, ny - 1), jnp.clip(my_i + di, 0, nx - 1)
        inside = (my_j + dj >= 0) & (my_j + dj < ny) & (my_i + di >= 0) & (my_i + di < nx)
        return jnp.where(inside, get(j, i), 0.0)

    def around(ref):
        tiles = [[near(dj, di, lambda j, i: ref[j, i]) for di in (-1, 0, 1)] for dj in (-1, 0, 1)]
        return [row[1] for row in tiles], [edge_of_tile(*row) for row in tiles]

    count_tiles, x_tiles = around(count_s), around(x_s)

    corner_tiles = {
        name: near(dj, di, lambda j, i: read(j, i, CHUNK_EDGE))
        for name, dj, di in (("se", -1, 1), ("sw", -1, -1), ("nw", 1, -1), ("ne", 1, 1))
    }

    def insert_corners(edge, name, row):
        for which, value, target in CORNER_PLACES.get((name, row), ()):
            for q in range(groups):
                lane = SEG * q + target
                source = CORNER_LANE + CORNER_STEP * q + value
                edge = jnp.where(lanes == lane, roll_lanes(corner_tiles[which], lane - source), edge)
        return edge

    sides = [read_sides(row) for row in range(SUB)]
    west, east = Many(side[0] for side in sides), Many(side[1] for side in sides)

    def rows(name, ref, q, first, last):
        south = [read_row(name, row, q) for row in range(first, 0)]
        north = [read_row(name, row, q) for row in range(SUB, last + 1)]
        return Many(south + load_rows(ref, q, levels).items + north)

    def edges(name, ref, first, last):
        out = edges_of_groups([rows(name, ref, q, first, last) for q in range(groups)])
        south = [insert_corners(out[row - first], name, row) for row in range(first, 0)]
        north = [insert_corners(out[row - first], name, row) for row in range(SUB, last + 1)]
        inner = insert_sides(out[-first : SUB - first], west, east, FIELDS.index(name))
        return Many(south + inner.items + north)

    total_rows = ny * SUB
    first_row = (my_j * SUB).astype(jnp.float32)
    turn_u = Many(0.5 + (first_row + (row + 0.5)) * (1.0 / total_rows) for row in range(-1, 8))
    turn_v = Many(-0.5 - (first_row + row) * (1.0 / total_rows) for row in range(0, 9))

    def adjoint(part, u, v, su, sv):
        kind = 1 if part == groups else 0
        level = numbers[part]
        counts, x = rows_of(count_tiles[kind], -2, 8), rows_of(x_tiles[kind], -2, 8)
        wet_u = counts[1:].minimum(counts[1:].at(-1)) > level
        wet_v = counts[1:].minimum(counts[:-1]) > level
        u_cot = su + ((x[1:] - x[1:].at(-1)) * thick[part]).where(wet_u, zero)
        v_cot = sv + ((x[1:] - x[:-1]) * thick[part]).where(wet_v, zero)
        a, b = (u_cot * ADVECT).where(wet_u, zero), (v_cot * ADVECT).where(wet_v, zero)
        v_pair = v[:-1] + v[1:]
        av = a * (v_pair + v_pair.at(-1)) * 0.25
        u_pair = u[2:10] + u[1:9]
        bu = b[1:9] * (u_pair + u_pair.at(1)) * 0.25
        au, bv = a[1:9] * u[2:10], b * v[:-1]
        to_v_bar = a[:-1] * ((u[:-2] - u[2:]) * 0.5 + turn_u)
        to_u_bar = b[1:] * ((v[1:10].at(-1) - v[1:10].at(1)) * 0.5 + turn_v)
        near_u, near_v = to_u_bar[:-1] + to_u_bar[1:], to_v_bar[1:] + to_v_bar[:-1]
        twist_u = au.at(1) - au.at(-1) - a[1:9] * (u[2:10].at(1) - u[2:10].at(-1)) + av[2:] - av[:-2]
        twist_v = bu.at(1) - bu.at(-1) - b[1:9] * (v[2:10] - v[0:8]) + bv[2:] - bv[:-2]
        du = u_cot[1:9] + twist_u * 0.5 + (near_u + near_u.at(-1)) * 0.25
        dv = v_cot[1:9] + twist_v * 0.5 + (near_v + near_v.at(1)) * 0.25
        return du, dv

    fields = (("u", u_ref, -2, 8), ("v", v_ref, -1, 9), ("su", su_ref, -1, 8), ("sv", sv_ref, -1, 8))
    edge_u, edge_v = adjoint(groups, *(edges(*field) for field in fields))
    for q in range(groups):
        du, dv = adjoint(q, *(rows(name, ref, q, first, last) for name, ref, first, last in fields))
        store_rows(du_ref, q, levels, merge_edges(du, edge_u, q) + load_rows(dut_ref, q, levels))
        store_rows(dv_ref, q, levels, merge_edges(dv, edge_v, q) + load_rows(dvt_ref, q, levels))


def swaps(mesh_shape, along, parity):
    ny, nx = mesh_shape
    pairs = []
    for j in range(ny):
        for i in range(nx):
            k, size = (j, ny) if along == "y" else (i, nx)
            other = k + 1 if k % 2 == parity else k - 1
            if 0 <= other < size:
                pairs.append((j * nx + i, other * nx + i if along == "y" else j * nx + other))
    return pairs


def call(kernel, outs, args, scratch=(), flops=0, size=0, far_in=False, far_out=(), limit=48):
    near, far = pl.BlockSpec(memory_space=pltpu.VMEM), pl.BlockSpec(memory_space=pltpu.HBM)
    outs = [out if isinstance(out, jax.ShapeDtypeStruct) else jax.ShapeDtypeStruct(out, jnp.float32) for out in outs]
    return pl.pallas_call(
        kernel,
        out_shape=outs,
        in_specs=[far if far_in else near] * len(args),
        out_specs=[far if n in far_out else near for n in range(len(outs))],
        scratch_shapes=list(scratch),
        compiler_params=pltpu.CompilerParams(vmem_limit_bytes=limit * 1024 * 1024),
        cost_estimate=pl.CostEstimate(flops=flops, bytes_accessed=size, transcendentals=0),
    )(*args)


def on_device(shape, u, v, t, count, su, sv, st, elev):
    ny, nx = shape
    levels = u.shape[0]
    groups = group_count(levels)
    flat = (levels * SUB, LANES)
    u, v, t, su, sv, st = (field.reshape(flat) for field in (u, v, t, su, sv, st))
    peers = ny * nx // 2
    row_packet = ((N_SLOTS * groups + 1) * SUB, LANES)
    column_packet = ((SUB + 1) * SUB, LANES)
    chunk = (peers, CHUNK_ROW + groups * SUB, LANES)
    tile = (SUB, LANES)
    y1, y2, xp, chunks = call(
        functools.partial(pack_kernel, levels, peers),
        [row_packet, row_packet, column_packet, chunk],
        (u, v, t, su, sv, st, count, elev),
        scratch=[pltpu.VMEM(flat, jnp.float32)] * 6
        + [pltpu.VMEM(tile, count.dtype)]
        + [pltpu.VMEM(shape, jnp.float32) for shape in (tile, row_packet, row_packet, column_packet, chunk[1:])]
        + [pltpu.SemaphoreType.DMA((9,))],
        flops=1 << 20,
        size=1 << 21,
        far_in=True,
        far_out=(0, 1, 2, 3),
        limit=60,
    )
    axes = ("ty", "y", "core")
    ga = lax.all_to_all(chunks, ("ty", "y"), 0, 0)
    x1 = lax.ppermute(xp, axes, swaps(shape, "x", 0))
    x2 = lax.ppermute(xp, axes, swaps(shape, "x", 1))
    y1 = lax.ppermute(y1, axes, swaps(shape, "y", 0))
    y2 = lax.ppermute(y2, axes, swaps(shape, "y", 1))
    dt, du_t, dv_t = call(
        functools.partial(tracer_kernel, levels),
        [flat] * 3,
        (u, v, t, st, count, y1, y2, x1, x2),
        flops=1 << 22,
        size=1 << 21,
    )
    ga, du_t = lax.optimization_barrier((ga, du_t))
    gb = lax.ppermute(ga, axes, swaps(shape, "x", 0))
    grid = pltpu.VMEM((ny, nx, SUB, LANES), jnp.float32)
    faces = pltpu.VMEM((6, ny, nx, SUB, LANES), jnp.float32)
    du, dv, eta = call(
        functools.partial(flow_kernel, levels, ny, nx),
        [flat, flat, (SUB, LANES)],
        (u, v, su, sv, ga, gb, y1, y2, x1, x2, du_t, dv_t),
        scratch=(grid, faces, grid, grid, grid),
        flops=1 << 23,
        size=1 << 22,
    )
    whole = (levels, SUB, LANES)
    return du.reshape(whole), dv.reshape(whole), dt.reshape(whole), eta


def solution(mesh):
    ny, nx = mesh.shape["ty"], mesh.shape["tx"]
    split = Mesh(mesh.devices.reshape(ny, nx // 2, 2), ("ty", "y", "core"))
    deep, flat = P(None, "ty", ("y", "core")), P("ty", ("y", "core"))
    return jax.shard_map(
        functools.partial(on_device, (ny, nx)),
        mesh=split,
        in_specs=(deep, deep, deep, flat, deep, deep, deep, flat),
        out_specs=(deep, deep, deep, flat),
        check_vma=False,
    )
```

time: 50.3 us -> 33.4 us (0.66)
  the two profiles are of different devices: /device:TPU:3 before, /device:TPU:11 now
where the time goes in v2:
time: 33.4 us; the launch traced here: 33.1 us
  starting transfers between devices  17.5 us (52%)
  Pallas kernels  7.98 us (24%)
  waiting for transfers between devices  6.71 us (20%)
  between operations  0.78 us (2%)
    pallas_call x3, Pallas kernels, call(): pl.pallas_call(kernel, out_shape=outs, in_specs=[far if far_in else near]...  7.98 us
    all_to_all x1, starting transfers between devices, on_device(): ga = lax.all_to_all(chunks, ('ty', 'y'), 0, 0)  6.78 us
    ppermute x1, starting transfers between devices, on_device(): x2 = lax.ppermute(xp, axes, swaps(shape, 'x', 1))  4.9 us
    ppermute x1, starting transfers between devices, on_device(): y2 = lax.ppermute(y2, axes, swaps(shape, 'y', 1))  3.98 us
    ppermute x1, waiting for transfers between devices, on_device(): x2 = lax.ppermute(xp, axes, swaps(shape, 'x', 1))  2.66 us
    ppermute x1, waiting for transfers between devices, on_device(): y2 = lax.ppermute(y2, axes, swaps(shape, 'y', 1))  2.6 us
    ppermute x1, starting transfers between devices, on_device(): gb = lax.ppermute(ga, axes, swaps(shape, 'x', 0))  1.45 us
    ppermute x1, waiting for transfers between devices, on_device(): gb = lax.ppermute(ga, axes, swaps(shape, 'x', 0))  1.44 us
  transfers between devices with their start and end apart: 6, of which 3 were waited for; matrix products, arithmetic and copies ran while one was open for 0% of the time, Pallas kernels for 5%

profile of v2, /device:TPU:11, one launch (start us, length us, event | category | flops | bytes accessed | tf_op | source)
XLA Modules:
  0.0 33.1 jit_solution(17499696978991678139)
XLA Ops:
  0.6 2.5 %shard_map.111 = (f32[296,128]{1,0:T(8,128)}, f32[296,128]{1,0:T(8,128)}, f32[72,128]{1,0:T(8,128)}, f32[16,56,128]{2,1,0:T(8,128)}) custom-call(f32[240,128]{1,0:T(8,128)} %bitcast.9, f32[240,128]{1,0:T(8,128)} %bitcast.12, f32[240,128]{1,0:T(8,128)} %bitcast.15, f32[240,128]{1,0:T(8,128)} %bitcast.19, f32[240,128]{1,0:T(8,128)} %bitcast.21, ...), custom_call_target="tpu_custom_call" | custom-call | flops 1048576 | bytes 2097152 | tf_op jit(solution)/shard_map/pallas_call | solution.py:601
  3.1 0.0 copy-start.8
  3.1 0.0 copy-start.7
  3.1 0.0 copy-start.9
  3.1 0.0 copy-start
  3.1 0.0 copy-start.1
  3.2 0.0 copy-start.2
  3.2 0.0 copy-start.3
  3.2 6.8 %all-to-all-start = ((f32[16,56,128]{2,1,0:T(8,128)}), f32[16,56,128]{2,1,0:T(8,128)S(1)}, u32[]{:S(2)}, u32[]{:S(2)}) async-start(f32[16,56,128]{2,1,0:T(8,128)} %get-tuple-element.16), calls=%async_computation | async-start | bytes 917504 | tf_op jit(solution)/shard_map/all_to_all | solution.py:638
  10.0 0.0 copy-start.6
  10.0 0.0 copy-done.8
  10.0 0.3 %collective-permute-start = (f32[296,128]{1,0:T(8,128)S(1)}, f32[296,128]{1,0:T(8,128)S(1)}, u32[]{:S(2)}, u32[]{:S(2)}) collective-permute-start(f32[296,128]{1,0:T(8,128)S(1)} %copy-done.8), channel_id=1, source_target_pairs={{0,4},{1,5},{2,6},{3,7},{4,0},{5,1},{6,2},{7,3},{8,12},{9,13},{10,... | collective-permute-start | bytes 454664 | tf_op jit(solution)/shard_map/ppermute | solution.py:641
  10.3 0.0 copy-done.7
  10.3 4.0 %collective-permute-start.1 = (f32[296,128]{1,0:T(8,128)S(1)}, f32[296,128]{1,0:T(8,128)S(1)}, u32[]{:S(2)}, u32[]{:S(2)}) collective-permute-start(f32[296,128]{1,0:T(8,128)S(1)} %copy-done.7), channel_id=1, source_target_pairs={{4,8},{5,9},{6,10},{7,11},{8,4},{9,5},{10,6},{11,7},{12,16},{13,17... | collective-permute-start | bytes 454664 | tf_op jit(solution)/shard_map/ppermute | solution.py:642
  14.3 0.0 copy-done.9
  14.3 0.0 copy-start.4
  14.3 0.0 copy-start.5
  14.3 4.9 %collective-permute-start.3 = (f32[72,128]{1,0:T(8,128)S(1)}, f32[72,128]{1,0:T(8,128)S(1)}, u32[]{:S(2)}, u32[]{:S(2)}) collective-permute-start(f32[72,128]{1,0:T(8,128)S(1)} %copy-done.9), channel_id=1, source_target_pairs={{1,2},{2,1},{5,6},{6,5},{9,10},{10,9},{13,14},{14,13},{17,18},{18,... | collective-permute-start | bytes 110600 | tf_op jit(solution)/shard_map/ppermute | solution.py:640
  19.3 0.1 collective-permute-start.2
  19.3 2.7 %collective-permute-done.3.x2_ref = f32[72,128]{1,0:T(8,128)S(1)} collective-permute-done((f32[72,128]{1,0:T(8,128)S(1)}, f32[72,128]{1,0:T(8,128)S(1)}, u32[]{:S(2)}, u32[]{:S(2)}) %collective-permute-start.3) | collective-permute-done | bytes 36896 | tf_op jit(solution)/shard_map/ppermute | solution.py:640
  22.0 0.0 collective-permute-done.2.x1_ref
  22.0 0.0 collective-permute-done.y1_ref
  22.0 2.6 %collective-permute-done.1.y2_ref = f32[296,128]{1,0:T(8,128)S(1)} collective-permute-done((f32[296,128]{1,0:T(8,128)S(1)}, f32[296,128]{1,0:T(8,128)S(1)}, u32[]{:S(2)}, u32[]{:S(2)}) %collective-permute-start.1) | collective-permute-done | bytes 151584 | tf_op jit(solution)/shard_map/ppermute | solution.py:642
  24.6 0.0 copy-done
  24.6 0.0 copy-done.1
  24.6 0.0 copy-done.2
  24.6 0.0 copy-done.3
  24.6 0.0 copy-done.6
  24.6 1.6 %shard_map.112 = (f32[240,128]{1,0:T(8,128)}, f32[240,128]{1,0:T(8,128)S(1)}, f32[240,128]{1,0:T(8,128)S(1)}) custom-call(f32[240,128]{1,0:T(8,128)S(1)} %bitcast.10, f32[240,128]{1,0:T(8,128)S(1)} %bitcast.13, f32[240,128]{1,0:T(8,128)S(1)} %bitcast.16, f32[240,128]{1,0:T(8,128)S(1)} %bitcast.18, s32[8,128]{1,0:T(8,128)S(1)} %copy-done.6, ...), custom_call_target="tpu_custom_call" | custom-call | flops 4194304 | bytes 2097152 | tf_op jit(solution)/shard_map/pallas_call | solution.py:601
  26.3 0.0 all-to-all-done.ga_ref
  26.3 1.5 %collective-permute-start.4 = (f32[16,56,128]{2,1,0:T(8,128)S(1)}, f32[16,56,128]{2,1,0:T(8,128)S(1)}, u32[]{:S(2)}, u32[]{:S(2)}) collective-permute-start(f32[16,56,128]{2,1,0:T(8,128)S(1)} %all-to-all-done.ga_ref), channel_id=1, source_target_pairs={{0,1},{1,0},{2,3},{3,2},{4,5},{5,4},{6,7},{7,6},{8,9},{9,8},{10,11... | collective-permute-start | bytes 1376264 | tf_op jit(solution)/shard_map/ppermute | solution.py:651
  27.7 1.4 %collective-permute-done.4.gb_ref = f32[16,56,128]{2,1,0:T(8,128)S(1)} collective-permute-done((f32[16,56,128]{2,1,0:T(8,128)S(1)}, f32[16,56,128]{2,1,0:T(8,128)S(1)}, u32[]{:S(2)}, u32[]{:S(2)}) %collective-permute-start.4) | collective-permute-done | bytes 458784 | tf_op jit(solution)/shard_map/ppermute | solution.py:651
  29.2 0.0 copy-done.4
  29.2 0.0 copy-done.5
  29.2 3.9 %shard_map.113 = (f32[240,128]{1,0:T(8,128)}, f32[240,128]{1,0:T(8,128)}, f32[8,128]{1,0:T(8,128)}) custom-call(f32[240,128]{1,0:T(8,128)S(1)} %bitcast.11, f32[240,128]{1,0:T(8,128)S(1)} %bitcast.14, f32[240,128]{1,0:T(8,128)S(1)} %bitcast.20, f32[240,128]{1,0:T(8,128)S(1)} %bitcast.22, f32[16,56,128]{2,1,0:T(8,128)S(1)} %all-to-all-done.ga_ref, ...), custom_call_target="tpu_custom_call" | custom-call | flops 8388608 | bytes 4194304 | tf_op jit(solution)/shard_map/pallas_call | solution.py:601
Async XLA Ops:
  3.1 6.9 %copy-start.8 = (f32[296,128]{1,0:T(8,128)S(1)}, f32[296,128]{1,0:T(8,128)}, u32[]{:S(2)}) copy-start(f32[296,128]{1,0:T(8,128)} %get-tuple-element.17) | copy-start | bytes 454660
  3.1 7.2 %copy-start.7 = (f32[296,128]{1,0:T(8,128)S(1)}, f32[296,128]{1,0:T(8,128)}, u32[]{:S(2)}) copy-start(f32[296,128]{1,0:T(8,128)} %get-tuple-element.18) | copy-start | bytes 454660
  3.1 11.2 %copy-start.9 = (f32[72,128]{1,0:T(8,128)S(1)}, f32[72,128]{1,0:T(8,128)}, u32[]{:S(2)}) copy-start(f32[72,128]{1,0:T(8,128)} %get-tuple-element.19) | copy-start | bytes 110596
  3.1 21.5 %copy-start = (f32[30,8,128]{2,1,0:T(8,128)S(1)}, f32[30,8,128]{2,1,0:T(8,128)}, u32[]{:S(2)}) copy-start(f32[30,8,128]{2,1,0:T(8,128)} %param.8) | copy-start | bytes 368644
  3.1 21.5 %copy-start.1 = (f32[30,8,128]{2,1,0:T(8,128)S(1)}, f32[30,8,128]{2,1,0:T(8,128)}, u32[]{:S(2)}) copy-start(f32[30,8,128]{2,1,0:T(8,128)} %param.9) | copy-start | bytes 368644
  3.2 21.5 %copy-start.2 = (f32[30,8,128]{2,1,0:T(8,128)S(1)}, f32[30,8,128]{2,1,0:T(8,128)}, u32[]{:S(2)}) copy-start(f32[30,8,128]{2,1,0:T(8,128)} %param.10) | copy-start | bytes 368644
  3.2 21.5 %copy-start.3 = (f32[30,8,128]{2,1,0:T(8,128)S(1)}, f32[30,8,128]{2,1,0:T(8,128)}, u32[]{:S(2)}) copy-start(f32[30,8,128]{2,1,0:T(8,128)} %param.14) | copy-start | bytes 368644
  3.2 23.1 %all-to-all-start = ((f32[16,56,128]{2,1,0:T(8,128)}), f32[16,56,128]{2,1,0:T(8,128)S(1)}, u32[]{:S(2)}, u32[]{:S(2)}) async-start(f32[16,56,128]{2,1,0:T(8,128)} %get-tuple-element.16), calls=%async_computation | async-start | bytes 917504 | tf_op jit(solution)/shard_map/all_to_all | solution.py:638
  10.0 14.7 %copy-start.6 = (s32[8,128]{1,0:T(8,128)S(1)}, s32[8,128]{1,0:T(8,128)}, u32[]{:S(2)}) copy-start(s32[8,128]{1,0:T(8,128)} %count_ref.1) | copy-start | bytes 12292
  10.0 12.0 %collective-permute-start = (f32[296,128]{1,0:T(8,128)S(1)}, f32[296,128]{1,0:T(8,128)S(1)}, u32[]{:S(2)}, u32[]{:S(2)}) collective-permute-start(f32[296,128]{1,0:T(8,128)S(1)} %copy-done.8), channel_id=1, source_target_pairs={{0,4},{1,5},{2,6},{3,7},{4,0},{5,1},{6,2},{7,3},{8,12},{9,13},{10,... | collective-permute-start | bytes 454664 | tf_op jit(solution)/shard_map/ppermute | solution.py:641
  10.3 14.3 %collective-permute-start.1 = (f32[296,128]{1,0:T(8,128)S(1)}, f32[296,128]{1,0:T(8,128)S(1)}, u32[]{:S(2)}, u32[]{:S(2)}) collective-permute-start(f32[296,128]{1,0:T(8,128)S(1)} %copy-done.7), channel_id=1, source_target_pairs={{4,8},{5,9},{6,10},{7,11},{8,4},{9,5},{10,6},{11,7},{12,16},{13,17... | collective-permute-start | bytes 454664 | tf_op jit(solution)/shard_map/ppermute | solution.py:642
  14.3 14.9 %copy-start.4 = (f32[30,8,128]{2,1,0:T(8,128)S(1)}, f32[30,8,128]{2,1,0:T(8,128)}, u32[]{:S(2)}) copy-start(f32[30,8,128]{2,1,0:T(8,128)} %param.12) | copy-start | bytes 368644
  14.3 14.9 %copy-start.5 = (f32[30,8,128]{2,1,0:T(8,128)S(1)}, f32[30,8,128]{2,1,0:T(8,128)}, u32[]{:S(2)}) copy-start(f32[30,8,128]{2,1,0:T(8,128)} %param.13) | copy-start | bytes 368644
  14.3 7.7 %collective-permute-start.3 = (f32[72,128]{1,0:T(8,128)S(1)}, f32[72,128]{1,0:T(8,128)S(1)}, u32[]{:S(2)}, u32[]{:S(2)}) collective-permute-start(f32[72,128]{1,0:T(8,128)S(1)} %copy-done.9), channel_id=1, source_target_pairs={{1,2},{2,1},{5,6},{6,5},{9,10},{10,9},{13,14},{14,13},{17,18},{18,... | collective-permute-start | bytes 110600 | tf_op jit(solution)/shard_map/ppermute | solution.py:640
  19.3 2.7 %collective-permute-start.2 = (f32[72,128]{1,0:T(8,128)S(1)}, f32[72,128]{1,0:T(8,128)S(1)}, u32[]{:S(2)}, u32[]{:S(2)}) collective-permute-start(f32[72,128]{1,0:T(8,128)S(1)} %copy-done.9), channel_id=1, source_target_pairs={{0,1},{1,0},{2,3},{3,2},{4,5},{5,4},{6,7},{7,6},{8,9},{9,8},{10,11... | collective-permute-start | bytes 110600 | tf_op jit(solution)/shard_map/ppermute | solution.py:639
  26.3 2.9 %collective-permute-start.4 = (f32[16,56,128]{2,1,0:T(8,128)S(1)}, f32[16,56,128]{2,1,0:T(8,128)S(1)}, u32[]{:S(2)}, u32[]{:S(2)}) collective-permute-start(f32[16,56,128]{2,1,0:T(8,128)S(1)} %all-to-all-done.ga_ref), channel_id=1, source_target_pairs={{0,1},{1,0},{2,3},{3,2},{4,5},{5,4},{6,7},{7,6},{8,9},{9,8},{10,11... | collective-permute-start | bytes 1376264 | tf_op jit(solution)/shard_map/ppermute | solution.py:651

commit v3 on v2

--- a/solution.py
+++ b/solution.py
@@ -15,6 +15,7 @@
 LANES = 128
 SEG = 32
 FIELDS = ("u", "v", "t", "st", "su", "sv")
+FLOW_FIELDS = ("u", "v", "su", "sv")
 SOUTH_SLOTS = {("u", -2): 0, ("u", -1): 1, ("v", -1): 2, ("t", -2): 3, ("t", -1): 4, ("st", -2): 5, ("st", -1): 6}
 SOUTH_SLOTS.update({("su", -1): 7, ("sv", -1): 8})
 NORTH_SLOTS = {("u", 8): 0, ("v", 8): 1, ("v", 9): 2, ("t", 8): 3, ("st", 8): 5, ("st", 9): 6, ("su", 8): 7, ("sv", 8): 8}
@@ -94,59 +95,68 @@
     return jnp.where(lanes < 2 * SEG, out, roll_lanes(out, 2 * SEG))
 
 
-def pack_kernel(
-    levels, peers, u_hbm, v_hbm, t_hbm, su_hbm, sv_hbm, st_hbm, count_hbm, elev_hbm,
-    y1_hbm, y2_hbm, x_hbm, chunk_hbm,
-    u_ref, v_ref, t_ref, su_ref, sv_ref, st_ref, count_ref, elev_ref, y1_ref, y2_ref, x_ref, chunk_ref, sems,
+def chunk_kernel(
+    levels, peers, u_hbm, v_hbm, su_hbm, sv_hbm, count_hbm, elev_hbm, chunk_hbm,
+    u_ref, v_ref, su_ref, sv_ref, count_ref, elev_ref, chunk_ref, sems,
 ):
     pairs = (
-        (count_hbm, count_ref), (su_hbm, su_ref), (sv_hbm, sv_ref), (elev_hbm, elev_ref),
-        (u_hbm, u_ref), (v_hbm, v_ref), (t_hbm, t_ref), (st_hbm, st_ref),
+        (count_hbm, count_ref), (su_hbm, su_ref), (sv_hbm, sv_ref), (elev_hbm, elev_ref), (u_hbm, u_ref), (v_hbm, v_ref),
     )
     copies = [pltpu.make_async_copy(source, target, sems.at[n]) for n, (source, target) in enumerate(pairs)]
     for copy in copies:
         copy.start()
-    for copy in copies:
-        copy.wait()
     groups = group_count(levels)
     lanes, rows = lane_ids(), row_ids()
+    refs = {"u": u_ref, "v": v_ref, "su": su_ref, "sv": sv_ref}
+    for copy in copies[:4]:
+        copy.wait()
+    count = count_ref[...].astype(jnp.float32)
+    zero = jnp.zeros((SUB, LANES), jnp.float32)
+
+    wet_u = jnp.where(lanes == 0, 0.0, jnp.minimum(count, roll_lanes(count, 1)))
+    wet_v = jnp.where(rows == 0, 0.0, jnp.minimum(count, roll_rows(count, 1)))
+    col_u, col_v, edge = [zero] * 4, [zero] * 4, zero
+    for k in range(levels):
+        su_level = su_ref[k * SUB : (k + 1) * SUB, :]
+        col_u[k % 4] = col_u[k % 4] + jnp.where(wet_u > float(k), su_level, 0.0)
+        col_v[k % 4] = col_v[k % 4] + jnp.where(wet_v > float(k), sv_ref[k * SUB : (k + 1) * SUB, :], 0.0)
+        edge = jnp.where(lanes == k, roll_lanes(su_level, k), edge)
+    col_u, col_v = ((col[0] + col[1]) + (col[2] + col[3]) for col in (col_u, col_v))
+    load = elev_ref[...] + GRAVITY_DT * (at(col_u, 1) - col_u + roll_rows(col_v, -1) - col_v)
+
+    for copy in copies[4:]:
+        copy.wait()
+    for place, (name, row, column) in enumerate(CORNERS):
+        for q in range(groups):
+            lane = CORNER_LANE + CORNER_STEP * q + place
+            edge = jnp.where(lanes == lane, roll_lanes(load_group(refs[name], row, q, levels), lane - column), edge)
+
+    chunk_ref[0:SUB, :] = count
+    chunk_ref[CHUNK_LOAD : CHUNK_LOAD + SUB, :] = load
+    chunk_ref[CHUNK_EDGE : CHUNK_EDGE + SUB, :] = edge
+    for q in range(groups):
+        chunk_ref[CHUNK_ROW + q * SUB : CHUNK_ROW + (q + 1) * SUB, :] = load_group(sv_ref, 0, q, levels)
+
+    def put(peer, carry):
+        pltpu.make_async_copy(chunk_ref, chunk_hbm.at[peer], sems.at[len(pairs)]).start()
+        return carry
+
+    lax.fori_loop(0, peers, put, 0, unroll=peers <= 32)
+    pltpu.make_async_copy(chunk_hbm, chunk_hbm, sems.at[len(pairs)]).wait()
+
+
+def packet_kernel(levels, u_ref, v_ref, t_ref, su_ref, sv_ref, st_ref, count_ref, y1_ref, y2_ref, x_ref):
+    groups = group_count(levels)
+    lanes = lane_ids()
+    zero = jnp.zeros((SUB, LANES), jnp.float32)
+    count = count_ref[...].astype(jnp.float32)
     even = lax.axis_index("ty") % 2 == 0
     refs = {"u": u_ref, "v": v_ref, "t": t_ref, "st": st_ref, "su": su_ref, "sv": sv_ref}
-    count = count_ref[...].astype(jnp.float32)
-    zero = jnp.zeros((SUB, LANES), jnp.float32)
-
-    wet_u = jnp.where(lanes == 0, 0.0, jnp.minimum(count, roll_lanes(count, 1)))
-    wet_v = jnp.where(rows == 0, 0.0, jnp.minimum(count, roll_rows(count, 1)))
-    col_u, col_v, edge = zero, zero, zero
-    for k in range(levels):
-        su_level = su_ref[k * SUB : (k + 1) * SUB, :]
-        col_u = col_u + jnp.where(wet_u > float(k), su_level, 0.0)
-        col_v = col_v + jnp.where(wet_v > float(k), sv_ref[k * SUB : (k + 1) * SUB, :], 0.0)
-        edge = jnp.where(lanes == k, roll_lanes(su_level, k), edge)
-    load = elev_ref[...] + GRAVITY_DT * (at(col_u, 1) - col_u + roll_rows(col_v, -1) - col_v)
-
     loaded = {}
     for name in FIELDS:
         for row in range(SUB):
             for q in range(groups):
                 loaded[name, row, q] = load_group(refs[name], row, q, levels)
-
-    for place, (name, row, column) in enumerate(CORNERS):
-        for q in range(groups):
-            lane = CORNER_LANE + CORNER_STEP * q + place
-            edge = jnp.where(lanes == lane, roll_lanes(loaded[name, row, q], lane - column), edge)
-
-    chunk_ref[0:SUB, :] = count
-    chunk_ref[CHUNK_LOAD : CHUNK_LOAD + SUB, :] = load
-    chunk_ref[CHUNK_EDGE : CHUNK_EDGE + SUB, :] = edge
-    for q in range(groups):
-        chunk_ref[CHUNK_ROW + q * SUB : CHUNK_ROW + (q + 1) * SUB, :] = loaded["sv", 0, q]
-
-    def put(peer, carry):
-        pltpu.make_async_copy(chunk_ref, chunk_hbm.at[peer], sems.at[len(pairs)]).start()
-        return carry
-
-    lax.fori_loop(0, peers, put, 0, unroll=peers <= 32)
 
     for slot in range(N_SLOTS):
         upper = [(name, row + SUB) for (name, row), place in SOUTH_SLOTS.items() if place == slot]
@@ -159,9 +169,6 @@
             y2_ref[place, :] = jnp.where(even, to_south, to_north)
     y1_ref[N_SLOTS * groups * SUB :, :] = count
     y2_ref[N_SLOTS * groups * SUB :, :] = count
-    out = [pltpu.make_async_copy(y1_ref, y1_hbm, sems.at[0]), pltpu.make_async_copy(y2_ref, y2_hbm, sems.at[1])]
-    out[0].start()
-    out[1].start()
 
     for row in range(SUB):
         packet = zero
@@ -171,11 +178,6 @@
                 packet = jnp.where((lanes >= lane) & (lanes < lane + 4), roll_lanes(loaded[name, row, q], lane + 2), packet)
         x_ref[row * SUB : (row + 1) * SUB, :] = packet
     x_ref[SUB * SUB :, :] = count
-    out.append(pltpu.make_async_copy(x_ref, x_hbm, sems.at[2]))
-    out[2].start()
-    for copy in out:
-        copy.wait()
-    pltpu.make_async_copy(chunk_hbm, chunk_hbm, sems.at[len(pairs)]).wait()
 
 
 class Many:
@@ -283,26 +285,26 @@
     return ((t0 + t_before) * 7.0 - (t_after + t_before2)) * (1.0 / 12.0)
 
 
-def tracer_kernel(levels, u_ref, v_ref, t_ref, st_ref, count_ref, y1_ref, y2_ref, x1_ref, x2_ref, dt_ref, du_ref, dv_ref):
+def edge_rows(ref, west, east, levels, groups, name):
+    own = edges_of_groups([load_rows(ref, q, levels) for q in range(groups)])
+    return insert_sides(own, west, east, FIELDS.index(name))
+
+
+def column_kernel(
+    levels, u_ref, v_ref, t_ref, st_ref, su_ref, sv_ref, count_ref, x1_ref, x2_ref, dt_ref, du_ref, edge_ref
+):
     groups = group_count(levels)
-    read_row, read_counts = slot_reader(y1_ref, y2_ref, groups)
     read_sides = side_reader(x1_ref, x2_ref)
     numbers = level_numbers(groups)
     zero = jnp.zeros((SUB, LANES), jnp.float32)
-
     count = count_ref[...].astype(jnp.float32)
-    count_south, count_north = read_counts()
     count_west, count_east = read_sides(SUB)
     count_edge = edge_of_tile(count_west, count, count_east)
-    counts = rows_of((count_south, count, count_north), -2, 9)
-    counts_v = counts[1:].minimum(counts[:-1])
-    own = (None, count, None)
-    counts_u = rows_of((None, jnp.minimum(count, at(count, -1)), None), 0, 7)
-    edge_counts = rows_of((None, count_edge, None), 0, 7)
-    edge_counts_u = rows_of((None, jnp.minimum(count_edge, at(count_edge, -1)), None), 0, 7)
-    del own
-
-    def along_columns(level, wet, wet_u, u, t, st):
+
+    def counts(tile):
+        return tuple(rows_of((None, part, None), 0, 7) for part in (tile, jnp.minimum(tile, at(tile, -1))))
+
+    def along(level, wet, wet_u, u, t, st):
         cell = (st * -ADVECT).where(wet > level, zero)
         flux = (cell.at(-1) - cell).where(wet_u > level, zero)
         back = u * flux
@@ -312,13 +314,33 @@
     sides = [read_sides(row) for row in range(SUB)]
     west, east = Many(side[0] for side in sides), Many(side[1] for side in sides)
     u, t, st = (
-        insert_sides(
-            edges_of_groups([load_rows(ref, q, levels) for q in range(groups)]), west, east, FIELDS.index(name)
-        )
-        for name, ref in (("u", u_ref), ("t", t_ref), ("st", st_ref))
-    )
-    edge_t, edge_u = along_columns(numbers[groups], edge_counts, edge_counts_u, u, t, st)
-
+        edge_rows(ref, west, east, levels, groups, name) for name, ref in (("u", u_ref), ("t", t_ref), ("st", st_ref))
+    )
+    edge_t, edge_u = along(numbers[groups], *counts(count_edge), u, t, st)
+    own = counts(count)
+    for q in range(groups):
+        st = load_rows(st_ref, q, levels)
+        from_x, to_u = along(numbers[q], *own, load_rows(u_ref, q, levels), load_rows(t_ref, q, levels), st)
+        store_rows(dt_ref, q, levels, st + merge_edges(from_x, edge_t, q))
+        store_rows(du_ref, q, levels, merge_edges(to_u, edge_u, q))
+    flow = (u,) + tuple(
+        edge_rows(ref, west, east, levels, groups, name) for name, ref in (("v", v_ref), ("su", su_ref), ("sv", sv_ref))
+    )
+    for n, rows in enumerate(flow):
+        for row in range(SUB):
+            edge_ref[(n * SUB + row) * SUB : (n * SUB + row + 1) * SUB, :] = rows[row]
+
+
+def row_kernel(levels, v_ref, t_ref, st_ref, count_ref, y1_ref, y2_ref, dtx_ref, dt_hbm, dv_ref, dt_ref, sems):
+    groups = group_count(levels)
+    read_row, read_counts = slot_reader(y1_ref, y2_ref, groups)
+    numbers = level_numbers(groups)
+    zero = jnp.zeros((SUB, LANES), jnp.float32)
+    count = count_ref[...].astype(jnp.float32)
+    count_south, count_north = read_counts()
+    counts = rows_of((count_south, count, count_north), -2, 9)
+    counts_v = counts[1:].minimum(counts[:-1])
+    out = []
     for q in range(groups):
         level = numbers[q]
 
@@ -328,22 +350,25 @@
             return Many(south + load_rows(ref, q, levels).items + north)
 
         t, st, v = rows("t", t_ref, -2, 8), rows("st", st_ref, -2, 9), rows("v", v_ref, -1, 9)
-        from_x, to_u = along_columns(level, counts[2:10], counts_u, load_rows(u_ref, q, levels), t[2:10], st[2:10])
         cell = (st * -ADVECT).where(counts > level, zero)
         flux = (cell[:-1] - cell[1:]).where(counts_v > level, zero)
         back = v * flux
         from_y = ((back[1:9] + back[2:10]) * 7.0 - (back[0:8] + back[3:11])) * (1.0 / 12.0)
         to_v = flux[1:9] * face_values(t[2:10], t[1:9], t[3:11], t[0:8])
-        store_rows(dt_ref, q, levels, st[2:10] + merge_edges(from_x, edge_t, q) + from_y)
-        store_rows(du_ref, q, levels, merge_edges(to_u, edge_u, q))
+        store_rows(dt_ref, q, levels, load_rows(dtx_ref, q, levels) + from_y)
         store_rows(dv_ref, q, levels, to_v)
+        part = pl.ds(q * SUB * SUB, min(SUB, levels - q * SUB) * SUB)
+        out.append(pltpu.make_async_copy(dt_ref.at[part, :], dt_hbm.at[part, :], sems.at[q]))
+        out[-1].start()
+    for copy in out:
+        copy.wait()
 
 
 def total(value):
     return jnp.sum(value, axis=(0, 1), keepdims=True)
 
 
-def surface_solve(levels, ny, nx, read, count_ref, face_ref, x_ref, r_ref, p_ref):
+def surface_solve(levels, ny, nx, read, count_ref, face_ref, x_ref, r_ref, p_ref, beside_work):
     groups = group_count(levels)
     lanes, rows = lane_ids(), row_ids()
     numbers = level_numbers(groups)
@@ -422,8 +447,9 @@
         return carry
 
     loop(faces)
-
-    def start(j, norm):
+    next(beside_work, None)
+
+    def start(j, carry):
         load = Many(read(j + dj, i, CHUNK_LOAD) for dj, i in cells)
         col_u, col_v = get(face_ref.at[4], j), get(face_ref.at[5], j)
         depth_u, depth_v = get(face_ref.at[0], j), get(face_ref.at[1], j)
@@ -437,9 +463,7 @@
         put(face_ref.at[2], j, none.where(at_end, east_of(depth_u)))
         put(face_ref.at[3], j, none.where(at_top, north_of(face_ref.at[1], j, depth_v)))
         put(r_ref, j, load)
-        put(p_ref, j, load)
-        put(x_ref, j, none)
-        return gathered(norm, load * load)
+        return carry
 
     def gathered(partial, values):
         items = list(values.items)
@@ -447,48 +471,47 @@
             items = [a + b for a, b in zip(items[::2], items[1::2])] + items[len(items) // 2 * 2 :]
         return partial + items[0]
 
-    norm = total(loop(start, zero))
+    loop(start)
+
+    def products(j, carry):
+        r = get(r_ref, j)
+        image = r + get(face_ref.at[0], j) * (r - west_of(r)) + get(face_ref.at[2], j) * (r - east_of(r))
+        image = image + get(face_ref.at[1], j) * (r - south_of(r_ref, j, r))
+        image = image + get(face_ref.at[3], j) * (r - north_of(r_ref, j, r))
+        put(face_ref.at[4], j, image)
+        return gathered(carry[0], r * r), gathered(carry[1], r * image)
+
+    norm, product = [total(part) for part in loop(products, (zero, zero))]
+    next(beside_work, None)
+    step, ratio = norm / product, None
 
     for iteration in range(ITERS):
         last = iteration + 1 == ITERS
 
-        def image_of(j):
-            p = get(p_ref, j)
-            image = p + get(face_ref.at[0], j) * (p - west_of(p)) + get(face_ref.at[2], j) * (p - east_of(p))
-            image = image + get(face_ref.at[1], j) * (p - south_of(p_ref, j, p))
-            return p, image + get(face_ref.at[3], j) * (p - north_of(p_ref, j, p))
-
-        def product(j, dot):
-            p, image = image_of(j)
-            put(face_ref.at[4], j, image)
-            return gathered(dot, p * image)
-
-        step = norm / total(loop(product, zero))
-
-        def advance(j, new):
-            put(x_ref, j, get(x_ref, j) + get(p_ref, j) * step)
-            if last:
-                return new
-            residual = get(r_ref, j) - get(face_ref.at[4], j) * step
-            put(r_ref, j, residual)
-            return gathered(new, residual * residual)
-
-        new = loop(advance, zero)
+        def advance(j, carry):
+            r = get(r_ref, j)
+            p = r if ratio is None else r + get(p_ref, j) * ratio
+            put(x_ref, j, p * step if ratio is None else get(x_ref, j) + p * step)
+            if not last:
+                image = get(face_ref.at[4], j)
+                image = image if ratio is None else image + get(face_ref.at[5], j) * ratio
+                put(p_ref, j, p)
+                put(face_ref.at[5], j, image)
+                put(r_ref, j, r - image * step)
+            return carry
+
+        loop(advance)
         if not last:
-            new = total(new)
+            new, product = [total(part) for part in loop(products, (zero, zero))]
+            next(beside_work, None)
             ratio = new / norm
+            step = new / (product - ratio * new / step)
             norm = new
 
-            def turn(j, carry):
-                put(p_ref, j, get(r_ref, j) + get(p_ref, j) * ratio)
-                return carry
-
-            loop(turn)
-
 
 def flow_kernel(
-    levels, ny, nx, u_ref, v_ref, su_ref, sv_ref, ga_ref, gb_ref, y1_ref, y2_ref, x1_ref, x2_ref, dut_ref, dvt_ref,
-    du_ref, dv_ref, eta_ref, count_s, face_s, x_s, r_s, p_s,
+    levels, ny, nx, u_ref, v_ref, su_ref, sv_ref, ga_ref, gb_ref, y1_ref, y2_ref, edge_ref, dut_ref, dvt_ref,
+    du_hbm, dv_hbm, eta_hbm, count_s, face_s, x_s, r_s, p_s, du_ref, dv_ref, sems,
 ):
     groups = group_count(levels)
     lanes = lane_ids()
@@ -498,26 +521,16 @@
     numbers = level_numbers(groups)
     thick = [1.0 + number * (1.0 / levels) for number in numbers]
     read_row, _ = slot_reader(y1_ref, y2_ref, groups)
-    read_sides = side_reader(x1_ref, x2_ref)
     zero = jnp.zeros((SUB, LANES), jnp.float32)
 
     def read(j, i, first):
         where = (j * (nx // 2) + i // 2, pl.ds(first, SUB), slice(None))
         return jnp.where(core == i % 2, ga_ref[where], gb_ref[where])
-
-    surface_solve(levels, ny, nx, read, count_s, face_s, x_s, r_s, p_s)
-    eta_ref[...] = x_s[my_j, my_i]
 
     def near(dj, di, get):
         j, i = jnp.clip(my_j + dj, 0, ny - 1), jnp.clip(my_i + di, 0, nx - 1)
         inside = (my_j + dj >= 0) & (my_j + dj < ny) & (my_i + di >= 0) & (my_i + di < nx)
         return jnp.where(inside, get(j, i), 0.0)
-
-    def around(ref):
-        tiles = [[near(dj, di, lambda j, i: ref[j, i]) for di in (-1, 0, 1)] for dj in (-1, 0, 1)]
-        return [row[1] for row in tiles], [edge_of_tile(*row) for row in tiles]
-
-    count_tiles, x_tiles = around(count_s), around(x_s)
 
     corner_tiles = {
         name: near(dj, di, lambda j, i: read(j, i, CHUNK_EDGE))
@@ -532,55 +545,95 @@
                 edge = jnp.where(lanes == lane, roll_lanes(corner_tiles[which], lane - source), edge)
         return edge
 
-    sides = [read_sides(row) for row in range(SUB)]
-    west, east = Many(side[0] for side in sides), Many(side[1] for side in sides)
-
     def rows(name, ref, q, first, last):
         south = [read_row(name, row, q) for row in range(first, 0)]
         north = [read_row(name, row, q) for row in range(SUB, last + 1)]
         return Many(south + load_rows(ref, q, levels).items + north)
 
-    def edges(name, ref, first, last):
-        out = edges_of_groups([rows(name, ref, q, first, last) for q in range(groups)])
-        south = [insert_corners(out[row - first], name, row) for row in range(first, 0)]
-        north = [insert_corners(out[row - first], name, row) for row in range(SUB, last + 1)]
-        inner = insert_sides(out[-first : SUB - first], west, east, FIELDS.index(name))
-        return Many(south + inner.items + north)
+    def edges(name, first, last):
+        outer = [row for row in range(first, last + 1) if not 0 <= row < SUB]
+        made = edges_of_groups([Many(read_row(name, row, q) for row in outer) for q in range(groups)])
+        made = [insert_corners(edge, name, row) for edge, row in zip(made.items, outer)]
+        n = FLOW_FIELDS.index(name)
+        own = [edge_ref[(n * SUB + row) * SUB : (n * SUB + row + 1) * SUB, :] for row in range(SUB)]
+        return Many(made[:-first] + own + made[-first:])
 
     total_rows = ny * SUB
     first_row = (my_j * SUB).astype(jnp.float32)
     turn_u = Many(0.5 + (first_row + (row + 0.5)) * (1.0 / total_rows) for row in range(-1, 8))
     turn_v = Many(-0.5 - (first_row + row) * (1.0 / total_rows) for row in range(0, 9))
 
-    def adjoint(part, u, v, su, sv):
+    fields = (("u", u_ref, -2, 8), ("v", v_ref, -1, 9), ("su", su_ref, -1, 8), ("sv", sv_ref, -1, 8))
+    data, made = {}, {}
+
+    def prepare(part):
+        if part == groups:
+            data[part] = [data[name] for name in FLOW_FIELDS]
+        else:
+            data[part] = [rows(name, ref, part, first, last) for name, ref, first, last in fields]
+        u, v = data[part][:2]
+        v_pair, u_pair = v[:-1] + v[1:], u[2:10] + u[1:9]
+        made[part] = (
+            (v_pair + v_pair.at(-1)) * 0.25,
+            (u_pair + u_pair.at(1)) * 0.25,
+            (u[:-2] - u[2:]) * 0.5 + turn_u,
+            (v[1:10].at(-1) - v[1:10].at(1)) * 0.5 + turn_v,
+            u[2:10].at(1) - u[2:10].at(-1),
+        )
+
+    def beside_work():
+        for name, ref, first, last in fields:
+            data[name] = edges(name, first, last)
+            yield
+        prepare(groups)
+        yield
+
+    work = beside_work()
+    surface_solve(levels, ny, nx, read, count_s, face_s, x_s, r_s, p_s, work)
+    for _ in work:
+        pass
+    out = [pltpu.make_async_copy(x_s.at[my_j, my_i], eta_hbm, sems.at[0])]
+    out[0].start()
+
+    def around(ref):
+        tiles = [[near(dj, di, lambda j, i: ref[j, i]) for di in (-1, 0, 1)] for dj in (-1, 0, 1)]
+        return [row[1] for row in tiles], [edge_of_tile(*row) for row in tiles]
+
+    count_tiles, x_tiles = around(count_s), around(x_s)
+
+    def adjoint(part):
         kind = 1 if part == groups else 0
         level = numbers[part]
+        u, v, su, sv = data[part]
+        v_bar, u_bar, from_v_bar, from_u_bar, u_across = made[part]
         counts, x = rows_of(count_tiles[kind], -2, 8), rows_of(x_tiles[kind], -2, 8)
         wet_u = counts[1:].minimum(counts[1:].at(-1)) > level
         wet_v = counts[1:].minimum(counts[:-1]) > level
         u_cot = su + ((x[1:] - x[1:].at(-1)) * thick[part]).where(wet_u, zero)
         v_cot = sv + ((x[1:] - x[:-1]) * thick[part]).where(wet_v, zero)
         a, b = (u_cot * ADVECT).where(wet_u, zero), (v_cot * ADVECT).where(wet_v, zero)
-        v_pair = v[:-1] + v[1:]
-        av = a * (v_pair + v_pair.at(-1)) * 0.25
-        u_pair = u[2:10] + u[1:9]
-        bu = b[1:9] * (u_pair + u_pair.at(1)) * 0.25
+        av, bu = a * v_bar, b[1:9] * u_bar
         au, bv = a[1:9] * u[2:10], b * v[:-1]
-        to_v_bar = a[:-1] * ((u[:-2] - u[2:]) * 0.5 + turn_u)
-        to_u_bar = b[1:] * ((v[1:10].at(-1) - v[1:10].at(1)) * 0.5 + turn_v)
+        to_v_bar, to_u_bar = a[:-1] * from_v_bar, b[1:] * from_u_bar
         near_u, near_v = to_u_bar[:-1] + to_u_bar[1:], to_v_bar[1:] + to_v_bar[:-1]
-        twist_u = au.at(1) - au.at(-1) - a[1:9] * (u[2:10].at(1) - u[2:10].at(-1)) + av[2:] - av[:-2]
+        twist_u = au.at(1) - au.at(-1) - a[1:9] * u_across + av[2:] - av[:-2]
         twist_v = bu.at(1) - bu.at(-1) - b[1:9] * (v[2:10] - v[0:8]) + bv[2:] - bv[:-2]
         du = u_cot[1:9] + twist_u * 0.5 + (near_u + near_u.at(-1)) * 0.25
         dv = v_cot[1:9] + twist_v * 0.5 + (near_v + near_v.at(1)) * 0.25
         return du, dv
 
-    fields = (("u", u_ref, -2, 8), ("v", v_ref, -1, 9), ("su", su_ref, -1, 8), ("sv", sv_ref, -1, 8))
-    edge_u, edge_v = adjoint(groups, *(edges(*field) for field in fields))
+    edge_u, edge_v = adjoint(groups)
     for q in range(groups):
-        du, dv = adjoint(q, *(rows(name, ref, q, first, last) for name, ref, first, last in fields))
+        prepare(q)
+        du, dv = adjoint(q)
         store_rows(du_ref, q, levels, merge_edges(du, edge_u, q) + load_rows(dut_ref, q, levels))
         store_rows(dv_ref, q, levels, merge_edges(dv, edge_v, q) + load_rows(dvt_ref, q, levels))
+        part = pl.ds(q * SUB * SUB, min(SUB, levels - q * SUB) * SUB)
+        for target, source in ((du_hbm, du_ref), (dv_hbm, dv_ref)):
+            out.append(pltpu.make_async_copy(source.at[part, :], target.at[part, :], sems.at[len(out)]))
+            out[-1].start()
+    for copy in out:
+        copy.wait()
 
 
 def swaps(mesh_shape, along, parity):
@@ -620,19 +673,25 @@
     column_packet = ((SUB + 1) * SUB, LANES)
     chunk = (peers, CHUNK_ROW + groups * SUB, LANES)
     tile = (SUB, LANES)
-    y1, y2, xp, chunks = call(
-        functools.partial(pack_kernel, levels, peers),
-        [row_packet, row_packet, column_packet, chunk],
-        (u, v, t, su, sv, st, count, elev),
-        scratch=[pltpu.VMEM(flat, jnp.float32)] * 6
-        + [pltpu.VMEM(tile, count.dtype)]
-        + [pltpu.VMEM(shape, jnp.float32) for shape in (tile, row_packet, row_packet, column_packet, chunk[1:])]
-        + [pltpu.SemaphoreType.DMA((9,))],
+    (chunks,) = call(
+        functools.partial(chunk_kernel, levels, peers),
+        [chunk],
+        (u, v, su, sv, count, elev),
+        scratch=[pltpu.VMEM(flat, jnp.float32)] * 4
+        + [pltpu.VMEM(tile, count.dtype), pltpu.VMEM(tile, jnp.float32), pltpu.VMEM(chunk[1:], jnp.float32)]
+        + [pltpu.SemaphoreType.DMA((7,))],
         flops=1 << 20,
         size=1 << 21,
         far_in=True,
-        far_out=(0, 1, 2, 3),
+        far_out=(0,),
         limit=60,
+    )
+    y1, y2, xp = call(
+        functools.partial(packet_kernel, levels),
+        [row_packet, row_packet, column_packet],
+        (u, v, t, su, sv, st, count),
+        flops=1 << 20,
+        size=1 << 21,
     )
     axes = ("ty", "y", "core")
     ga = lax.all_to_all(chunks, ("ty", "y"), 0, 0)
@@ -640,22 +699,33 @@
     x2 = lax.ppermute(xp, axes, swaps(shape, "x", 1))
     y1 = lax.ppermute(y1, axes, swaps(shape, "y", 0))
     y2 = lax.ppermute(y2, axes, swaps(shape, "y", 1))
-    dt, du_t, dv_t = call(
-        functools.partial(tracer_kernel, levels),
-        [flat] * 3,
-        (u, v, t, st, count, y1, y2, x1, x2),
+    dtx, du_t, edge = call(
+        functools.partial(column_kernel, levels),
+        [flat, flat, (len(FLOW_FIELDS) * SUB * SUB, LANES)],
+        (u, v, t, st, su, sv, count, x1, x2),
         flops=1 << 22,
         size=1 << 21,
     )
-    ga, du_t = lax.optimization_barrier((ga, du_t))
+    ga, y1, y2, dtx = lax.optimization_barrier((ga, y1, y2, dtx))
     gb = lax.ppermute(ga, axes, swaps(shape, "x", 0))
+    dt, dv_t = call(
+        functools.partial(row_kernel, levels),
+        [flat, flat],
+        (v, t, st, count, y1, y2, dtx),
+        scratch=(pltpu.VMEM(flat, jnp.float32), pltpu.SemaphoreType.DMA((groups,))),
+        flops=1 << 22,
+        size=1 << 21,
+        far_out=(0,),
+    )
     grid = pltpu.VMEM((ny, nx, SUB, LANES), jnp.float32)
     faces = pltpu.VMEM((6, ny, nx, SUB, LANES), jnp.float32)
     du, dv, eta = call(
         functools.partial(flow_kernel, levels, ny, nx),
         [flat, flat, (SUB, LANES)],
-        (u, v, su, sv, ga, gb, y1, y2, x1, x2, du_t, dv_t),
-        scratch=(grid, faces, grid, grid, grid),
+        (u, v, su, sv, ga, gb, y1, y2, edge, du_t, dv_t),
+        far_out=(0, 1, 2),
+        scratch=(grid, faces, grid, grid, grid, pltpu.VMEM(flat, jnp.float32), pltpu.VMEM(flat, jnp.float32))
+        + (pltpu.SemaphoreType.DMA((2 * groups + 1,)),),
         flops=1 << 23,
         size=1 << 22,
     )

time: 33.4 us -> 31 us (0.928)
  waiting for transfers between devices: 6.71 us -> 4.4 us
    ppermute x1, waiting for transfers between devices: 2.6 us -> 1.24 us  [on_device(): y2 = lax.ppermute(y2, axes, swaps(shape, 'y', 1))]
    ppermute x1, waiting for transfers between devices: 1.44 us -> 0.67 us  [on_device(): gb = lax.ppermute(ga, axes, swaps(shape, 'x', 0))]
    pallas_call x3 -> x5, Pallas kernels: 7.98 us -> 8.06 us  [call(): pl.pallas_call(kernel, out_shape=outs, in_specs=[far if far_in else near]...]
  transfers between devices with their start and end apart: 6 -> 6, of which waited for: 3 -> 3; matrix products, arithmetic and copies ran while one was open for 0% -> 0% of each run, Pallas kernels for 5% -> 8%
where the time goes in v3:
time: 31 us; the launch traced here: 30.7 us
  starting transfers between devices  17.4 us (56%)
  Pallas kernels  8.06 us (26%)
  waiting for transfers between devices  4.4 us (14%)
  between operations  0.8 us (3%)
    pallas_call x5, Pallas kernels, call(): pl.pallas_call(kernel, out_shape=outs, in_specs=[far if far_in else near]...  8.06 us
    all_to_all x1, starting transfers between devices, on_device(): ga = lax.all_to_all(chunks, ('ty', 'y'), 0, 0)  6.78 us
    ppermute x1, starting transfers between devices, on_device(): x2 = lax.ppermute(xp, axes, swaps(shape, 'x', 1))  4.77 us
    ppermute x1, starting transfers between devices, on_device(): y2 = lax.ppermute(y2, axes, swaps(shape, 'y', 1))  3.98 us
    ppermute x1, waiting for transfers between devices, on_device(): x2 = lax.ppermute(xp, axes, swaps(shape, 'x', 1))  2.48 us
    ppermute x1, starting transfers between devices, on_device(): gb = lax.ppermute(ga, axes, swaps(shape, 'x', 0))  1.45 us
    ppermute x1, waiting for transfers between devices, on_device(): y2 = lax.ppermute(y2, axes, swaps(shape, 'y', 1))  1.24 us
    ppermute x1, waiting for transfers between devices, on_device(): gb = lax.ppermute(ga, axes, swaps(shape, 'x', 0))  0.67 us
  transfers between devices with their start and end apart: 6, of which 3 were waited for; matrix products, arithmetic and copies ran while one was open for 0% of the time, Pallas kernels for 8%

profile of v3, /device:TPU:11, one launch (start us, length us, event | category | flops | bytes accessed | tf_op | source)
XLA Modules:
  0.0 30.7 jit_solution(16420283028104780823)
XLA Ops:
  0.6 2.1 %shard_map.111 = f32[16,56,128]{2,1,0:T(8,128)} custom-call(f32[240,128]{1,0:T(8,128)} %bitcast.14, f32[240,128]{1,0:T(8,128)} %bitcast.9, f32[240,128]{1,0:T(8,128)} %bitcast.18, f32[240,128]{1,0:T(8,128)} %bitcast.22, s32[8,128]{1,0:T(8,128)} %count_ref.5, f32[8,128]{1,0:T(8,128)} %elev_hbm.1), custom_call_target="tpu_custom_call" | custom-call | flops 1048576 | bytes 2097152 | tf_op jit(solution)/shard_map/pallas_call | solution.py:654
  2.7 0.0 copy-start
  2.7 0.0 copy-start.1
  2.7 0.0 copy-start.2
  2.8 0.0 copy-start.3
  2.8 0.0 copy-start.4
  2.8 0.0 copy-start.5
  2.8 0.0 copy-start.6
  2.8 6.8 %all-to-all-start = ((f32[16,56,128]{2,1,0:T(8,128)}), f32[16,56,128]{2,1,0:T(8,128)S(1)}, u32[]{:S(2)}, u32[]{:S(2)}) async-start(f32[16,56,128]{2,1,0:T(8,128)} %shard_map.111), calls=%async_computation | async-start | bytes 917504 | tf_op jit(solution)/shard_map/all_to_all | solution.py:697
  9.6 0.0 copy-done
  9.6 0.0 copy-done.1
  9.6 0.0 copy-done.2
  9.6 0.0 copy-done.3
  9.6 0.0 copy-done.4
  9.6 0.0 copy-done.5
  9.6 0.0 copy-done.6
  9.7 0.3 shard_map.112
  10.0 0.3 %collective-permute-start = (f32[296,128]{1,0:T(8,128)S(1)}, f32[296,128]{1,0:T(8,128)S(1)}, u32[]{:S(2)}, u32[]{:S(2)}) collective-permute-start(f32[296,128]{1,0:T(8,128)S(1)} %get-tuple-element.19), channel_id=1, source_target_pairs={{0,4},{1,5},{2,6},{3,7},{4,0},{5,1},{6,2},{7,3},{8,12},{9,13},{10,... | collective-permute-start | bytes 454664 | tf_op jit(solution)/shard_map/ppermute | solution.py:700
  10.3 4.0 %collective-permute-start.1 = (f32[296,128]{1,0:T(8,128)S(1)}, f32[296,128]{1,0:T(8,128)S(1)}, u32[]{:S(2)}, u32[]{:S(2)}) collective-permute-start(f32[296,128]{1,0:T(8,128)S(1)} %get-tuple-element.20), channel_id=1, source_target_pairs={{4,8},{5,9},{6,10},{7,11},{8,4},{9,5},{10,6},{11,7},{12,16},{13,17... | collective-permute-start | bytes 454664 | tf_op jit(solution)/shard_map/ppermute | solution.py:701
  14.3 4.8 %collective-permute-start.3 = (f32[72,128]{1,0:T(8,128)S(1)}, f32[72,128]{1,0:T(8,128)S(1)}, u32[]{:S(2)}, u32[]{:S(2)}) collective-permute-start(f32[72,128]{1,0:T(8,128)S(1)} %get-tuple-element.21), channel_id=1, source_target_pairs={{1,2},{2,1},{5,6},{6,5},{9,10},{10,9},{13,14},{14,13},{17,18},{18,... | collective-permute-start | bytes 110600 | tf_op jit(solution)/shard_map/ppermute | solution.py:699
  19.1 0.1 collective-permute-start.2
  19.1 2.5 %collective-permute-done.3.x2_ref = f32[72,128]{1,0:T(8,128)S(1)} collective-permute-done((f32[72,128]{1,0:T(8,128)S(1)}, f32[72,128]{1,0:T(8,128)S(1)}, u32[]{:S(2)}, u32[]{:S(2)}) %collective-permute-start.3) | collective-permute-done | bytes 36896 | tf_op jit(solution)/shard_map/ppermute | solution.py:699
  21.6 0.0 collective-permute-done.2.x1_ref
  21.6 1.3 %shard_map.113 = (f32[240,128]{1,0:T(8,128)S(1)}, f32[240,128]{1,0:T(8,128)S(1)}, f32[256,128]{1,0:T(8,128)S(1)}) custom-call(f32[240,128]{1,0:T(8,128)S(1)} %bitcast.16, f32[240,128]{1,0:T(8,128)S(1)} %bitcast.11, f32[240,128]{1,0:T(8,128)S(1)} %bitcast.27, f32[240,128]{1,0:T(8,128)S(1)} %bitcast.30, f32[240,128]{1,0:T(8,128)S(1)} %bitcast.20, ...), custom_call_target="tpu_custom_call" | custom-call | flops 4194304 | bytes 2097152 | tf_op jit(solution)/shard_map/pallas_call | solution.py:654
  23.0 0.0 collective-permute-done.y1_ref
  23.0 1.2 %collective-permute-done.1.y2_ref = f32[296,128]{1,0:T(8,128)S(1)} collective-permute-done((f32[296,128]{1,0:T(8,128)S(1)}, f32[296,128]{1,0:T(8,128)S(1)}, u32[]{:S(2)}, u32[]{:S(2)}) %collective-permute-start.1) | collective-permute-done | bytes 151584 | tf_op jit(solution)/shard_map/ppermute | solution.py:701
  24.2 0.0 all-to-all-done.ga_ref
  24.2 1.5 %collective-permute-start.4 = (f32[16,56,128]{2,1,0:T(8,128)S(1)}, f32[16,56,128]{2,1,0:T(8,128)S(1)}, u32[]{:S(2)}, u32[]{:S(2)}) collective-permute-start(f32[16,56,128]{2,1,0:T(8,128)S(1)} %all-to-all-done.ga_ref), channel_id=1, source_target_pairs={{0,1},{1,0},{2,3},{3,2},{4,5},{5,4},{6,7},{7,6},{8,9},{9,8},{10,11... | collective-permute-start | bytes 1376264 | tf_op jit(solution)/shard_map/ppermute | solution.py:710
  25.7 0.8 %shard_map.114 = (f32[240,128]{1,0:T(8,128)}, f32[240,128]{1,0:T(8,128)S(1)}) custom-call(f32[240,128]{1,0:T(8,128)S(1)} %bitcast.12, f32[240,128]{1,0:T(8,128)S(1)} %bitcast.28, f32[240,128]{1,0:T(8,128)S(1)} %bitcast.31, s32[8,128]{1,0:T(8,128)S(1)} %copy-done.6, f32[296,128]{1,0:T(8,128)S(1)} %collective-permute-done.y1_ref, ...), custom_call_target="tpu_custom_call" | custom-call | flops 4194304 | bytes 2097152 | tf_op jit(solution)/shard_map/pallas_call | solution.py:654
  26.5 0.7 %collective-permute-done.4.gb_ref = f32[16,56,128]{2,1,0:T(8,128)S(1)} collective-permute-done((f32[16,56,128]{2,1,0:T(8,128)S(1)}, f32[16,56,128]{2,1,0:T(8,128)S(1)}, u32[]{:S(2)}, u32[]{:S(2)}) %collective-permute-start.4) | collective-permute-done | bytes 458784 | tf_op jit(solution)/shard_map/ppermute | solution.py:710
  27.1 3.6 %shard_map.115 = (f32[240,128]{1,0:T(8,128)}, f32[240,128]{1,0:T(8,128)}, f32[8,128]{1,0:T(8,128)}) custom-call(f32[240,128]{1,0:T(8,128)S(1)} %bitcast.17, f32[240,128]{1,0:T(8,128)S(1)} %bitcast.13, f32[240,128]{1,0:T(8,128)S(1)} %bitcast.21, f32[240,128]{1,0:T(8,128)S(1)} %bitcast.25, f32[16,56,128]{2,1,0:T(8,128)S(1)} %all-to-all-done.ga_ref, ...), custom_call_target="tpu_custom_call" | custom-call | flops 8388608 | bytes 4194304 | tf_op jit(solution)/shard_map/pallas_call | solution.py:654
Async XLA Ops:
  2.7 6.9 %copy-start = (f32[30,8,128]{2,1,0:T(8,128)S(1)}, f32[30,8,128]{2,1,0:T(8,128)}, u32[]{:S(2)}) copy-start(f32[30,8,128]{2,1,0:T(8,128)} %param.9) | copy-start | bytes 368644
  2.7 6.9 %copy-start.1 = (f32[30,8,128]{2,1,0:T(8,128)S(1)}, f32[30,8,128]{2,1,0:T(8,128)}, u32[]{:S(2)}) copy-start(f32[30,8,128]{2,1,0:T(8,128)} %param.8) | copy-start | bytes 368644
  2.7 6.9 %copy-start.2 = (f32[30,8,128]{2,1,0:T(8,128)S(1)}, f32[30,8,128]{2,1,0:T(8,128)}, u32[]{:S(2)}) copy-start(f32[30,8,128]{2,1,0:T(8,128)} %param.12) | copy-start | bytes 368644
  2.8 6.9 %copy-start.3 = (f32[30,8,128]{2,1,0:T(8,128)S(1)}, f32[30,8,128]{2,1,0:T(8,128)}, u32[]{:S(2)}) copy-start(f32[30,8,128]{2,1,0:T(8,128)} %param.13) | copy-start | bytes 368644
  2.8 6.9 %copy-start.4 = (f32[30,8,128]{2,1,0:T(8,128)S(1)}, f32[30,8,128]{2,1,0:T(8,128)}, u32[]{:S(2)}) copy-start(f32[30,8,128]{2,1,0:T(8,128)} %param.10) | copy-start | bytes 368644
  2.8 6.9 %copy-start.5 = (f32[30,8,128]{2,1,0:T(8,128)S(1)}, f32[30,8,128]{2,1,0:T(8,128)}, u32[]{:S(2)}) copy-start(f32[30,8,128]{2,1,0:T(8,128)} %param.14) | copy-start | bytes 368644
  2.8 6.8 %copy-start.6 = (s32[8,128]{1,0:T(8,128)S(1)}, s32[8,128]{1,0:T(8,128)}, u32[]{:S(2)}) copy-start(s32[8,128]{1,0:T(8,128)} %count_ref.5) | copy-start | bytes 12292
  2.8 21.4 %all-to-all-start = ((f32[16,56,128]{2,1,0:T(8,128)}), f32[16,56,128]{2,1,0:T(8,128)S(1)}, u32[]{:S(2)}, u32[]{:S(2)}) async-start(f32[16,56,128]{2,1,0:T(8,128)} %shard_map.111), calls=%async_computation | async-start | bytes 917504 | tf_op jit(solution)/shard_map/all_to_all | solution.py:697
  10.0 13.0 %collective-permute-start = (f32[296,128]{1,0:T(8,128)S(1)}, f32[296,128]{1,0:T(8,128)S(1)}, u32[]{:S(2)}, u32[]{:S(2)}) collective-permute-start(f32[296,128]{1,0:T(8,128)S(1)} %get-tuple-element.19), channel_id=1, source_target_pairs={{0,4},{1,5},{2,6},{3,7},{4,0},{5,1},{6,2},{7,3},{8,12},{9,13},{10,... | collective-permute-start | bytes 454664 | tf_op jit(solution)/shard_map/ppermute | solution.py:700
  10.3 13.9 %collective-permute-start.1 = (f32[296,128]{1,0:T(8,128)S(1)}, f32[296,128]{1,0:T(8,128)S(1)}, u32[]{:S(2)}, u32[]{:S(2)}) collective-permute-start(f32[296,128]{1,0:T(8,128)S(1)} %get-tuple-element.20), channel_id=1, source_target_pairs={{4,8},{5,9},{6,10},{7,11},{8,4},{9,5},{10,6},{11,7},{12,16},{13,17... | collective-permute-start | bytes 454664 | tf_op jit(solution)/shard_map/ppermute | solution.py:701
  14.3 7.3 %collective-permute-start.3 = (f32[72,128]{1,0:T(8,128)S(1)}, f32[72,128]{1,0:T(8,128)S(1)}, u32[]{:S(2)}, u32[]{:S(2)}) collective-permute-start(f32[72,128]{1,0:T(8,128)S(1)} %get-tuple-element.21), channel_id=1, source_target_pairs={{1,2},{2,1},{5,6},{6,5},{9,10},{10,9},{13,14},{14,13},{17,18},{18,... | collective-permute-start | bytes 110600 | tf_op jit(solution)/shard_map/ppermute | solution.py:699
  19.1 2.6 %collective-permute-start.2 = (f32[72,128]{1,0:T(8,128)S(1)}, f32[72,128]{1,0:T(8,128)S(1)}, u32[]{:S(2)}, u32[]{:S(2)}) collective-permute-start(f32[72,128]{1,0:T(8,128)S(1)} %get-tuple-element.21), channel_id=1, source_target_pairs={{0,1},{1,0},{2,3},{3,2},{4,5},{5,4},{6,7},{7,6},{8,9},{9,8},{10,11... | collective-permute-start | bytes 110600 | tf_op jit(solution)/shard_map/ppermute | solution.py:698
  24.2 2.9 %collective-permute-start.4 = (f32[16,56,128]{2,1,0:T(8,128)S(1)}, f32[16,56,128]{2,1,0:T(8,128)S(1)}, u32[]{:S(2)}, u32[]{:S(2)}) collective-permute-start(f32[16,56,128]{2,1,0:T(8,128)S(1)} %all-to-all-done.ga_ref), channel_id=1, source_target_pairs={{0,1},{1,0},{2,3},{3,2},{4,5},{5,4},{6,7},{7,6},{8,9},{9,8},{10,11... | collective-permute-start | bytes 1376264 | tf_op jit(solution)/shard_map/ppermute | solution.py:710

commit v4 on v3

--- a/solution.py
+++ b/solution.py
@@ -15,7 +15,12 @@
 LANES = 128
 SEG = 32
 FIELDS = ("u", "v", "t", "st", "su", "sv")
+BAND_BLOCKS = 32
 FLOW_FIELDS = ("u", "v", "su", "sv")
+FLOW_ROWS = {"u": (-2, 8), "v": (-1, 9), "su": (-1, 8), "sv": (-1, 8)}
+OUTER_ROWS = tuple((n, r) for n in FLOW_FIELDS for r in range(FLOW_ROWS[n][0], FLOW_ROWS[n][1] + 1) if not 0 <= r < 8)
+MADE_SIZES = (10, 8, 9, 9, 8, 8)
+MADE_ROWS = sum(MADE_SIZES)
 SOUTH_SLOTS = {("u", -2): 0, ("u", -1): 1, ("v", -1): 2, ("t", -2): 3, ("t", -1): 4, ("st", -2): 5, ("st", -1): 6}
 SOUTH_SLOTS.update({("su", -1): 7, ("sv", -1): 8})
 NORTH_SLOTS = {("u", 8): 0, ("v", 8): 1, ("v", 9): 2, ("t", 8): 3, ("st", 8): 5, ("st", 9): 6, ("su", 8): 7, ("sv", 8): 8}
@@ -23,8 +28,7 @@
 CHUNK_LOAD = SUB
 CHUNK_EDGE = 2 * SUB
 CHUNK_ROW = 3 * SUB
-CORNER_LANE = 32
-CORNER_STEP = 24
+EDGE_LEVELS = 20
 CORNERS = (("u", 6, 0), ("u", 7, 0), ("u", 7, 1), ("su", 7, 0), ("v", 7, 127), ("u", 7, 127))
 CORNERS += (("v", 0, 127), ("v", 1, 127), ("v", 0, 126), ("sv", 0, 127), ("v", 0, 0), ("u", 0, 0))
 CORNER_PLACES = {
@@ -96,8 +100,8 @@
 
 
 def chunk_kernel(
-    levels, peers, u_hbm, v_hbm, su_hbm, sv_hbm, count_hbm, elev_hbm, chunk_hbm,
-    u_ref, v_ref, su_ref, sv_ref, count_ref, elev_ref, chunk_ref, sems,
+    levels, peers, u_hbm, v_hbm, su_hbm, sv_hbm, count_hbm, elev_hbm, chunk_ref,
+    u_ref, v_ref, su_ref, sv_ref, count_ref, elev_ref, sems,
 ):
     pairs = (
         (count_hbm, count_ref), (su_hbm, su_ref), (sv_hbm, sv_ref), (elev_hbm, elev_ref), (u_hbm, u_ref), (v_hbm, v_ref),
@@ -120,7 +124,8 @@
         su_level = su_ref[k * SUB : (k + 1) * SUB, :]
         col_u[k % 4] = col_u[k % 4] + jnp.where(wet_u > float(k), su_level, 0.0)
         col_v[k % 4] = col_v[k % 4] + jnp.where(wet_v > float(k), sv_ref[k * SUB : (k + 1) * SUB, :], 0.0)
-        edge = jnp.where(lanes == k, roll_lanes(su_level, k), edge)
+        lane = SEG * (k // EDGE_LEVELS) + k % EDGE_LEVELS
+        edge = jnp.where(lanes == lane, roll_lanes(su_level, lane), edge)
     col_u, col_v = ((col[0] + col[1]) + (col[2] + col[3]) for col in (col_u, col_v))
     load = elev_ref[...] + GRAVITY_DT * (at(col_u, 1) - col_u + roll_rows(col_v, -1) - col_v)
 
@@ -128,21 +133,20 @@
         copy.wait()
     for place, (name, row, column) in enumerate(CORNERS):
         for q in range(groups):
-            lane = CORNER_LANE + CORNER_STEP * q + place
+            lane = SEG * q + EDGE_LEVELS + place
             edge = jnp.where(lanes == lane, roll_lanes(load_group(refs[name], row, q, levels), lane - column), edge)
 
-    chunk_ref[0:SUB, :] = count
-    chunk_ref[CHUNK_LOAD : CHUNK_LOAD + SUB, :] = load
-    chunk_ref[CHUNK_EDGE : CHUNK_EDGE + SUB, :] = edge
-    for q in range(groups):
-        chunk_ref[CHUNK_ROW + q * SUB : CHUNK_ROW + (q + 1) * SUB, :] = load_group(sv_ref, 0, q, levels)
+    south_row = [load_group(sv_ref, 0, q, levels) for q in range(groups)]
 
     def put(peer, carry):
-        pltpu.make_async_copy(chunk_ref, chunk_hbm.at[peer], sems.at[len(pairs)]).start()
+        chunk_ref[peer, 0:SUB, :] = count
+        chunk_ref[peer, CHUNK_LOAD : CHUNK_LOAD + SUB, :] = load
+        chunk_ref[peer, CHUNK_EDGE : CHUNK_EDGE + SUB, :] = edge
+        for q in range(groups):
+            chunk_ref[peer, CHUNK_ROW + q * SUB : CHUNK_ROW + (q + 1) * SUB, :] = south_row[q]
         return carry
 
-    lax.fori_loop(0, peers, put, 0, unroll=peers <= 32)
-    pltpu.make_async_copy(chunk_hbm, chunk_hbm, sems.at[len(pairs)]).wait()
+    lax.fori_loop(0, peers, put, 0, unroll=4)
 
 
 def packet_kernel(levels, u_ref, v_ref, t_ref, su_ref, sv_ref, st_ref, count_ref, y1_ref, y2_ref, x_ref):
@@ -234,10 +238,13 @@
     return east.rolled(22 - 4 * field).where((place == 24) | (place == 25), edge)
 
 
-def merge_edges(values, edge, q):
+def outer_columns(edge):
+    return edge.rolled(-16).where((lane_ids() & (SEG - 1)) < 8, edge)
+
+
+def merge_edges(values, outer, q):
     lanes = lane_ids()
-    values = edge.rolled(-(SEG * q + 8)).where(lanes < 2, values)
-    return edge.rolled(104 - SEG * q).where(lanes >= LANES - 2, values)
+    return outer.rolled(-(SEG * q + 8)).where((lanes < 2) | (lanes >= LANES - 2), values)
 
 
 def load_rows(ref, q, levels):
@@ -316,7 +323,7 @@
     u, t, st = (
         edge_rows(ref, west, east, levels, groups, name) for name, ref in (("u", u_ref), ("t", t_ref), ("st", st_ref))
     )
-    edge_t, edge_u = along(numbers[groups], *counts(count_edge), u, t, st)
+    edge_t, edge_u = (outer_columns(part) for part in along(numbers[groups], *counts(count_edge), u, t, st))
     own = counts(count)
     for q in range(groups):
         st = load_rows(st_ref, q, levels)
@@ -331,7 +338,28 @@
             edge_ref[(n * SUB + row) * SUB : (n * SUB + row + 1) * SUB, :] = rows[row]
 
 
-def row_kernel(levels, v_ref, t_ref, st_ref, count_ref, y1_ref, y2_ref, dtx_ref, dt_hbm, dv_ref, dt_ref, sems):
+def turns(ny):
+    first_row = (lax.axis_index("ty") * SUB).astype(jnp.float32)
+    scale = 0.5 / (ny * SUB)
+    turn_u = Many(0.25 + (first_row + (row + 0.5)) * scale for row in range(-1, 8))
+    return turn_u, Many(-0.25 - (first_row + row) * scale for row in range(0, 9))
+
+
+def prepared(u, v, turn_u, turn_v):
+    v_pair, u_pair = v[:-1] + v[1:], u[2:10] + u[1:9]
+    return (
+        (v_pair + v_pair.at(-1)) * 0.25,
+        (u_pair + u_pair.at(1)) * 0.25,
+        (u[:-2] - u[2:]) * 0.25 + turn_u,
+        (v[1:10].at(-1) - v[1:10].at(1)) * 0.25 + turn_v,
+        u[2:10].at(1) - u[2:10].at(-1),
+        v[2:10] - v[0:8],
+    )
+
+
+def row_kernel(
+    levels, ny, u_ref, v_ref, t_ref, st_ref, count_ref, y1_ref, y2_ref, dtx_ref, dt_hbm, dv_ref, made_ref, edge_ref, dt_ref, sems
+):
     groups = group_count(levels)
     read_row, read_counts = slot_reader(y1_ref, y2_ref, groups)
     numbers = level_numbers(groups)
@@ -341,6 +369,9 @@
     counts = rows_of((count_south, count, count_north), -2, 9)
     counts_v = counts[1:].minimum(counts[:-1])
     out = []
+    for n, (name, row) in enumerate(OUTER_ROWS):
+        (edge,) = edges_of_groups([Many([read_row(name, row, q)]) for q in range(groups)]).items
+        edge_ref[n * SUB : (n + 1) * SUB, :] = edge
     for q in range(groups):
         level = numbers[q]
 
@@ -350,6 +381,10 @@
             return Many(south + load_rows(ref, q, levels).items + north)
 
         t, st, v = rows("t", t_ref, -2, 8), rows("st", st_ref, -2, 9), rows("v", v_ref, -1, 9)
+        made = prepared(rows("u", u_ref, -2, 8), v, *turns(ny))
+        for n, value in enumerate(value for values in made for value in values.items):
+            place = pl.ds((q * MADE_ROWS + n) * SUB, SUB)
+            made_ref[place, :] = value
         cell = (st * -ADVECT).where(counts > level, zero)
         flux = (cell[:-1] - cell[1:]).where(counts_v > level, zero)
         back = v * flux
@@ -368,19 +403,21 @@
     return jnp.sum(value, axis=(0, 1), keepdims=True)
 
 
-def surface_solve(levels, ny, nx, read, count_ref, face_ref, x_ref, r_ref, p_ref, beside_work):
+def surface_solve(levels, ny, nx, read, count_ref, face_ref, r_refs, beside_setup, beside_sum):
     groups = group_count(levels)
     lanes, rows = lane_ids(), row_ids()
     numbers = level_numbers(groups)
     zero = jnp.zeros((SUB, LANES), jnp.float32)
-    band = max(1, min(ny, 32 // nx))
+    band = max(1, min(ny, BAND_BLOCKS // nx))
     while ny % band:
         band -= 1
     cells = [(dj, i) for dj in range(band) for i in range(nx)]
 
     def loop(body, init=0):
-        if band == ny:
-            return body(0, init)
+        if ny * nx <= 32:
+            for j in range(0, ny, band):
+                init = body(j, init)
+            return init
         return lax.fori_loop(0, ny // band, lambda step, carry: body(step * band, carry), init)
 
     def get(ref, j):
@@ -394,11 +431,12 @@
         return Many(values[dj * nx + min(max(i + step, 0), nx - 1)] for dj, i in cells)
 
     def below(ref, j, values):
-        outside = [ref[jnp.maximum(j - 1, 0), i] for i in range(nx)] if band < ny else values.items[:nx]
+        outside = [ref[max(j - 1, 0) if isinstance(j, int) else jnp.maximum(j - 1, 0), i] for i in range(nx)]
         return Many(outside + values.items[:-nx])
 
     def above(ref, j, values):
-        outside = [ref[jnp.minimum(j + band, ny - 1), i] for i in range(nx)] if band < ny else values.items[-nx:]
+        top = min(j + band, ny - 1) if isinstance(j, int) else jnp.minimum(j + band, ny - 1)
+        outside = [ref[top, i] for i in range(nx)]
         return Many(values.items[nx:] + outside)
 
     def west_of(values):
@@ -414,7 +452,7 @@
         return above(ref, j, values).where(rows == 0, values).apply(lambda a: roll_rows(a, -1))
 
     def depth(wet):
-        return wet.apply(lambda m: GRAVITY_DT * (m + m * (m - 1.0) * (0.5 / levels)))
+        return wet.apply(lambda m: m * (m * (GRAVITY_DT * 0.5 / levels) + GRAVITY_DT * (1.0 - 0.5 / levels)))
 
     def gather(j, carry):
         put(count_ref, j, Many(read(j + dj, i, 0) for dj, i in cells))
@@ -433,7 +471,9 @@
         put(face_ref.at[1], j, depth(wet_v))
         edge = Many(read(j + dj, i, CHUNK_EDGE) for dj, i in cells)
         wet_west = wet_u.apply(lambda a: jnp.broadcast_to(a[:, 0:1], (SUB, LANES)))
-        reach = jnp.where(lanes < levels, lanes.astype(jnp.float32), float(levels))
+        place = lanes & (SEG - 1)
+        number = (lanes >> 5) * EDGE_LEVELS + place
+        reach = jnp.where((place < EDGE_LEVELS) & (number < levels), number.astype(jnp.float32), float(levels))
         inside = edge.where(wet_west > reach, zero)
         col_u = inside.apply(lambda a: jnp.broadcast_to(jnp.sum(a, axis=1, keepdims=True), (SUB, LANES)))
         put(face_ref.at[4], j, col_u * GRAVITY_DT)
@@ -447,7 +487,7 @@
         return carry
 
     loop(faces)
-    next(beside_work, None)
+    beside_setup()
 
     def start(j, carry):
         load = Many(read(j + dj, i, CHUNK_LOAD) for dj, i in cells)
@@ -460,9 +500,12 @@
         none = Many([zero] * len(cells))
         load = load - col_u.where(lanes == 0, zero) - col_v.where(rows == 0, zero)
         load = load + beside(col_u, 1).where(last_column, none) + above(face_ref.at[5], j, col_v).where(last_row, none)
-        put(face_ref.at[2], j, none.where(at_end, east_of(depth_u)))
-        put(face_ref.at[3], j, none.where(at_top, north_of(face_ref.at[1], j, depth_v)))
-        put(r_ref, j, load)
+        depth_east = none.where(at_end, east_of(depth_u))
+        depth_north = none.where(at_top, north_of(face_ref.at[1], j, depth_v))
+        put(face_ref.at[2], j, depth_east)
+        put(face_ref.at[3], j, depth_north)
+        put(face_ref.at[6], j, (depth_u + depth_east) + (depth_v + depth_north) + 1.0)
+        put(r_refs.at[0], j, load)
         return carry
 
     def gathered(partial, values):
@@ -473,48 +516,57 @@
 
     loop(start)
 
-    def products(j, carry):
-        r = get(r_ref, j)
-        image = r + get(face_ref.at[0], j) * (r - west_of(r)) + get(face_ref.at[2], j) * (r - east_of(r))
-        image = image + get(face_ref.at[1], j) * (r - south_of(r_ref, j, r))
-        image = image + get(face_ref.at[3], j) * (r - north_of(r_ref, j, r))
-        put(face_ref.at[4], j, image)
-        return gathered(carry[0], r * r), gathered(carry[1], r * image)
-
-    norm, product = [total(part) for part in loop(products, (zero, zero))]
-    next(beside_work, None)
-    step, ratio = norm / product, None
-
-    for iteration in range(ITERS):
-        last = iteration + 1 == ITERS
+    def products(k):
+        r_ref = r_refs.at[k]
+
+        def body(j, carry):
+            r = get(r_ref, j)
+            image = r * get(face_ref.at[6], j) - get(face_ref.at[0], j) * west_of(r) - get(face_ref.at[2], j) * east_of(r)
+            image = image - get(face_ref.at[1], j) * south_of(r_ref, j, r)
+            image = image - get(face_ref.at[3], j) * north_of(r_ref, j, r)
+            put(face_ref.at[4], j, image)
+            return gathered(carry[0], r * r), gathered(carry[1], r * image)
+
+        return [total(part) for part in loop(body, (zero, zero))]
+
+    norm, product = products(0)
+    beside_sum(0)
+    step = norm / product
+    steps, ratios = [step], []
+
+    for k in range(ITERS - 1):
 
         def advance(j, carry):
-            r = get(r_ref, j)
-            p = r if ratio is None else r + get(p_ref, j) * ratio
-            put(x_ref, j, p * step if ratio is None else get(x_ref, j) + p * step)
-            if not last:
-                image = get(face_ref.at[4], j)
-                image = image if ratio is None else image + get(face_ref.at[5], j) * ratio
-                put(p_ref, j, p)
+            image = get(face_ref.at[4], j)
+            if k > 0:
+                image = image + get(face_ref.at[5], j) * ratio
+            if k + 2 < ITERS:
                 put(face_ref.at[5], j, image)
-                put(r_ref, j, r - image * step)
+            put(r_refs.at[k + 1], j, get(r_refs.at[k], j) - image * step)
             return carry
 
         loop(advance)
-        if not last:
-            new, product = [total(part) for part in loop(products, (zero, zero))]
-            next(beside_work, None)
-            ratio = new / norm
-            step = new / (product - ratio * new / step)
-            norm = new
+        new, product = products(k + 1)
+        beside_sum(k + 1)
+        ratio = new / norm
+        step = new / (product - ratio * new / step)
+        norm = new
+        steps.append(step)
+        ratios.append(ratio)
+
+    weights = [steps[-1]]
+    for k in reversed(range(ITERS - 1)):
+        weights.append(steps[k] + ratios[k] * weights[-1])
+    weights.reverse()
+    return weights
 
 
 def flow_kernel(
-    levels, ny, nx, u_ref, v_ref, su_ref, sv_ref, ga_ref, gb_ref, y1_ref, y2_ref, edge_ref, dut_ref, dvt_ref,
-    du_hbm, dv_hbm, eta_hbm, count_s, face_s, x_s, r_s, p_s, du_ref, dv_ref, sems,
+    levels, ny, nx, u_ref, v_ref, su_ref, sv_ref, ga_ref, gb_ref, y1_ref, y2_ref, edge_ref, outer_ref, made_ref, dut_ref, dvt_ref,
+    du_hbm, dv_hbm, eta_hbm, count_s, face_s, r_s, eta_ref, du_ref, dv_ref, sems,
 ):
     groups = group_count(levels)
-    lanes = lane_ids()
+    lanes, rows_id = lane_ids(), row_ids()
     core = lax.axis_index("core")
     my_j = lax.axis_index("ty")
     my_i = lax.axis_index("y") * 2 + core
@@ -527,6 +579,9 @@
         where = (j * (nx // 2) + i // 2, pl.ds(first, SUB), slice(None))
         return jnp.where(core == i % 2, ga_ref[where], gb_ref[where])
 
+    def block(dj, di, get):
+        return get(jnp.clip(my_j + dj, 0, ny - 1), jnp.clip(my_i + di, 0, nx - 1))
+
     def near(dj, di, get):
         j, i = jnp.clip(my_j + dj, 0, ny - 1), jnp.clip(my_i + di, 0, nx - 1)
         inside = (my_j + dj >= 0) & (my_j + dj < ny) & (my_i + di >= 0) & (my_i + di < nx)
@@ -539,10 +594,8 @@
 
     def insert_corners(edge, name, row):
         for which, value, target in CORNER_PLACES.get((name, row), ()):
-            for q in range(groups):
-                lane = SEG * q + target
-                source = CORNER_LANE + CORNER_STEP * q + value
-                edge = jnp.where(lanes == lane, roll_lanes(corner_tiles[which], lane - source), edge)
+            there = (lanes & (SEG - 1)) == target
+            edge = jnp.where(there, roll_lanes(corner_tiles[which], target - EDGE_LEVELS - value), edge)
         return edge
 
     def rows(name, ref, q, first, last):
@@ -550,79 +603,90 @@
         north = [read_row(name, row, q) for row in range(SUB, last + 1)]
         return Many(south + load_rows(ref, q, levels).items + north)
 
-    def edges(name, first, last):
-        outer = [row for row in range(first, last + 1) if not 0 <= row < SUB]
-        made = edges_of_groups([Many(read_row(name, row, q) for row in outer) for q in range(groups)])
-        made = [insert_corners(edge, name, row) for edge, row in zip(made.items, outer)]
+    def edges(name):
+        first, last = FLOW_ROWS[name]
         n = FLOW_FIELDS.index(name)
-        own = [edge_ref[(n * SUB + row) * SUB : (n * SUB + row + 1) * SUB, :] for row in range(SUB)]
-        return Many(made[:-first] + own + made[-first:])
-
-    total_rows = ny * SUB
-    first_row = (my_j * SUB).astype(jnp.float32)
-    turn_u = Many(0.5 + (first_row + (row + 0.5)) * (1.0 / total_rows) for row in range(-1, 8))
-    turn_v = Many(-0.5 - (first_row + row) * (1.0 / total_rows) for row in range(0, 9))
-
-    fields = (("u", u_ref, -2, 8), ("v", v_ref, -1, 9), ("su", su_ref, -1, 8), ("sv", sv_ref, -1, 8))
+
+        def register(row):
+            if 0 <= row < SUB:
+                return edge_ref[(n * SUB + row) * SUB : (n * SUB + row + 1) * SUB, :]
+            place = OUTER_ROWS.index((name, row)) * SUB
+            return insert_corners(outer_ref[place : place + SUB, :], name, row)
+
+        return Many(register(row) for row in range(first, last + 1))
+
+    refs = {"u": u_ref, "v": v_ref, "su": su_ref, "sv": sv_ref}
     data, made = {}, {}
 
     def prepare(part):
         if part == groups:
-            data[part] = [data[name] for name in FLOW_FIELDS]
-        else:
-            data[part] = [rows(name, ref, part, first, last) for name, ref, first, last in fields]
-        u, v = data[part][:2]
-        v_pair, u_pair = v[:-1] + v[1:], u[2:10] + u[1:9]
-        made[part] = (
-            (v_pair + v_pair.at(-1)) * 0.25,
-            (u_pair + u_pair.at(1)) * 0.25,
-            (u[:-2] - u[2:]) * 0.5 + turn_u,
-            (v[1:10].at(-1) - v[1:10].at(1)) * 0.5 + turn_v,
-            u[2:10].at(1) - u[2:10].at(-1),
-        )
-
-    def beside_work():
-        for name, ref, first, last in fields:
-            data[name] = edges(name, first, last)
-            yield
+            data[part] = [edges(name) for name in FLOW_FIELDS]
+            made[part] = prepared(*data[part][:2], *turns(ny))
+            return
+        data[part] = [rows(name, refs[name], part, *FLOW_ROWS[name]) for name in FLOW_FIELDS]
+        made[part], n = [], part * MADE_ROWS
+        for size in MADE_SIZES:
+            made[part].append(Many(made_ref[k * SUB : (k + 1) * SUB, :] for k in range(n, n + size)))
+            n += size
+
+    def pairs(get, operation):
+        tiles = [[get(dj, di) for di in (-1, 0, 1)] for dj in (-1, 0, 1)]
+        out = []
+        for south, own, north in ([row[1] for row in tiles], [edge_of_tile(*row) for row in tiles]):
+            outer = jnp.where(rows_id == SUB - 1, south, north)
+            below = roll_rows(jnp.where(rows_id == SUB - 1, south, own), 1)
+            below_outer = roll_rows(jnp.where(rows_id == SUB - 2, south, own), 1)
+            out.append(
+                (operation(own, at(own, -1)), operation(outer, at(outer, -1)), operation(own, below), operation(outer, below_outer))
+            )
+        return out
+
+    def outer_and_own(own, outer):
+        return Many([row_of(outer, SUB - 1)] + [row_of(own, row) for row in range(SUB)] + [row_of(outer, 0)])
+
+    wet_counts, differences = [], []
+
+    def beside_setup():
+        wet_counts.extend(pairs(lambda dj, di: near(dj, di, lambda j, i: count_s[j, i]), jnp.minimum))
         prepare(groups)
-        yield
-
-    work = beside_work()
-    surface_solve(levels, ny, nx, read, count_s, face_s, x_s, r_s, p_s, work)
-    for _ in work:
-        pass
-    out = [pltpu.make_async_copy(x_s.at[my_j, my_i], eta_hbm, sems.at[0])]
+
+    def beside_sum(k):
+        differences.append(pairs(lambda dj, di: block(dj, di, lambda j, i: r_s[k, j, i]), lambda a, b: a - b))
+
+    weights = surface_solve(levels, ny, nx, read, count_s, face_s, r_s, beside_setup, beside_sum)
+
+    def weighted(parts):
+        total_of = parts[0] * weights[0]
+        for part, weight in zip(parts[1:], weights[1:]):
+            total_of = total_of + part * weight
+        return total_of
+
+    slopes = [[weighted([d[kind][n] for d in differences]) for n in range(4)] for kind in range(2)]
+    eta_ref[...] = weighted([r_s[k, my_j, my_i] for k in range(ITERS)])
+    out = [pltpu.make_async_copy(eta_ref, eta_hbm, sems.at[0])]
     out[0].start()
-
-    def around(ref):
-        tiles = [[near(dj, di, lambda j, i: ref[j, i]) for di in (-1, 0, 1)] for dj in (-1, 0, 1)]
-        return [row[1] for row in tiles], [edge_of_tile(*row) for row in tiles]
-
-    count_tiles, x_tiles = around(count_s), around(x_s)
 
     def adjoint(part):
         kind = 1 if part == groups else 0
         level = numbers[part]
         u, v, su, sv = data[part]
-        v_bar, u_bar, from_v_bar, from_u_bar, u_across = made[part]
-        counts, x = rows_of(count_tiles[kind], -2, 8), rows_of(x_tiles[kind], -2, 8)
-        wet_u = counts[1:].minimum(counts[1:].at(-1)) > level
-        wet_v = counts[1:].minimum(counts[:-1]) > level
-        u_cot = su + ((x[1:] - x[1:].at(-1)) * thick[part]).where(wet_u, zero)
-        v_cot = sv + ((x[1:] - x[:-1]) * thick[part]).where(wet_v, zero)
-        a, b = (u_cot * ADVECT).where(wet_u, zero), (v_cot * ADVECT).where(wet_v, zero)
+        v_bar, u_bar, from_v_bar, from_u_bar, u_across, v_across = made[part]
+        wet_u = outer_and_own(*wet_counts[kind][:2]) > level
+        wet_v = outer_and_own(*wet_counts[kind][2:]) > level
+        u_cot = su + (outer_and_own(*slopes[kind][:2]) * thick[part]).where(wet_u, zero)
+        v_cot = sv + (outer_and_own(*slopes[kind][2:]) * thick[part]).where(wet_v, zero)
+        a, b = (u_cot * (0.5 * ADVECT)).where(wet_u, zero), (v_cot * (0.5 * ADVECT)).where(wet_v, zero)
         av, bu = a * v_bar, b[1:9] * u_bar
         au, bv = a[1:9] * u[2:10], b * v[:-1]
         to_v_bar, to_u_bar = a[:-1] * from_v_bar, b[1:] * from_u_bar
         near_u, near_v = to_u_bar[:-1] + to_u_bar[1:], to_v_bar[1:] + to_v_bar[:-1]
-        twist_u = au.at(1) - au.at(-1) - a[1:9] * u_across + av[2:] - av[:-2]
-        twist_v = bu.at(1) - bu.at(-1) - b[1:9] * (v[2:10] - v[0:8]) + bv[2:] - bv[:-2]
-        du = u_cot[1:9] + twist_u * 0.5 + (near_u + near_u.at(-1)) * 0.25
-        dv = v_cot[1:9] + twist_v * 0.5 + (near_v + near_v.at(1)) * 0.25
+        du = u_cot[1:9] - a[1:9] * u_across + av[2:] - av[:-2] + near_u
+        du = du + au.at(1) + (near_u - au).at(-1)
+        dv = v_cot[1:9] - b[1:9] * v_across + bv[2:] - bv[:-2] + near_v
+        dv = dv + (near_v + bu).at(1) - bu.at(-1)
         return du, dv
 
-    edge_u, edge_v = adjoint(groups)
+    edge_u, edge_v = (outer_columns(part) for part in adjoint(groups))
     for q in range(groups):
         prepare(q)
         du, dv = adjoint(q)
@@ -678,12 +742,10 @@
         [chunk],
         (u, v, su, sv, count, elev),
         scratch=[pltpu.VMEM(flat, jnp.float32)] * 4
-        + [pltpu.VMEM(tile, count.dtype), pltpu.VMEM(tile, jnp.float32), pltpu.VMEM(chunk[1:], jnp.float32)]
-        + [pltpu.SemaphoreType.DMA((7,))],
+        + [pltpu.VMEM(tile, count.dtype), pltpu.VMEM(tile, jnp.float32), pltpu.SemaphoreType.DMA((6,))],
         flops=1 << 20,
         size=1 << 21,
         far_in=True,
-        far_out=(0,),
         limit=60,
     )
     y1, y2, xp = call(
@@ -708,23 +770,24 @@
     )
     ga, y1, y2, dtx = lax.optimization_barrier((ga, y1, y2, dtx))
     gb = lax.ppermute(ga, axes, swaps(shape, "x", 0))
-    dt, dv_t = call(
-        functools.partial(row_kernel, levels),
-        [flat, flat],
-        (v, t, st, count, y1, y2, dtx),
+    dt, dv_t, made, outer = call(
+        functools.partial(row_kernel, levels, ny),
+        [flat, flat, (groups * MADE_ROWS * SUB, LANES), (len(OUTER_ROWS) * SUB, LANES)],
+        (u, v, t, st, count, y1, y2, dtx),
         scratch=(pltpu.VMEM(flat, jnp.float32), pltpu.SemaphoreType.DMA((groups,))),
         flops=1 << 22,
         size=1 << 21,
         far_out=(0,),
     )
     grid = pltpu.VMEM((ny, nx, SUB, LANES), jnp.float32)
-    faces = pltpu.VMEM((6, ny, nx, SUB, LANES), jnp.float32)
+    faces, residuals = (pltpu.VMEM((n, ny, nx, SUB, LANES), jnp.float32) for n in (7, ITERS))
     du, dv, eta = call(
         functools.partial(flow_kernel, levels, ny, nx),
         [flat, flat, (SUB, LANES)],
-        (u, v, su, sv, ga, gb, y1, y2, edge, du_t, dv_t),
+        (u, v, su, sv, ga, gb, y1, y2, edge, outer, made, du_t, dv_t),
         far_out=(0, 1, 2),
-        scratch=(grid, faces, grid, grid, grid, pltpu.VMEM(flat, jnp.float32), pltpu.VMEM(flat, jnp.float32))
+        scratch=(grid, faces, residuals)
+        + tuple(pltpu.VMEM(shape, jnp.float32) for shape in (tile, flat, flat))
         + (pltpu.SemaphoreType.DMA((2 * groups + 1,)),),
         flops=1 << 23,
         size=1 << 22,

time: 31 us -> 30.5 us (0.984)
  transfers between devices with their start and end apart: 6 -> 6, of which waited for: 3 -> 3; matrix products, arithmetic and copies ran while one was open for 0% -> 0% of each run, Pallas kernels for 8% -> 9%
where the time goes in v4:
time: 30.5 us; the launch traced here: 30.3 us
  starting transfers between devices  17.4 us (57%)
  Pallas kernels  7.82 us (26%)
  waiting for transfers between devices  4.2 us (14%)
  between operations  0.8 us (3%)
    pallas_call x5, Pallas kernels, call(): pl.pallas_call(kernel, out_shape=outs, in_specs=[far if far_in else near]...  7.82 us
    all_to_all x1, starting transfers between devices, on_device(): ga = lax.all_to_all(chunks, ('ty', 'y'), 0, 0)  6.78 us
    ppermute x1, starting transfers between devices, on_device(): x2 = lax.ppermute(xp, axes, swaps(shape, 'x', 1))  4.77 us
    ppermute x1, starting transfers between devices, on_device(): y2 = lax.ppermute(y2, axes, swaps(shape, 'y', 1))  3.98 us
    ppermute x1, waiting for transfers between devices, on_device(): x2 = lax.ppermute(xp, axes, swaps(shape, 'x', 1))  2.48 us
    ppermute x1, starting transfers between devices, on_device(): gb = lax.ppermute(ga, axes, swaps(shape, 'x', 0))  1.45 us
    ppermute x1, waiting for transfers between devices, on_device(): y2 = lax.ppermute(y2, axes, swaps(shape, 'y', 1))  1.29 us
  transfers between devices with their start and end apart: 6, of which 3 were waited for; matrix products, arithmetic and copies ran while one was open for 0% of the time, Pallas kernels for 9%

profile of v4, /device:TPU:11, one launch (start us, length us, event | category | flops | bytes accessed | tf_op | source)
XLA Modules:
  0.0 30.3 jit_solution(6473005481238061742)
XLA Ops:
  0.6 2.1 %shard_map.111 = f32[16,56,128]{2,1,0:T(8,128)} custom-call(f32[240,128]{1,0:T(8,128)} %bitcast.9, f32[240,128]{1,0:T(8,128)} %bitcast.14, f32[240,128]{1,0:T(8,128)} %bitcast.19, f32[240,128]{1,0:T(8,128)} %bitcast.23, s32[8,128]{1,0:T(8,128)} %count_ref.5, f32[8,128]{1,0:T(8,128)} %elev_hbm.1), custom_call_target="tpu_custom_call" | custom-call | flops 1048576 | bytes 2097152 | tf_op jit(solution)/shard_map/pallas_call | solution.py:718
  2.7 0.0 copy-start
  2.8 0.0 copy-start.1
  2.8 0.0 copy-start.2
  2.8 0.0 copy-start.3
  2.8 0.0 copy-start.4
  2.8 0.0 copy-start.5
  2.8 0.0 copy-start.6
  2.8 6.8 %all-to-all-start = ((f32[16,56,128]{2,1,0:T(8,128)}), f32[16,56,128]{2,1,0:T(8,128)S(1)}, u32[]{:S(2)}, u32[]{:S(2)}) async-start(f32[16,56,128]{2,1,0:T(8,128)} %shard_map.111), calls=%async_computation | async-start | bytes 917504 | tf_op jit(solution)/shard_map/all_to_all | solution.py:759
  9.6 0.0 copy-done
  9.6 0.0 copy-done.1
  9.6 0.0 copy-done.2
  9.6 0.0 copy-done.3
  9.6 0.0 copy-done.4
  9.7 0.0 copy-done.5
  9.7 0.0 copy-done.6
  9.7 0.3 shard_map.112
  10.0 0.3 %collective-permute-start = (f32[296,128]{1,0:T(8,128)S(1)}, f32[296,128]{1,0:T(8,128)S(1)}, u32[]{:S(2)}, u32[]{:S(2)}) collective-permute-start(f32[296,128]{1,0:T(8,128)S(1)} %get-tuple-element.21), channel_id=1, source_target_pairs={{0,4},{1,5},{2,6},{3,7},{4,0},{5,1},{6,2},{7,3},{8,12},{9,13},{10,... | collective-permute-start | bytes 454664 | tf_op jit(solution)/shard_map/ppermute | solution.py:762
  10.3 4.0 %collective-permute-start.1 = (f32[296,128]{1,0:T(8,128)S(1)}, f32[296,128]{1,0:T(8,128)S(1)}, u32[]{:S(2)}, u32[]{:S(2)}) collective-permute-start(f32[296,128]{1,0:T(8,128)S(1)} %get-tuple-element.22), channel_id=1, source_target_pairs={{4,8},{5,9},{6,10},{7,11},{8,4},{9,5},{10,6},{11,7},{12,16},{13,17... | collective-permute-start | bytes 454664 | tf_op jit(solution)/shard_map/ppermute | solution.py:763
  14.3 4.8 %collective-permute-start.3 = (f32[72,128]{1,0:T(8,128)S(1)}, f32[72,128]{1,0:T(8,128)S(1)}, u32[]{:S(2)}, u32[]{:S(2)}) collective-permute-start(f32[72,128]{1,0:T(8,128)S(1)} %get-tuple-element.23), channel_id=1, source_target_pairs={{1,2},{2,1},{5,6},{6,5},{9,10},{10,9},{13,14},{14,13},{17,18},{18,... | collective-permute-start | bytes 110600 | tf_op jit(solution)/shard_map/ppermute | solution.py:761
  19.1 0.1 collective-permute-start.2
  19.2 2.5 %collective-permute-done.3.x2_ref = f32[72,128]{1,0:T(8,128)S(1)} collective-permute-done((f32[72,128]{1,0:T(8,128)S(1)}, f32[72,128]{1,0:T(8,128)S(1)}, u32[]{:S(2)}, u32[]{:S(2)}) %collective-permute-start.3) | collective-permute-done | bytes 36896 | tf_op jit(solution)/shard_map/ppermute | solution.py:761
  21.7 0.0 collective-permute-done.2.x1_ref
  21.7 1.3 %shard_map.113 = (f32[240,128]{1,0:T(8,128)S(1)}, f32[240,128]{1,0:T(8,128)S(1)}, f32[256,128]{1,0:T(8,128)S(1)}) custom-call(f32[240,128]{1,0:T(8,128)S(1)} %bitcast.11, f32[240,128]{1,0:T(8,128)S(1)} %bitcast.16, f32[240,128]{1,0:T(8,128)S(1)} %bitcast.28, f32[240,128]{1,0:T(8,128)S(1)} %bitcast.31, f32[240,128]{1,0:T(8,128)S(1)} %bitcast.21, ...), custom_call_target="tpu_custom_call" | custom-call | flops 4194304 | bytes 2097152 | tf_op jit(solution)/shard_map/pallas_call | solution.py:718
  23.0 0.0 collective-permute-done.y1_ref
  23.0 1.3 %collective-permute-done.1.y2_ref = f32[296,128]{1,0:T(8,128)S(1)} collective-permute-done((f32[296,128]{1,0:T(8,128)S(1)}, f32[296,128]{1,0:T(8,128)S(1)}, u32[]{:S(2)}, u32[]{:S(2)}) %collective-permute-start.1) | collective-permute-done | bytes 151584 | tf_op jit(solution)/shard_map/ppermute | solution.py:763
  24.3 0.0 all-to-all-done.ga_ref
  24.3 1.5 %collective-permute-start.4 = (f32[16,56,128]{2,1,0:T(8,128)S(1)}, f32[16,56,128]{2,1,0:T(8,128)S(1)}, u32[]{:S(2)}, u32[]{:S(2)}) collective-permute-start(f32[16,56,128]{2,1,0:T(8,128)S(1)} %all-to-all-done.ga_ref), channel_id=1, source_target_pairs={{0,1},{1,0},{2,3},{3,2},{4,5},{5,4},{6,7},{7,6},{8,9},{9,8},{10,11... | collective-permute-start | bytes 1376264 | tf_op jit(solution)/shard_map/ppermute | solution.py:772
  25.7 1.0 %shard_map.114 = (f32[240,128]{1,0:T(8,128)}, f32[240,128]{1,0:T(8,128)S(1)}, f32[1664,128]{1,0:T(8,128)S(1)}, f32[80,128]{1,0:T(8,128)S(1)}) custom-call(f32[240,128]{1,0:T(8,128)S(1)} %bitcast.12, f32[240,128]{1,0:T(8,128)S(1)} %bitcast.17, f32[240,128]{1,0:T(8,128)S(1)} %bitcast.29, f32[240,128]{1,0:T(8,128)S(1)} %bitcast.32, s32[8,128]{1,0:T(8,128)S(1)} %copy-done.6, ...), custom_call_target="tpu_custom_call" | custom-call | flops 4194304 | bytes 2097152 | tf_op jit(solution)/shard_map/pallas_call | solution.py:718
  26.7 0.4 %collective-permute-done.4.gb_ref = f32[16,56,128]{2,1,0:T(8,128)S(1)} collective-permute-done((f32[16,56,128]{2,1,0:T(8,128)S(1)}, f32[16,56,128]{2,1,0:T(8,128)S(1)}, u32[]{:S(2)}, u32[]{:S(2)}) %collective-permute-start.4) | collective-permute-done | bytes 458784 | tf_op jit(solution)/shard_map/ppermute | solution.py:772
  27.2 3.1 %shard_map.115 = (f32[240,128]{1,0:T(8,128)}, f32[240,128]{1,0:T(8,128)}, f32[8,128]{1,0:T(8,128)}) custom-call(f32[240,128]{1,0:T(8,128)S(1)} %bitcast.13, f32[240,128]{1,0:T(8,128)S(1)} %bitcast.18, f32[240,128]{1,0:T(8,128)S(1)} %bitcast.22, f32[240,128]{1,0:T(8,128)S(1)} %bitcast.26, f32[16,56,128]{2,1,0:T(8,128)S(1)} %all-to-all-done.ga_ref, ...), custom_call_target="tpu_custom_call" | custom-call | flops 8388608 | bytes 4194304 | tf_op jit(solution)/shard_map/pallas_call | solution.py:718
Async XLA Ops:
  2.7 6.9 %copy-start = (f32[30,8,128]{2,1,0:T(8,128)S(1)}, f32[30,8,128]{2,1,0:T(8,128)}, u32[]{:S(2)}) copy-start(f32[30,8,128]{2,1,0:T(8,128)} %param.8) | copy-start | bytes 368644
  2.8 6.9 %copy-start.1 = (f32[30,8,128]{2,1,0:T(8,128)S(1)}, f32[30,8,128]{2,1,0:T(8,128)}, u32[]{:S(2)}) copy-start(f32[30,8,128]{2,1,0:T(8,128)} %param.9) | copy-start | bytes 368644
  2.8 6.9 %copy-start.2 = (f32[30,8,128]{2,1,0:T(8,128)S(1)}, f32[30,8,128]{2,1,0:T(8,128)}, u32[]{:S(2)}) copy-start(f32[30,8,128]{2,1,0:T(8,128)} %param.12) | copy-start | bytes 368644
  2.8 6.9 %copy-start.3 = (f32[30,8,128]{2,1,0:T(8,128)S(1)}, f32[30,8,128]{2,1,0:T(8,128)}, u32[]{:S(2)}) copy-start(f32[30,8,128]{2,1,0:T(8,128)} %param.13) | copy-start | bytes 368644
  2.8 6.9 %copy-start.4 = (f32[30,8,128]{2,1,0:T(8,128)S(1)}, f32[30,8,128]{2,1,0:T(8,128)}, u32[]{:S(2)}) copy-start(f32[30,8,128]{2,1,0:T(8,128)} %param.10) | copy-start | bytes 368644
  2.8 6.9 %copy-start.5 = (f32[30,8,128]{2,1,0:T(8,128)S(1)}, f32[30,8,128]{2,1,0:T(8,128)}, u32[]{:S(2)}) copy-start(f32[30,8,128]{2,1,0:T(8,128)} %param.14) | copy-start | bytes 368644
  2.8 6.8 %copy-start.6 = (s32[8,128]{1,0:T(8,128)S(1)}, s32[8,128]{1,0:T(8,128)}, u32[]{:S(2)}) copy-start(s32[8,128]{1,0:T(8,128)} %count_ref.5) | copy-start | bytes 12292
  2.8 21.4 %all-to-all-start = ((f32[16,56,128]{2,1,0:T(8,128)}), f32[16,56,128]{2,1,0:T(8,128)S(1)}, u32[]{:S(2)}, u32[]{:S(2)}) async-start(f32[16,56,128]{2,1,0:T(8,128)} %shard_map.111), calls=%async_computation | async-start | bytes 917504 | tf_op jit(solution)/shard_map/all_to_all | solution.py:759
  10.0 13.0 %collective-permute-start = (f32[296,128]{1,0:T(8,128)S(1)}, f32[296,128]{1,0:T(8,128)S(1)}, u32[]{:S(2)}, u32[]{:S(2)}) collective-permute-start(f32[296,128]{1,0:T(8,128)S(1)} %get-tuple-element.21), channel_id=1, source_target_pairs={{0,4},{1,5},{2,6},{3,7},{4,0},{5,1},{6,2},{7,3},{8,12},{9,13},{10,... | collective-permute-start | bytes 454664 | tf_op jit(solution)/shard_map/ppermute | solution.py:762
  10.3 13.9 %collective-permute-start.1 = (f32[296,128]{1,0:T(8,128)S(1)}, f32[296,128]{1,0:T(8,128)S(1)}, u32[]{:S(2)}, u32[]{:S(2)}) collective-permute-start(f32[296,128]{1,0:T(8,128)S(1)} %get-tuple-element.22), channel_id=1, source_target_pairs={{4,8},{5,9},{6,10},{7,11},{8,4},{9,5},{10,6},{11,7},{12,16},{13,17... | collective-permute-start | bytes 454664 | tf_op jit(solution)/shard_map/ppermute | solution.py:763
  14.3 7.3 %collective-permute-start.3 = (f32[72,128]{1,0:T(8,128)S(1)}, f32[72,128]{1,0:T(8,128)S(1)}, u32[]{:S(2)}, u32[]{:S(2)}) collective-permute-start(f32[72,128]{1,0:T(8,128)S(1)} %get-tuple-element.23), channel_id=1, source_target_pairs={{1,2},{2,1},{5,6},{6,5},{9,10},{10,9},{13,14},{14,13},{17,18},{18,... | collective-permute-start | bytes 110600 | tf_op jit(solution)/shard_map/ppermute | solution.py:761
  19.1 2.6 %collective-permute-start.2 = (f32[72,128]{1,0:T(8,128)S(1)}, f32[72,128]{1,0:T(8,128)S(1)}, u32[]{:S(2)}, u32[]{:S(2)}) collective-permute-start(f32[72,128]{1,0:T(8,128)S(1)} %get-tuple-element.23), channel_id=1, source_target_pairs={{0,1},{1,0},{2,3},{3,2},{4,5},{5,4},{6,7},{7,6},{8,9},{9,8},{10,11... | collective-permute-start | bytes 110600 | tf_op jit(solution)/shard_map/ppermute | solution.py:760
  24.3 2.9 %collective-permute-start.4 = (f32[16,56,128]{2,1,0:T(8,128)S(1)}, f32[16,56,128]{2,1,0:T(8,128)S(1)}, u32[]{:S(2)}, u32[]{:S(2)}) collective-permute-start(f32[16,56,128]{2,1,0:T(8,128)S(1)} %all-to-all-done.ga_ref), channel_id=1, source_target_pairs={{0,1},{1,0},{2,3},{3,2},{4,5},{5,4},{6,7},{7,6},{8,9},{9,8},{10,11... | collective-permute-start | bytes 1376264 | tf_op jit(solution)/shard_map/ppermute | solution.py:772

commit v5 on v4

--- a/solution.py
+++ b/solution.py
@@ -16,6 +16,7 @@
 SEG = 32
 FIELDS = ("u", "v", "t", "st", "su", "sv")
 BAND_BLOCKS = 32
+ADJOINT_PARTS = ((4, 0), (1, 2), (3,))
 FLOW_FIELDS = ("u", "v", "su", "sv")
 FLOW_ROWS = {"u": (-2, 8), "v": (-1, 9), "su": (-1, 8), "sv": (-1, 8)}
 OUTER_ROWS = tuple((n, r) for n in FLOW_FIELDS for r in range(FLOW_ROWS[n][0], FLOW_ROWS[n][1] + 1) if not 0 <= r < 8)
@@ -184,20 +185,32 @@
     x_ref[SUB * SUB :, :] = count
 
 
+def joined(parts):
+    return Many([item for part in parts for item in part.items], len(parts))
+
+
 class Many:
-    def __init__(self, items):
+    def __init__(self, items, parts=1):
         self.items = list(items)
+        self.parts = parts
 
     def __getitem__(self, where):
-        return Many(self.items[where]) if isinstance(where, slice) else self.items[where]
+        if not isinstance(where, slice):
+            return self.items[where]
+        rows = len(self.items) // self.parts
+        return Many([item for n in range(self.parts) for item in self.items[n * rows : (n + 1) * rows][where]], self.parts)
 
     def __len__(self):
         return len(self.items)
+
+    def split(self):
+        rows = len(self.items) // self.parts
+        return [Many(self.items[n * rows : (n + 1) * rows]) for n in range(self.parts)]
 
     def apply(self, operation, *others):
         others = [other.items if isinstance(other, Many) else [other] * len(self) for other in others]
         assert all(len(other) == len(self) for other in others)
-        return Many(operation(*parts) for parts in zip(self.items, *others))
+        return Many([operation(*parts) for parts in zip(self.items, *others)], self.parts)
 
     def __add__(self, other):
         return self.apply(lambda a, b: a + b, other)
@@ -648,9 +661,10 @@
 
     def beside_setup():
         wet_counts.extend(pairs(lambda dj, di: near(dj, di, lambda j, i: count_s[j, i]), jnp.minimum))
-        prepare(groups)
 
     def beside_sum(k):
+        if k == ITERS - 1:
+            prepare(groups)
         differences.append(pairs(lambda dj, di: block(dj, di, lambda j, i: r_s[k, j, i]), lambda a, b: a - b))
 
     weights = surface_solve(levels, ny, nx, read, count_s, face_s, r_s, beside_setup, beside_sum)
@@ -666,15 +680,21 @@
     out = [pltpu.make_async_copy(eta_ref, eta_hbm, sems.at[0])]
     out[0].start()
 
-    def adjoint(part):
-        kind = 1 if part == groups else 0
-        level = numbers[part]
-        u, v, su, sv = data[part]
-        v_bar, u_bar, from_v_bar, from_u_bar, u_across, v_across = made[part]
-        wet_u = outer_and_own(*wet_counts[kind][:2]) > level
-        wet_v = outer_and_own(*wet_counts[kind][2:]) > level
-        u_cot = su + (outer_and_own(*slopes[kind][:2]) * thick[part]).where(wet_u, zero)
-        v_cot = sv + (outer_and_own(*slopes[kind][2:]) * thick[part]).where(wet_v, zero)
+    def adjoint(parts):
+        u, v, su, sv = (joined([data[part][n] for part in parts]) for n in range(4))
+        v_bar, u_bar, from_v_bar, from_u_bar, u_across, v_across = (
+            joined([made[part][n] for part in parts]) for n in range(len(MADE_SIZES))
+        )
+
+        def each(values):
+            return Many([values[part] for part in parts for _ in range(SUB + 2)], len(parts))
+
+        def around(of, n):
+            return joined([outer_and_own(*of[1 if part == groups else 0][n : n + 2]) for part in parts])
+
+        wet_u, wet_v = around(wet_counts, 0) > each(numbers), around(wet_counts, 2) > each(numbers)
+        u_cot = su + (around(slopes, 0) * each(thick)).where(wet_u, zero)
+        v_cot = sv + (around(slopes, 2) * each(thick)).where(wet_v, zero)
         a, b = (u_cot * (0.5 * ADVECT)).where(wet_u, zero), (v_cot * (0.5 * ADVECT)).where(wet_v, zero)
         av, bu = a * v_bar, b[1:9] * u_bar
         au, bv = a[1:9] * u[2:10], b * v[:-1]
@@ -684,12 +704,16 @@
         du = du + au.at(1) + (near_u - au).at(-1)
         dv = v_cot[1:9] - b[1:9] * v_across + bv[2:] - bv[:-2] + near_v
         dv = dv + (near_v + bu).at(1) - bu.at(-1)
-        return du, dv
-
-    edge_u, edge_v = (outer_columns(part) for part in adjoint(groups))
+        return list(zip(du.split(), dv.split()))
+
+    for part in range(groups):
+        prepare(part)
+    flow = {}
+    for parts in ADJOINT_PARTS:
+        flow.update(zip(parts, adjoint(parts)))
+    edge_u, edge_v = (outer_columns(part) for part in flow[groups])
     for q in range(groups):
-        prepare(q)
-        du, dv = adjoint(q)
+        du, dv = flow[q]
         store_rows(du_ref, q, levels, merge_edges(du, edge_u, q) + load_rows(dut_ref, q, levels))
         store_rows(dv_ref, q, levels, merge_edges(dv, edge_v, q) + load_rows(dvt_ref, q, levels))
         part = pl.ds(q * SUB * SUB, min(SUB, levels - q * SUB) * SUB)

time: 30.5 us -> 30.3 us (level)
  no operation moved by 1% of the time
where the time goes in v5:
time: 30.3 us; the launch traced here: 30 us
  starting transfers between devices  17.4 us (57%)
  Pallas kernels  7.58 us (25%)
  waiting for transfers between devices  4.2 us (14%)
  between operations  0.8 us (3%)
    pallas_call x5, Pallas kernels, call(): pl.pallas_call(kernel, out_shape=outs, in_specs=[far if far_in else near]...  7.58 us
    all_to_all x1, starting transfers between devices, on_device(): ga = lax.all_to_all(chunks, ('ty', 'y'), 0, 0)  6.78 us
    ppermute x1, starting transfers between devices, on_device(): x2 = lax.ppermute(xp, axes, swaps(shape, 'x', 1))  4.77 us
    ppermute x1, starting transfers between devices, on_device(): y2 = lax.ppermute(y2, axes, swaps(shape, 'y', 1))  3.98 us
    ppermute x1, waiting for transfers between devices, on_device(): x2 = lax.ppermute(xp, axes, swaps(shape, 'x', 1))  2.48 us
    ppermute x1, starting transfers between devices, on_device(): gb = lax.ppermute(ga, axes, swaps(shape, 'x', 0))  1.45 us
    ppermute x1, waiting for transfers between devices, on_device(): y2 = lax.ppermute(y2, axes, swaps(shape, 'y', 1))  1.29 us
  transfers between devices with their start and end apart: 6, of which 3 were waited for; matrix products, arithmetic and copies ran while one was open for 0% of the time, Pallas kernels for 9%

profile of v5, /device:TPU:11, one launch (start us, length us, event | category | flops | bytes accessed | tf_op | source)
XLA Modules:
  0.0 30.0 jit_solution(165309276693015626)
XLA Ops:
  0.6 2.1 %shard_map.111 = f32[16,56,128]{2,1,0:T(8,128)} custom-call(f32[240,128]{1,0:T(8,128)} %bitcast.9, f32[240,128]{1,0:T(8,128)} %bitcast.14, f32[240,128]{1,0:T(8,128)} %bitcast.19, f32[240,128]{1,0:T(8,128)} %bitcast.23, s32[8,128]{1,0:T(8,128)} %count_ref.5, f32[8,128]{1,0:T(8,128)} %elev_hbm.1), custom_call_target="tpu_custom_call" | custom-call | flops 1048576 | bytes 2097152 | tf_op jit(solution)/shard_map/pallas_call | solution.py:742
  2.7 0.0 copy-start
  2.8 0.0 copy-start.1
  2.8 0.0 copy-start.2
  2.8 0.0 copy-start.3
  2.8 0.0 copy-start.4
  2.8 0.0 copy-start.5
  2.8 0.0 copy-start.6
  2.8 6.8 %all-to-all-start = ((f32[16,56,128]{2,1,0:T(8,128)}), f32[16,56,128]{2,1,0:T(8,128)S(1)}, u32[]{:S(2)}, u32[]{:S(2)}) async-start(f32[16,56,128]{2,1,0:T(8,128)} %shard_map.111), calls=%async_computation | async-start | bytes 917504 | tf_op jit(solution)/shard_map/all_to_all | solution.py:783
  9.6 0.0 copy-done
  9.6 0.0 copy-done.1
  9.6 0.0 copy-done.2
  9.6 0.0 copy-done.3
  9.6 0.0 copy-done.4
  9.7 0.0 copy-done.5
  9.7 0.0 copy-done.6
  9.7 0.3 shard_map.112
  10.0 0.3 %collective-permute-start = (f32[296,128]{1,0:T(8,128)S(1)}, f32[296,128]{1,0:T(8,128)S(1)}, u32[]{:S(2)}, u32[]{:S(2)}) collective-permute-start(f32[296,128]{1,0:T(8,128)S(1)} %get-tuple-element.21), channel_id=1, source_target_pairs={{0,4},{1,5},{2,6},{3,7},{4,0},{5,1},{6,2},{7,3},{8,12},{9,13},{10,... | collective-permute-start | bytes 454664 | tf_op jit(solution)/shard_map/ppermute | solution.py:786
  10.3 4.0 %collective-permute-start.1 = (f32[296,128]{1,0:T(8,128)S(1)}, f32[296,128]{1,0:T(8,128)S(1)}, u32[]{:S(2)}, u32[]{:S(2)}) collective-permute-start(f32[296,128]{1,0:T(8,128)S(1)} %get-tuple-element.22), channel_id=1, source_target_pairs={{4,8},{5,9},{6,10},{7,11},{8,4},{9,5},{10,6},{11,7},{12,16},{13,17... | collective-permute-start | bytes 454664 | tf_op jit(solution)/shard_map/ppermute | solution.py:787
  14.3 4.8 %collective-permute-start.3 = (f32[72,128]{1,0:T(8,128)S(1)}, f32[72,128]{1,0:T(8,128)S(1)}, u32[]{:S(2)}, u32[]{:S(2)}) collective-permute-start(f32[72,128]{1,0:T(8,128)S(1)} %get-tuple-element.23), channel_id=1, source_target_pairs={{1,2},{2,1},{5,6},{6,5},{9,10},{10,9},{13,14},{14,13},{17,18},{18,... | collective-permute-start | bytes 110600 | tf_op jit(solution)/shard_map/ppermute | solution.py:785
  19.1 0.1 collective-permute-start.2
  19.2 2.5 %collective-permute-done.3.x2_ref = f32[72,128]{1,0:T(8,128)S(1)} collective-permute-done((f32[72,128]{1,0:T(8,128)S(1)}, f32[72,128]{1,0:T(8,128)S(1)}, u32[]{:S(2)}, u32[]{:S(2)}) %collective-permute-start.3) | collective-permute-done | bytes 36896 | tf_op jit(solution)/shard_map/ppermute | solution.py:785
  21.7 0.0 collective-permute-done.2.x1_ref
  21.7 1.3 %shard_map.113 = (f32[240,128]{1,0:T(8,128)S(1)}, f32[240,128]{1,0:T(8,128)S(1)}, f32[256,128]{1,0:T(8,128)S(1)}) custom-call(f32[240,128]{1,0:T(8,128)S(1)} %bitcast.11, f32[240,128]{1,0:T(8,128)S(1)} %bitcast.16, f32[240,128]{1,0:T(8,128)S(1)} %bitcast.28, f32[240,128]{1,0:T(8,128)S(1)} %bitcast.31, f32[240,128]{1,0:T(8,128)S(1)} %bitcast.21, ...), custom_call_target="tpu_custom_call" | custom-call | flops 4194304 | bytes 2097152 | tf_op jit(solution)/shard_map/pallas_call | solution.py:742
  23.0 0.0 collective-permute-done.y1_ref
  23.0 1.3 %collective-permute-done.1.y2_ref = f32[296,128]{1,0:T(8,128)S(1)} collective-permute-done((f32[296,128]{1,0:T(8,128)S(1)}, f32[296,128]{1,0:T(8,128)S(1)}, u32[]{:S(2)}, u32[]{:S(2)}) %collective-permute-start.1) | collective-permute-done | bytes 151584 | tf_op jit(solution)/shard_map/ppermute | solution.py:787
  24.3 0.0 all-to-all-done.ga_ref
  24.3 1.5 %collective-permute-start.4 = (f32[16,56,128]{2,1,0:T(8,128)S(1)}, f32[16,56,128]{2,1,0:T(8,128)S(1)}, u32[]{:S(2)}, u32[]{:S(2)}) collective-permute-start(f32[16,56,128]{2,1,0:T(8,128)S(1)} %all-to-all-done.ga_ref), channel_id=1, source_target_pairs={{0,1},{1,0},{2,3},{3,2},{4,5},{5,4},{6,7},{7,6},{8,9},{9,8},{10,11... | collective-permute-start | bytes 1376264 | tf_op jit(solution)/shard_map/ppermute | solution.py:796
  25.7 1.0 %shard_map.114 = (f32[240,128]{1,0:T(8,128)}, f32[240,128]{1,0:T(8,128)S(1)}, f32[1664,128]{1,0:T(8,128)S(1)}, f32[80,128]{1,0:T(8,128)S(1)}) custom-call(f32[240,128]{1,0:T(8,128)S(1)} %bitcast.12, f32[240,128]{1,0:T(8,128)S(1)} %bitcast.17, f32[240,128]{1,0:T(8,128)S(1)} %bitcast.29, f32[240,128]{1,0:T(8,128)S(1)} %bitcast.32, s32[8,128]{1,0:T(8,128)S(1)} %copy-done.6, ...), custom_call_target="tpu_custom_call" | custom-call | flops 4194304 | bytes 2097152 | tf_op jit(solution)/shard_map/pallas_call | solution.py:742
  26.7 0.4 %collective-permute-done.4.gb_ref = f32[16,56,128]{2,1,0:T(8,128)S(1)} collective-permute-done((f32[16,56,128]{2,1,0:T(8,128)S(1)}, f32[16,56,128]{2,1,0:T(8,128)S(1)}, u32[]{:S(2)}, u32[]{:S(2)}) %collective-permute-start.4) | collective-permute-done | bytes 458784 | tf_op jit(solution)/shard_map/ppermute | solution.py:796
  27.2 2.9 %shard_map.115 = (f32[240,128]{1,0:T(8,128)}, f32[240,128]{1,0:T(8,128)}, f32[8,128]{1,0:T(8,128)}) custom-call(f32[240,128]{1,0:T(8,128)S(1)} %bitcast.13, f32[240,128]{1,0:T(8,128)S(1)} %bitcast.18, f32[240,128]{1,0:T(8,128)S(1)} %bitcast.22, f32[240,128]{1,0:T(8,128)S(1)} %bitcast.26, f32[16,56,128]{2,1,0:T(8,128)S(1)} %all-to-all-done.ga_ref, ...), custom_call_target="tpu_custom_call" | custom-call | flops 8388608 | bytes 4194304 | tf_op jit(solution)/shard_map/pallas_call | solution.py:742
Async XLA Ops:
  2.7 6.9 %copy-start = (f32[30,8,128]{2,1,0:T(8,128)S(1)}, f32[30,8,128]{2,1,0:T(8,128)}, u32[]{:S(2)}) copy-start(f32[30,8,128]{2,1,0:T(8,128)} %param.8) | copy-start | bytes 368644
  2.8 6.9 %copy-start.1 = (f32[30,8,128]{2,1,0:T(8,128)S(1)}, f32[30,8,128]{2,1,0:T(8,128)}, u32[]{:S(2)}) copy-start(f32[30,8,128]{2,1,0:T(8,128)} %param.9) | copy-start | bytes 368644
  2.8 6.9 %copy-start.2 = (f32[30,8,128]{2,1,0:T(8,128)S(1)}, f32[30,8,128]{2,1,0:T(8,128)}, u32[]{:S(2)}) copy-start(f32[30,8,128]{2,1,0:T(8,128)} %param.12) | copy-start | bytes 368644
  2.8 6.9 %copy-start.3 = (f32[30,8,128]{2,1,0:T(8,128)S(1)}, f32[30,8,128]{2,1,0:T(8,128)}, u32[]{:S(2)}) copy-start(f32[30,8,128]{2,1,0:T(8,128)} %param.13) | copy-start | bytes 368644
  2.8 6.9 %copy-start.4 = (f32[30,8,128]{2,1,0:T(8,128)S(1)}, f32[30,8,128]{2,1,0:T(8,128)}, u32[]{:S(2)}) copy-start(f32[30,8,128]{2,1,0:T(8,128)} %param.10) | copy-start | bytes 368644
  2.8 6.9 %copy-start.5 = (f32[30,8,128]{2,1,0:T(8,128)S(1)}, f32[30,8,128]{2,1,0:T(8,128)}, u32[]{:S(2)}) copy-start(f32[30,8,128]{2,1,0:T(8,128)} %param.14) | copy-start | bytes 368644
  2.8 6.8 %copy-start.6 = (s32[8,128]{1,0:T(8,128)S(1)}, s32[8,128]{1,0:T(8,128)}, u32[]{:S(2)}) copy-start(s32[8,128]{1,0:T(8,128)} %count_ref.5) | copy-start | bytes 12292
  2.8 21.4 %all-to-all-start = ((f32[16,56,128]{2,1,0:T(8,128)}), f32[16,56,128]{2,1,0:T(8,128)S(1)}, u32[]{:S(2)}, u32[]{:S(2)}) async-start(f32[16,56,128]{2,1,0:T(8,128)} %shard_map.111), calls=%async_computation | async-start | bytes 917504 | tf_op jit(solution)/shard_map/all_to_all | solution.py:783
  10.0 13.0 %collective-permute-start = (f32[296,128]{1,0:T(8,128)S(1)}, f32[296,128]{1,0:T(8,128)S(1)}, u32[]{:S(2)}, u32[]{:S(2)}) collective-permute-start(f32[296,128]{1,0:T(8,128)S(1)} %get-tuple-element.21), channel_id=1, source_target_pairs={{0,4},{1,5},{2,6},{3,7},{4,0},{5,1},{6,2},{7,3},{8,12},{9,13},{10,... | collective-permute-start | bytes 454664 | tf_op jit(solution)/shard_map/ppermute | solution.py:786
  10.3 13.9 %collective-permute-start.1 = (f32[296,128]{1,0:T(8,128)S(1)}, f32[296,128]{1,0:T(8,128)S(1)}, u32[]{:S(2)}, u32[]{:S(2)}) collective-permute-start(f32[296,128]{1,0:T(8,128)S(1)} %get-tuple-element.22), channel_id=1, source_target_pairs={{4,8},{5,9},{6,10},{7,11},{8,4},{9,5},{10,6},{11,7},{12,16},{13,17... | collective-permute-start | bytes 454664 | tf_op jit(solution)/shard_map/ppermute | solution.py:787
  14.3 7.3 %collective-permute-start.3 = (f32[72,128]{1,0:T(8,128)S(1)}, f32[72,128]{1,0:T(8,128)S(1)}, u32[]{:S(2)}, u32[]{:S(2)}) collective-permute-start(f32[72,128]{1,0:T(8,128)S(1)} %get-tuple-element.23), channel_id=1, source_target_pairs={{1,2},{2,1},{5,6},{6,5},{9,10},{10,9},{13,14},{14,13},{17,18},{18,... | collective-permute-start | bytes 110600 | tf_op jit(solution)/shard_map/ppermute | solution.py:785
  19.1 2.6 %collective-permute-start.2 = (f32[72,128]{1,0:T(8,128)S(1)}, f32[72,128]{1,0:T(8,128)S(1)}, u32[]{:S(2)}, u32[]{:S(2)}) collective-permute-start(f32[72,128]{1,0:T(8,128)S(1)} %get-tuple-element.23), channel_id=1, source_target_pairs={{0,1},{1,0},{2,3},{3,2},{4,5},{5,4},{6,7},{7,6},{8,9},{9,8},{10,11... | collective-permute-start | bytes 110600 | tf_op jit(solution)/shard_map/ppermute | solution.py:784
  24.3 2.9 %collective-permute-start.4 = (f32[16,56,128]{2,1,0:T(8,128)S(1)}, f32[16,56,128]{2,1,0:T(8,128)S(1)}, u32[]{:S(2)}, u32[]{:S(2)}) collective-permute-start(f32[16,56,128]{2,1,0:T(8,128)S(1)} %all-to-all-done.ga_ref), channel_id=1, source_target_pairs={{0,1},{1,0},{2,3},{3,2},{4,5},{5,4},{6,7},{7,6},{8,9},{9,8},{10,11... | collective-permute-start | bytes 1376264 | tf_op jit(solution)/shard_map/ppermute | solution.py:796

commit v6 on v5

--- a/solution.py
+++ b/solution.py
@@ -26,10 +26,11 @@
 SOUTH_SLOTS.update({("su", -1): 7, ("sv", -1): 8})
 NORTH_SLOTS = {("u", 8): 0, ("v", 8): 1, ("v", 9): 2, ("t", 8): 3, ("st", 8): 5, ("st", 9): 6, ("su", 8): 7, ("sv", 8): 8}
 N_SLOTS = 9
-CHUNK_LOAD = SUB
-CHUNK_EDGE = 2 * SUB
-CHUNK_ROW = 3 * SUB
-EDGE_LEVELS = 20
+TILE = SUB * LANES
+CHUNK_LOAD = TILE
+CHUNK_ROW = 2 * TILE
+WEST_LEVELS = LANES // SUB
+CORNERS_PER_ROW = 4
 CORNERS = (("u", 6, 0), ("u", 7, 0), ("u", 7, 1), ("su", 7, 0), ("v", 7, 127), ("u", 7, 127))
 CORNERS += (("v", 0, 127), ("v", 1, 127), ("v", 0, 126), ("sv", 0, 127), ("v", 0, 0), ("u", 0, 0))
 CORNER_PLACES = {
@@ -120,31 +121,45 @@
 
     wet_u = jnp.where(lanes == 0, 0.0, jnp.minimum(count, roll_lanes(count, 1)))
     wet_v = jnp.where(rows == 0, 0.0, jnp.minimum(count, roll_rows(count, 1)))
-    col_u, col_v, edge = [zero] * 4, [zero] * 4, zero
+    col_u, col_v = [zero] * 4, [zero] * 4
+    west = [zero] * (levels // WEST_LEVELS + 1)
     for k in range(levels):
         su_level = su_ref[k * SUB : (k + 1) * SUB, :]
         col_u[k % 4] = col_u[k % 4] + jnp.where(wet_u > float(k), su_level, 0.0)
         col_v[k % 4] = col_v[k % 4] + jnp.where(wet_v > float(k), sv_ref[k * SUB : (k + 1) * SUB, :], 0.0)
-        lane = SEG * (k // EDGE_LEVELS) + k % EDGE_LEVELS
-        edge = jnp.where(lanes == lane, roll_lanes(su_level, lane), edge)
+        n = k // WEST_LEVELS
+        there = lanes == rows + k % WEST_LEVELS * SUB
+        west[n] = jnp.where(there, jnp.broadcast_to(su_level[:, 0:1], (SUB, LANES)), west[n])
     col_u, col_v = ((col[0] + col[1]) + (col[2] + col[3]) for col in (col_u, col_v))
     load = elev_ref[...] + GRAVITY_DT * (at(col_u, 1) - col_u + roll_rows(col_v, -1) - col_v)
 
     for copy in copies[4:]:
         copy.wait()
+    corners = [zero] * (len(CORNERS) // CORNERS_PER_ROW)
     for place, (name, row, column) in enumerate(CORNERS):
+        n, base = place // CORNERS_PER_ROW, place % CORNERS_PER_ROW * SUB
         for q in range(groups):
-            lane = SEG * q + EDGE_LEVELS + place
-            edge = jnp.where(lanes == lane, roll_lanes(load_group(refs[name], row, q, levels), lane - column), edge)
-
-    south_row = [load_group(sv_ref, 0, q, levels) for q in range(groups)]
+            value = load_group(refs[name], row, q, levels)[:, column : column + 1]
+            there = lanes == SEG * q + base + SUB - 1 - rows
+            corners[n] = jnp.where(there, jnp.broadcast_to(value, (SUB, LANES)), corners[n])
+
+    def in_a_row(tile):
+        return jnp.broadcast_to(jnp.sum(tile, axis=0, keepdims=True), (SUB, LANES))
+
+    tiles = [count, load] + [load_group(sv_ref, 0, q, levels) for q in range(groups)]
+    for n, part in enumerate(west):
+        tiles[-1] = jnp.where(rows == SUB - len(west) + n, in_a_row(part), tiles[-1])
+    last = zero
+    for n, part in enumerate(corners):
+        last = jnp.where(rows == n, in_a_row(part), last)
+    tiles = [tile.reshape(1, TILE) for tile in tiles + [last]]
+    tiles[-1] = tiles[-1][:, : len(corners) * LANES]
 
     def put(peer, carry):
-        chunk_ref[peer, 0:SUB, :] = count
-        chunk_ref[peer, CHUNK_LOAD : CHUNK_LOAD + SUB, :] = load
-        chunk_ref[peer, CHUNK_EDGE : CHUNK_EDGE + SUB, :] = edge
-        for q in range(groups):
-            chunk_ref[peer, CHUNK_ROW + q * SUB : CHUNK_ROW + (q + 1) * SUB, :] = south_row[q]
+        first = 0
+        for tile in tiles:
+            chunk_ref[peer, :, first : first + tile.shape[1]] = tile
+            first += tile.shape[1]
         return carry
 
     lax.fori_loop(0, peers, put, 0, unroll=4)
@@ -482,19 +497,19 @@
         wet_v = Many([zero] * len(cells)).where(Many(first_row), wet_v)
         put(face_ref.at[0], j, depth(wet_u))
         put(face_ref.at[1], j, depth(wet_v))
-        edge = Many(read(j + dj, i, CHUNK_EDGE) for dj, i in cells)
         wet_west = wet_u.apply(lambda a: jnp.broadcast_to(a[:, 0:1], (SUB, LANES)))
-        place = lanes & (SEG - 1)
-        number = (lanes >> 5) * EDGE_LEVELS + place
-        reach = jnp.where((place < EDGE_LEVELS) & (number < levels), number.astype(jnp.float32), float(levels))
-        inside = edge.where(wet_west > reach, zero)
+        souths = [Many(read(j + dj, i, CHUNK_ROW + q * TILE) for dj, i in cells) for q in range(groups)]
+        inside = Many([zero] * len(cells))
+        for n in range(levels // WEST_LEVELS + 1):
+            reach = jnp.where((lanes & (SUB - 1)) == rows, (lanes >> 3) + n * WEST_LEVELS, levels).astype(jnp.float32)
+            west = souths[-1].apply(lambda a: row_of(a, SUB - 1 - levels // WEST_LEVELS + n))
+            inside = inside + west.where(wet_west > reach, zero)
         col_u = inside.apply(lambda a: jnp.broadcast_to(jnp.sum(a, axis=1, keepdims=True), (SUB, LANES)))
         put(face_ref.at[4], j, col_u * GRAVITY_DT)
         wet_south = wet_v.apply(lambda a: row_of(a, 0))
         col_v = Many([zero] * len(cells))
         for q in range(groups):
-            south = Many(read(j + dj, i, CHUNK_ROW + q * SUB) for dj, i in cells)
-            col_v = col_v + south.where(wet_south > numbers[q], zero)
+            col_v = col_v + souths[q].where(wet_south > numbers[q], zero)
         col_v = col_v.apply(lambda a: jnp.broadcast_to(jnp.sum(a, axis=0, keepdims=True), (SUB, LANES)))
         put(face_ref.at[5], j, col_v * GRAVITY_DT)
         return carry
@@ -589,8 +604,13 @@
     zero = jnp.zeros((SUB, LANES), jnp.float32)
 
     def read(j, i, first):
-        where = (j * (nx // 2) + i // 2, pl.ds(first, SUB), slice(None))
-        return jnp.where(core == i % 2, ga_ref[where], gb_ref[where])
+        where = (j * (nx // 2) + i // 2, slice(None), pl.ds(first, TILE))
+        return jnp.where(core == i % 2, ga_ref[where].reshape(SUB, LANES), gb_ref[where].reshape(SUB, LANES))
+
+    def read_corners(n, j, i):
+        where = (j * (nx // 2) + i // 2, slice(None), pl.ds(CHUNK_ROW + groups * TILE + n * LANES, LANES))
+        row = jnp.broadcast_to(jnp.where(core == i % 2, ga_ref[where], gb_ref[where]), (SUB, LANES))
+        return pltpu.roll(row, LANES - SUB + 1, 1, stride=1, stride_axis=0)
 
     def block(dj, di, get):
         return get(jnp.clip(my_j + dj, 0, ny - 1), jnp.clip(my_i + di, 0, nx - 1))
@@ -600,15 +620,19 @@
         inside = (my_j + dj >= 0) & (my_j + dj < ny) & (my_i + di >= 0) & (my_i + di < nx)
         return jnp.where(inside, get(j, i), 0.0)
 
-    corner_tiles = {
-        name: near(dj, di, lambda j, i: read(j, i, CHUNK_EDGE))
-        for name, dj, di in (("se", -1, 1), ("sw", -1, -1), ("nw", 1, -1), ("ne", 1, 1))
-    }
+    diagonal = {"se": (-1, 1), "sw": (-1, -1), "nw": (1, -1), "ne": (1, 1)}
+    corner_tiles = {}
+    for places in CORNER_PLACES.values():
+        for which, value, _ in places:
+            n = value // CORNERS_PER_ROW
+            if (which, n) not in corner_tiles:
+                corner_tiles[which, n] = near(*diagonal[which], functools.partial(read_corners, n))
 
     def insert_corners(edge, name, row):
         for which, value, target in CORNER_PLACES.get((name, row), ()):
             there = (lanes & (SEG - 1)) == target
-            edge = jnp.where(there, roll_lanes(corner_tiles[which], target - EDGE_LEVELS - value), edge)
+            tile = corner_tiles[which, value // CORNERS_PER_ROW]
+            edge = jnp.where(there, roll_lanes(tile, target - value % CORNERS_PER_ROW * SUB), edge)
         return edge
 
     def rows(name, ref, q, first, last):
@@ -759,7 +783,7 @@
     peers = ny * nx // 2
     row_packet = ((N_SLOTS * groups + 1) * SUB, LANES)
     column_packet = ((SUB + 1) * SUB, LANES)
-    chunk = (peers, CHUNK_ROW + groups * SUB, LANES)
+    chunk = (peers, 1, CHUNK_ROW + groups * TILE + len(CORNERS) // CORNERS_PER_ROW * LANES)
     tile = (SUB, LANES)
     (chunks,) = call(
         functools.partial(chunk_kernel, levels, peers),

time: 30.3 us -> 29.5 us (0.974)
  waiting for transfers between devices: 4.2 us -> 3.32 us
    ppermute x1, waiting for transfers between devices: 2.48 us -> 2.02 us  [on_device(): x2 = lax.ppermute(xp, axes, swaps(shape, 'x', 1))]
    ppermute x1, waiting for transfers between devices: 1.29 us -> 0.93 us  [on_device(): y2 = lax.ppermute(y2, axes, swaps(shape, 'y', 1))]
where the time goes in v6:
time: 29.5 us; the launch traced here: 29.3 us
  starting transfers between devices  17.4 us (59%)
  Pallas kernels  7.71 us (26%)
  waiting for transfers between devices  3.32 us (11%)
  between operations  0.8 us (3%)
    pallas_call x5, Pallas kernels, call(): pl.pallas_call(kernel, out_shape=outs, in_specs=[far if far_in else near]...  7.71 us
    all_to_all x1, starting transfers between devices, on_device(): ga = lax.all_to_all(chunks, ('ty', 'y'), 0, 0)  6.78 us
    ppermute x1, starting transfers between devices, on_device(): x2 = lax.ppermute(xp, axes, swaps(shape, 'x', 1))  4.77 us
    ppermute x1, starting transfers between devices, on_device(): y2 = lax.ppermute(y2, axes, swaps(shape, 'y', 1))  3.98 us
    ppermute x1, waiting for transfers between devices, on_device(): x2 = lax.ppermute(xp, axes, swaps(shape, 'x', 1))  2.02 us
    ppermute x1, starting transfers between devices, on_device(): gb = lax.ppermute(ga, axes, swaps(shape, 'x', 0))  1.45 us
    ppermute x1, waiting for transfers between devices, on_device(): y2 = lax.ppermute(y2, axes, swaps(shape, 'y', 1))  0.93 us
  transfers between devices with their start and end apart: 6, of which 3 were waited for; matrix products, arithmetic and copies ran while one was open for 0% of the time, Pallas kernels for 9%

profile of v6, /device:TPU:11, one launch (start us, length us, event | category | flops | bytes accessed | tf_op | source)
XLA Modules:
  0.0 29.3 jit_solution(367018766847643458)
XLA Ops:
  0.6 2.1 %shard_map.111 = f32[16,1,6528]{2,1,0:T(1,128)} custom-call(f32[240,128]{1,0:T(8,128)} %bitcast.9, f32[240,128]{1,0:T(8,128)} %bitcast.14, f32[240,128]{1,0:T(8,128)} %bitcast.19, f32[240,128]{1,0:T(8,128)} %bitcast.23, s32[8,128]{1,0:T(8,128)} %count_ref.5, f32[8,128]{1,0:T(8,128)} %elev_hbm.1), custom_call_target="tpu_custom_call" | custom-call | flops 1048576 | bytes 2097152 | tf_op jit(solution)/shard_map/pallas_call | solution.py:766
  2.7 0.0 copy-start
  2.8 0.0 copy-start.1
  2.8 0.0 copy-start.2
  2.8 0.0 copy-start.3
  2.8 0.0 copy-start.4
  2.8 0.0 copy-start.5
  2.8 0.0 copy-start.6
  2.8 6.8 %all-to-all-start = ((f32[16,1,6528]{2,1,0:T(1,128)}), f32[16,1,6528]{2,1,0:T(1,128)S(1)}, u32[]{:S(2)}, u32[]{:S(2)}) async-start(f32[16,1,6528]{2,1,0:T(1,128)} %shard_map.111), calls=%async_computation | async-start | bytes 835584 | tf_op jit(solution)/shard_map/all_to_all | solution.py:807
  9.6 0.0 copy-done
  9.6 0.0 copy-done.1
  9.6 0.0 copy-done.2
  9.6 0.0 copy-done.3
  9.6 0.0 copy-done.4
  9.7 0.0 copy-done.5
  9.7 0.0 copy-done.6
  9.7 0.3 %shard_map.112 = (f32[296,128]{1,0:T(8,128)S(1)}, f32[296,128]{1,0:T(8,128)S(1)}, f32[72,128]{1,0:T(8,128)S(1)}) custom-call(f32[240,128]{1,0:T(8,128)S(1)} %bitcast.10, f32[240,128]{1,0:T(8,128)S(1)} %bitcast.15, f32[240,128]{1,0:T(8,128)S(1)} %bitcast.27, f32[240,128]{1,0:T(8,128)S(1)} %bitcast.20, f32[240,128]{1,0:T(8,128)S(1)} %bitcast.24, ...), custom_call_target="tpu_custom_call" | custom-call | flops 1048576 | bytes 2097152 | tf_op jit(solution)/shard_map/pallas_call | solution.py:766
  10.0 0.3 %collective-permute-start = (f32[296,128]{1,0:T(8,128)S(1)}, f32[296,128]{1,0:T(8,128)S(1)}, u32[]{:S(2)}, u32[]{:S(2)}) collective-permute-start(f32[296,128]{1,0:T(8,128)S(1)} %get-tuple-element.21), channel_id=1, source_target_pairs={{0,4},{1,5},{2,6},{3,7},{4,0},{5,1},{6,2},{7,3},{8,12},{9,13},{10,... | collective-permute-start | bytes 454664 | tf_op jit(solution)/shard_map/ppermute | solution.py:810
  10.3 4.0 %collective-permute-start.1 = (f32[296,128]{1,0:T(8,128)S(1)}, f32[296,128]{1,0:T(8,128)S(1)}, u32[]{:S(2)}, u32[]{:S(2)}) collective-permute-start(f32[296,128]{1,0:T(8,128)S(1)} %get-tuple-element.22), channel_id=1, source_target_pairs={{4,8},{5,9},{6,10},{7,11},{8,4},{9,5},{10,6},{11,7},{12,16},{13,17... | collective-permute-start | bytes 454664 | tf_op jit(solution)/shard_map/ppermute | solution.py:811
  14.3 4.8 %collective-permute-start.3 = (f32[72,128]{1,0:T(8,128)S(1)}, f32[72,128]{1,0:T(8,128)S(1)}, u32[]{:S(2)}, u32[]{:S(2)}) collective-permute-start(f32[72,128]{1,0:T(8,128)S(1)} %get-tuple-element.23), channel_id=1, source_target_pairs={{1,2},{2,1},{5,6},{6,5},{9,10},{10,9},{13,14},{14,13},{17,18},{18,... | collective-permute-start | bytes 110600 | tf_op jit(solution)/shard_map/ppermute | solution.py:809
  19.1 0.1 collective-permute-start.2
  19.2 2.0 %collective-permute-done.3.x2_ref = f32[72,128]{1,0:T(8,128)S(1)} collective-permute-done((f32[72,128]{1,0:T(8,128)S(1)}, f32[72,128]{1,0:T(8,128)S(1)}, u32[]{:S(2)}, u32[]{:S(2)}) %collective-permute-start.3) | collective-permute-done | bytes 36896 | tf_op jit(solution)/shard_map/ppermute | solution.py:809
  21.2 0.0 collective-permute-done.2.x1_ref
  21.2 1.3 %shard_map.113 = (f32[240,128]{1,0:T(8,128)S(1)}, f32[240,128]{1,0:T(8,128)S(1)}, f32[256,128]{1,0:T(8,128)S(1)}) custom-call(f32[240,128]{1,0:T(8,128)S(1)} %bitcast.11, f32[240,128]{1,0:T(8,128)S(1)} %bitcast.16, f32[240,128]{1,0:T(8,128)S(1)} %bitcast.28, f32[240,128]{1,0:T(8,128)S(1)} %bitcast.31, f32[240,128]{1,0:T(8,128)S(1)} %bitcast.21, ...), custom_call_target="tpu_custom_call" | custom-call | flops 4194304 | bytes 2097152 | tf_op jit(solution)/shard_map/pallas_call | solution.py:766
  22.5 0.0 collective-permute-done.y1_ref
  22.5 0.9 %collective-permute-done.1.y2_ref = f32[296,128]{1,0:T(8,128)S(1)} collective-permute-done((f32[296,128]{1,0:T(8,128)S(1)}, f32[296,128]{1,0:T(8,128)S(1)}, u32[]{:S(2)}, u32[]{:S(2)}) %collective-permute-start.1) | collective-permute-done | bytes 151584 | tf_op jit(solution)/shard_map/ppermute | solution.py:811
  23.4 0.0 all-to-all-done.ga_ref
  23.4 1.5 %collective-permute-start.4 = (f32[16,1,6528]{2,1,0:T(1,128)S(1)}, f32[16,1,6528]{2,1,0:T(1,128)S(1)}, u32[]{:S(2)}, u32[]{:S(2)}) collective-permute-start(f32[16,1,6528]{2,1,0:T(1,128)S(1)} %all-to-all-done.ga_ref), channel_id=1, source_target_pairs={{0,1},{1,0},{2,3},{3,2},{4,5},{5,4},{6,7},{7,6},{8,9},{9,8},{10,11... | collective-permute-start | bytes 1253384 | tf_op jit(solution)/shard_map/ppermute | solution.py:820
  24.9 1.0 %shard_map.114 = (f32[240,128]{1,0:T(8,128)}, f32[240,128]{1,0:T(8,128)S(1)}, f32[1664,128]{1,0:T(8,128)S(1)}, f32[80,128]{1,0:T(8,128)S(1)}) custom-call(f32[240,128]{1,0:T(8,128)S(1)} %bitcast.12, f32[240,128]{1,0:T(8,128)S(1)} %bitcast.17, f32[240,128]{1,0:T(8,128)S(1)} %bitcast.29, f32[240,128]{1,0:T(8,128)S(1)} %bitcast.32, s32[8,128]{1,0:T(8,128)S(1)} %copy-done.6, ...), custom_call_target="tpu_custom_call" | custom-call | flops 4194304 | bytes 2097152 | tf_op jit(solution)/shard_map/pallas_call | solution.py:766
  25.9 0.4 %collective-permute-done.4.gb_ref = f32[16,1,6528]{2,1,0:T(1,128)S(1)} collective-permute-done((f32[16,1,6528]{2,1,0:T(1,128)S(1)}, f32[16,1,6528]{2,1,0:T(1,128)S(1)}, u32[]{:S(2)}, u32[]{:S(2)}) %collective-permute-start.4) | collective-permute-done | bytes 417824 | tf_op jit(solution)/shard_map/ppermute | solution.py:820
  26.3 3.0 %shard_map.115 = (f32[240,128]{1,0:T(8,128)}, f32[240,128]{1,0:T(8,128)}, f32[8,128]{1,0:T(8,128)}) custom-call(f32[240,128]{1,0:T(8,128)S(1)} %bitcast.13, f32[240,128]{1,0:T(8,128)S(1)} %bitcast.18, f32[240,128]{1,0:T(8,128)S(1)} %bitcast.22, f32[240,128]{1,0:T(8,128)S(1)} %bitcast.26, f32[16,1,6528]{2,1,0:T(1,128)S(1)} %all-to-all-done.ga_ref, ...), custom_call_target="tpu_custom_call" | custom-call | flops 8388608 | bytes 4194304 | tf_op jit(solution)/shard_map/pallas_call | solution.py:766
Async XLA Ops:
  2.7 6.9 %copy-start = (f32[30,8,128]{2,1,0:T(8,128)S(1)}, f32[30,8,128]{2,1,0:T(8,128)}, u32[]{:S(2)}) copy-start(f32[30,8,128]{2,1,0:T(8,128)} %param.8) | copy-start | bytes 368644
  2.8 6.9 %copy-start.1 = (f32[30,8,128]{2,1,0:T(8,128)S(1)}, f32[30,8,128]{2,1,0:T(8,128)}, u32[]{:S(2)}) copy-start(f32[30,8,128]{2,1,0:T(8,128)} %param.9) | copy-start | bytes 368644
  2.8 6.9 %copy-start.2 = (f32[30,8,128]{2,1,0:T(8,128)S(1)}, f32[30,8,128]{2,1,0:T(8,128)}, u32[]{:S(2)}) copy-start(f32[30,8,128]{2,1,0:T(8,128)} %param.12) | copy-start | bytes 368644
  2.8 6.9 %copy-start.3 = (f32[30,8,128]{2,1,0:T(8,128)S(1)}, f32[30,8,128]{2,1,0:T(8,128)}, u32[]{:S(2)}) copy-start(f32[30,8,128]{2,1,0:T(8,128)} %param.13) | copy-start | bytes 368644
  2.8 6.9 %copy-start.4 = (f32[30,8,128]{2,1,0:T(8,128)S(1)}, f32[30,8,128]{2,1,0:T(8,128)}, u32[]{:S(2)}) copy-start(f32[30,8,128]{2,1,0:T(8,128)} %param.10) | copy-start | bytes 368644
  2.8 6.9 %copy-start.5 = (f32[30,8,128]{2,1,0:T(8,128)S(1)}, f32[30,8,128]{2,1,0:T(8,128)}, u32[]{:S(2)}) copy-start(f32[30,8,128]{2,1,0:T(8,128)} %param.14) | copy-start | bytes 368644
  2.8 6.8 %copy-start.6 = (s32[8,128]{1,0:T(8,128)S(1)}, s32[8,128]{1,0:T(8,128)}, u32[]{:S(2)}) copy-start(s32[8,128]{1,0:T(8,128)} %count_ref.5) | copy-start | bytes 12292
  2.8 20.6 %all-to-all-start = ((f32[16,1,6528]{2,1,0:T(1,128)}), f32[16,1,6528]{2,1,0:T(1,128)S(1)}, u32[]{:S(2)}, u32[]{:S(2)}) async-start(f32[16,1,6528]{2,1,0:T(1,128)} %shard_map.111), calls=%async_computation | async-start | bytes 835584 | tf_op jit(solution)/shard_map/all_to_all | solution.py:807
  10.0 12.5 %collective-permute-start = (f32[296,128]{1,0:T(8,128)S(1)}, f32[296,128]{1,0:T(8,128)S(1)}, u32[]{:S(2)}, u32[]{:S(2)}) collective-permute-start(f32[296,128]{1,0:T(8,128)S(1)} %get-tuple-element.21), channel_id=1, source_target_pairs={{0,4},{1,5},{2,6},{3,7},{4,0},{5,1},{6,2},{7,3},{8,12},{9,13},{10,... | collective-permute-start | bytes 454664 | tf_op jit(solution)/shard_map/ppermute | solution.py:810
  10.3 13.1 %collective-permute-start.1 = (f32[296,128]{1,0:T(8,128)S(1)}, f32[296,128]{1,0:T(8,128)S(1)}, u32[]{:S(2)}, u32[]{:S(2)}) collective-permute-start(f32[296,128]{1,0:T(8,128)S(1)} %get-tuple-element.22), channel_id=1, source_target_pairs={{4,8},{5,9},{6,10},{7,11},{8,4},{9,5},{10,6},{11,7},{12,16},{13,17... | collective-permute-start | bytes 454664 | tf_op jit(solution)/shard_map/ppermute | solution.py:811
  14.3 6.9 %collective-permute-start.3 = (f32[72,128]{1,0:T(8,128)S(1)}, f32[72,128]{1,0:T(8,128)S(1)}, u32[]{:S(2)}, u32[]{:S(2)}) collective-permute-start(f32[72,128]{1,0:T(8,128)S(1)} %get-tuple-element.23), channel_id=1, source_target_pairs={{1,2},{2,1},{5,6},{6,5},{9,10},{10,9},{13,14},{14,13},{17,18},{18,... | collective-permute-start | bytes 110600 | tf_op jit(solution)/shard_map/ppermute | solution.py:809
  19.1 2.1 %collective-permute-start.2 = (f32[72,128]{1,0:T(8,128)S(1)}, f32[72,128]{1,0:T(8,128)S(1)}, u32[]{:S(2)}, u32[]{:S(2)}) collective-permute-start(f32[72,128]{1,0:T(8,128)S(1)} %get-tuple-element.23), channel_id=1, source_target_pairs={{0,1},{1,0},{2,3},{3,2},{4,5},{5,4},{6,7},{7,6},{8,9},{9,8},{10,11... | collective-permute-start | bytes 110600 | tf_op jit(solution)/shard_map/ppermute | solution.py:808
  23.4 2.8 %collective-permute-start.4 = (f32[16,1,6528]{2,1,0:T(1,128)S(1)}, f32[16,1,6528]{2,1,0:T(1,128)S(1)}, u32[]{:S(2)}, u32[]{:S(2)}) collective-permute-start(f32[16,1,6528]{2,1,0:T(1,128)S(1)} %all-to-all-done.ga_ref), channel_id=1, source_target_pairs={{0,1},{1,0},{2,3},{3,2},{4,5},{5,4},{6,7},{7,6},{8,9},{9,8},{10,11... | collective-permute-start | bytes 1253384 | tf_op jit(solution)/shard_map/ppermute | solution.py:820

commit v7 on v6

--- a/solution.py
+++ b/solution.py
@@ -779,6 +779,7 @@
     levels = u.shape[0]
     groups = group_count(levels)
     flat = (levels * SUB, LANES)
+    room = (groups * SUB * SUB, LANES)
     u, v, t, su, sv, st = (field.reshape(flat) for field in (u, v, t, su, sv, st))
     peers = ny * nx // 2
     row_packet = ((N_SLOTS * groups + 1) * SUB, LANES)
@@ -811,7 +812,7 @@
     y2 = lax.ppermute(y2, axes, swaps(shape, "y", 1))
     dtx, du_t, edge = call(
         functools.partial(column_kernel, levels),
-        [flat, flat, (len(FLOW_FIELDS) * SUB * SUB, LANES)],
+        [room, room, (len(FLOW_FIELDS) * SUB * SUB, LANES)],
         (u, v, t, st, su, sv, count, x1, x2),
         flops=1 << 22,
         size=1 << 21,
@@ -820,9 +821,9 @@
     gb = lax.ppermute(ga, axes, swaps(shape, "x", 0))
     dt, dv_t, made, outer = call(
         functools.partial(row_kernel, levels, ny),
-        [flat, flat, (groups * MADE_ROWS * SUB, LANES), (len(OUTER_ROWS) * SUB, LANES)],
+        [flat, room, (groups * MADE_ROWS * SUB, LANES), (len(OUTER_ROWS) * SUB, LANES)],
         (u, v, t, st, count, y1, y2, dtx),
-        scratch=(pltpu.VMEM(flat, jnp.float32), pltpu.SemaphoreType.DMA((groups,))),
+        scratch=(pltpu.VMEM(room, jnp.float32), pltpu.SemaphoreType.DMA((groups,))),
         flops=1 << 22,
         size=1 << 21,
         far_out=(0,),
@@ -835,7 +836,7 @@
         (u, v, su, sv, ga, gb, y1, y2, edge, outer, made, du_t, dv_t),
         far_out=(0, 1, 2),
         scratch=(grid, faces, residuals)
-        + tuple(pltpu.VMEM(shape, jnp.float32) for shape in (tile, flat, flat))
+        + tuple(pltpu.VMEM(shape, jnp.float32) for shape in (tile, room, room))
         + (pltpu.SemaphoreType.DMA((2 * groups + 1,)),),
         flops=1 << 23,
         size=1 << 22,

time: 29.5 us -> 29.5 us (level)
  no operation moved by 1% of the time
where the time goes in v7:
time: 29.5 us; the launch traced here: 29.3 us
  starting transfers between devices  17.4 us (59%)
  Pallas kernels  7.72 us (26%)
  waiting for transfers between devices  3.32 us (11%)
  between operations  0.8 us (3%)
    pallas_call x5, Pallas kernels, call(): pl.pallas_call(kernel, out_shape=outs, in_specs=[far if far_in else near]...  7.72 us
    all_to_all x1, starting transfers between devices, on_device(): ga = lax.all_to_all(chunks, ('ty', 'y'), 0, 0)  6.78 us
    ppermute x1, starting transfers between devices, on_device(): x2 = lax.ppermute(xp, axes, swaps(shape, 'x', 1))  4.77 us
    ppermute x1, starting transfers between devices, on_device(): y2 = lax.ppermute(y2, axes, swaps(shape, 'y', 1))  3.98 us
    ppermute x1, waiting for transfers between devices, on_device(): x2 = lax.ppermute(xp, axes, swaps(shape, 'x', 1))  2.02 us
    ppermute x1, starting transfers between devices, on_device(): gb = lax.ppermute(ga, axes, swaps(shape, 'x', 0))  1.45 us
    ppermute x1, waiting for transfers between devices, on_device(): y2 = lax.ppermute(y2, axes, swaps(shape, 'y', 1))  0.93 us
  transfers between devices with their start and end apart: 6, of which 3 were waited for; matrix products, arithmetic and copies ran while one was open for 0% of the time, Pallas kernels for 9%

profile of v7, /device:TPU:11, one launch (start us, length us, event | category | flops | bytes accessed | tf_op | source)
XLA Modules:
  0.0 29.3 jit_solution(17306458225960085780)
XLA Ops:
  0.6 2.1 %shard_map.111 = f32[16,1,6528]{2,1,0:T(1,128)} custom-call(f32[240,128]{1,0:T(8,128)} %bitcast.9, f32[240,128]{1,0:T(8,128)} %bitcast.14, f32[240,128]{1,0:T(8,128)} %bitcast.19, f32[240,128]{1,0:T(8,128)} %bitcast.23, s32[8,128]{1,0:T(8,128)} %count_ref.5, f32[8,128]{1,0:T(8,128)} %elev_hbm.1), custom_call_target="tpu_custom_call" | custom-call | flops 1048576 | bytes 2097152 | tf_op jit(solution)/shard_map/pallas_call | solution.py:766
  2.7 0.0 copy-start
  2.8 0.0 copy-start.1
  2.8 0.0 copy-start.2
  2.8 0.0 copy-start.3
  2.8 0.0 copy-start.4
  2.8 0.0 copy-start.5
  2.8 0.0 copy-start.6
  2.8 6.8 %all-to-all-start = ((f32[16,1,6528]{2,1,0:T(1,128)}), f32[16,1,6528]{2,1,0:T(1,128)S(1)}, u32[]{:S(2)}, u32[]{:S(2)}) async-start(f32[16,1,6528]{2,1,0:T(1,128)} %shard_map.111), calls=%async_computation | async-start | bytes 835584 | tf_op jit(solution)/shard_map/all_to_all | solution.py:808
  9.6 0.0 copy-done
  9.6 0.0 copy-done.1
  9.6 0.0 copy-done.2
  9.6 0.0 copy-done.3
  9.6 0.0 copy-done.4
  9.7 0.0 copy-done.5
  9.7 0.0 copy-done.6
  9.7 0.3 %shard_map.112 = (f32[296,128]{1,0:T(8,128)S(1)}, f32[296,128]{1,0:T(8,128)S(1)}, f32[72,128]{1,0:T(8,128)S(1)}) custom-call(f32[240,128]{1,0:T(8,128)S(1)} %bitcast.10, f32[240,128]{1,0:T(8,128)S(1)} %bitcast.15, f32[240,128]{1,0:T(8,128)S(1)} %bitcast.27, f32[240,128]{1,0:T(8,128)S(1)} %bitcast.20, f32[240,128]{1,0:T(8,128)S(1)} %bitcast.24, ...), custom_call_target="tpu_custom_call" | custom-call | flops 1048576 | bytes 2097152 | tf_op jit(solution)/shard_map/pallas_call | solution.py:766
  10.0 0.3 %collective-permute-start = (f32[296,128]{1,0:T(8,128)S(1)}, f32[296,128]{1,0:T(8,128)S(1)}, u32[]{:S(2)}, u32[]{:S(2)}) collective-permute-start(f32[296,128]{1,0:T(8,128)S(1)} %get-tuple-element.21), channel_id=1, source_target_pairs={{0,4},{1,5},{2,6},{3,7},{4,0},{5,1},{6,2},{7,3},{8,12},{9,13},{10,... | collective-permute-start | bytes 454664 | tf_op jit(solution)/shard_map/ppermute | solution.py:811
  10.3 4.0 %collective-permute-start.1 = (f32[296,128]{1,0:T(8,128)S(1)}, f32[296,128]{1,0:T(8,128)S(1)}, u32[]{:S(2)}, u32[]{:S(2)}) collective-permute-start(f32[296,128]{1,0:T(8,128)S(1)} %get-tuple-element.22), channel_id=1, source_target_pairs={{4,8},{5,9},{6,10},{7,11},{8,4},{9,5},{10,6},{11,7},{12,16},{13,17... | collective-permute-start | bytes 454664 | tf_op jit(solution)/shard_map/ppermute | solution.py:812
  14.3 4.8 %collective-permute-start.3 = (f32[72,128]{1,0:T(8,128)S(1)}, f32[72,128]{1,0:T(8,128)S(1)}, u32[]{:S(2)}, u32[]{:S(2)}) collective-permute-start(f32[72,128]{1,0:T(8,128)S(1)} %get-tuple-element.23), channel_id=1, source_target_pairs={{1,2},{2,1},{5,6},{6,5},{9,10},{10,9},{13,14},{14,13},{17,18},{18,... | collective-permute-start | bytes 110600 | tf_op jit(solution)/shard_map/ppermute | solution.py:810
  19.1 0.1 collective-permute-start.2
  19.2 2.0 %collective-permute-done.3.x2_ref = f32[72,128]{1,0:T(8,128)S(1)} collective-permute-done((f32[72,128]{1,0:T(8,128)S(1)}, f32[72,128]{1,0:T(8,128)S(1)}, u32[]{:S(2)}, u32[]{:S(2)}) %collective-permute-start.3) | collective-permute-done | bytes 36896 | tf_op jit(solution)/shard_map/ppermute | solution.py:810
  21.2 0.0 collective-permute-done.2.x1_ref
  21.2 1.3 %shard_map.113 = (f32[256,128]{1,0:T(8,128)S(1)}, f32[256,128]{1,0:T(8,128)S(1)}, f32[256,128]{1,0:T(8,128)S(1)}) custom-call(f32[240,128]{1,0:T(8,128)S(1)} %bitcast.11, f32[240,128]{1,0:T(8,128)S(1)} %bitcast.16, f32[240,128]{1,0:T(8,128)S(1)} %bitcast.28, f32[240,128]{1,0:T(8,128)S(1)} %bitcast.31, f32[240,128]{1,0:T(8,128)S(1)} %bitcast.21, ...), custom_call_target="tpu_custom_call" | custom-call | flops 4194304 | bytes 2097152 | tf_op jit(solution)/shard_map/pallas_call | solution.py:766
  22.5 0.0 collective-permute-done.y1_ref
  22.5 0.9 %collective-permute-done.1.y2_ref = f32[296,128]{1,0:T(8,128)S(1)} collective-permute-done((f32[296,128]{1,0:T(8,128)S(1)}, f32[296,128]{1,0:T(8,128)S(1)}, u32[]{:S(2)}, u32[]{:S(2)}) %collective-permute-start.1) | collective-permute-done | bytes 151584 | tf_op jit(solution)/shard_map/ppermute | solution.py:812
  23.4 0.0 all-to-all-done.ga_ref
  23.4 1.5 %collective-permute-start.4 = (f32[16,1,6528]{2,1,0:T(1,128)S(1)}, f32[16,1,6528]{2,1,0:T(1,128)S(1)}, u32[]{:S(2)}, u32[]{:S(2)}) collective-permute-start(f32[16,1,6528]{2,1,0:T(1,128)S(1)} %all-to-all-done.ga_ref), channel_id=1, source_target_pairs={{0,1},{1,0},{2,3},{3,2},{4,5},{5,4},{6,7},{7,6},{8,9},{9,8},{10,11... | collective-permute-start | bytes 1253384 | tf_op jit(solution)/shard_map/ppermute | solution.py:821
  24.9 1.0 %shard_map.114 = (f32[240,128]{1,0:T(8,128)}, f32[256,128]{1,0:T(8,128)S(1)}, f32[1664,128]{1,0:T(8,128)S(1)}, f32[80,128]{1,0:T(8,128)S(1)}) custom-call(f32[240,128]{1,0:T(8,128)S(1)} %bitcast.12, f32[240,128]{1,0:T(8,128)S(1)} %bitcast.17, f32[240,128]{1,0:T(8,128)S(1)} %bitcast.29, f32[240,128]{1,0:T(8,128)S(1)} %bitcast.32, s32[8,128]{1,0:T(8,128)S(1)} %copy-done.6, ...), custom_call_target="tpu_custom_call" | custom-call | flops 4194304 | bytes 2097152 | tf_op jit(solution)/shard_map/pallas_call | solution.py:766
  25.9 0.4 %collective-permute-done.4.gb_ref = f32[16,1,6528]{2,1,0:T(1,128)S(1)} collective-permute-done((f32[16,1,6528]{2,1,0:T(1,128)S(1)}, f32[16,1,6528]{2,1,0:T(1,128)S(1)}, u32[]{:S(2)}, u32[]{:S(2)}) %collective-permute-start.4) | collective-permute-done | bytes 417824 | tf_op jit(solution)/shard_map/ppermute | solution.py:821
  26.3 3.0 %shard_map.115 = (f32[240,128]{1,0:T(8,128)}, f32[240,128]{1,0:T(8,128)}, f32[8,128]{1,0:T(8,128)}) custom-call(f32[240,128]{1,0:T(8,128)S(1)} %bitcast.13, f32[240,128]{1,0:T(8,128)S(1)} %bitcast.18, f32[240,128]{1,0:T(8,128)S(1)} %bitcast.22, f32[240,128]{1,0:T(8,128)S(1)} %bitcast.26, f32[16,1,6528]{2,1,0:T(1,128)S(1)} %all-to-all-done.ga_ref, ...), custom_call_target="tpu_custom_call" | custom-call | flops 8388608 | bytes 4194304 | tf_op jit(solution)/shard_map/pallas_call | solution.py:766
Async XLA Ops:
  2.7 6.9 %copy-start = (f32[30,8,128]{2,1,0:T(8,128)S(1)}, f32[30,8,128]{2,1,0:T(8,128)}, u32[]{:S(2)}) copy-start(f32[30,8,128]{2,1,0:T(8,128)} %param.8) | copy-start | bytes 368644
  2.8 6.9 %copy-start.1 = (f32[30,8,128]{2,1,0:T(8,128)S(1)}, f32[30,8,128]{2,1,0:T(8,128)}, u32[]{:S(2)}) copy-start(f32[30,8,128]{2,1,0:T(8,128)} %param.9) | copy-start | bytes 368644
  2.8 6.9 %copy-start.2 = (f32[30,8,128]{2,1,0:T(8,128)S(1)}, f32[30,8,128]{2,1,0:T(8,128)}, u32[]{:S(2)}) copy-start(f32[30,8,128]{2,1,0:T(8,128)} %param.12) | copy-start | bytes 368644
  2.8 6.9 %copy-start.3 = (f32[30,8,128]{2,1,0:T(8,128)S(1)}, f32[30,8,128]{2,1,0:T(8,128)}, u32[]{:S(2)}) copy-start(f32[30,8,128]{2,1,0:T(8,128)} %param.13) | copy-start | bytes 368644
  2.8 6.9 %copy-start.4 = (f32[30,8,128]{2,1,0:T(8,128)S(1)}, f32[30,8,128]{2,1,0:T(8,128)}, u32[]{:S(2)}) copy-start(f32[30,8,128]{2,1,0:T(8,128)} %param.10) | copy-start | bytes 368644
  2.8 6.9 %copy-start.5 = (f32[30,8,128]{2,1,0:T(8,128)S(1)}, f32[30,8,128]{2,1,0:T(8,128)}, u32[]{:S(2)}) copy-start(f32[30,8,128]{2,1,0:T(8,128)} %param.14) | copy-start | bytes 368644
  2.8 6.8 %copy-start.6 = (s32[8,128]{1,0:T(8,128)S(1)}, s32[8,128]{1,0:T(8,128)}, u32[]{:S(2)}) copy-start(s32[8,128]{1,0:T(8,128)} %count_ref.5) | copy-start | bytes 12292
  2.8 20.6 %all-to-all-start = ((f32[16,1,6528]{2,1,0:T(1,128)}), f32[16,1,6528]{2,1,0:T(1,128)S(1)}, u32[]{:S(2)}, u32[]{:S(2)}) async-start(f32[16,1,6528]{2,1,0:T(1,128)} %shard_map.111), calls=%async_computation | async-start | bytes 835584 | tf_op jit(solution)/shard_map/all_to_all | solution.py:808
  10.0 12.5 %collective-permute-start = (f32[296,128]{1,0:T(8,128)S(1)}, f32[296,128]{1,0:T(8,128)S(1)}, u32[]{:S(2)}, u32[]{:S(2)}) collective-permute-start(f32[296,128]{1,0:T(8,128)S(1)} %get-tuple-element.21), channel_id=1, source_target_pairs={{0,4},{1,5},{2,6},{3,7},{4,0},{5,1},{6,2},{7,3},{8,12},{9,13},{10,... | collective-permute-start | bytes 454664 | tf_op jit(solution)/shard_map/ppermute | solution.py:811
  10.3 13.1 %collective-permute-start.1 = (f32[296,128]{1,0:T(8,128)S(1)}, f32[296,128]{1,0:T(8,128)S(1)}, u32[]{:S(2)}, u32[]{:S(2)}) collective-permute-start(f32[296,128]{1,0:T(8,128)S(1)} %get-tuple-element.22), channel_id=1, source_target_pairs={{4,8},{5,9},{6,10},{7,11},{8,4},{9,5},{10,6},{11,7},{12,16},{13,17... | collective-permute-start | bytes 454664 | tf_op jit(solution)/shard_map/ppermute | solution.py:812
  14.3 6.9 %collective-permute-start.3 = (f32[72,128]{1,0:T(8,128)S(1)}, f32[72,128]{1,0:T(8,128)S(1)}, u32[]{:S(2)}, u32[]{:S(2)}) collective-permute-start(f32[72,128]{1,0:T(8,128)S(1)} %get-tuple-element.23), channel_id=1, source_target_pairs={{1,2},{2,1},{5,6},{6,5},{9,10},{10,9},{13,14},{14,13},{17,18},{18,... | collective-permute-start | bytes 110600 | tf_op jit(solution)/shard_map/ppermute | solution.py:810
  19.1 2.1 %collective-permute-start.2 = (f32[72,128]{1,0:T(8,128)S(1)}, f32[72,128]{1,0:T(8,128)S(1)}, u32[]{:S(2)}, u32[]{:S(2)}) collective-permute-start(f32[72,128]{1,0:T(8,128)S(1)} %get-tuple-element.23), channel_id=1, source_target_pairs={{0,1},{1,0},{2,3},{3,2},{4,5},{5,4},{6,7},{7,6},{8,9},{9,8},{10,11... | collective-permute-start | bytes 110600 | tf_op jit(solution)/shard_map/ppermute | solution.py:809
  23.4 2.8 %collective-permute-start.4 = (f32[16,1,6528]{2,1,0:T(1,128)S(1)}, f32[16,1,6528]{2,1,0:T(1,128)S(1)}, u32[]{:S(2)}, u32[]{:S(2)}) collective-permute-start(f32[16,1,6528]{2,1,0:T(1,128)S(1)} %all-to-all-done.ga_ref), channel_id=1, source_target_pairs={{0,1},{1,0},{2,3},{3,2},{4,5},{5,4},{6,7},{7,6},{8,9},{9,8},{10,11... | collective-permute-start | bytes 1253384 | tf_op jit(solution)/shard_map/ppermute | solution.py:821

commit v8 on v7

--- a/solution.py
+++ b/solution.py
@@ -549,6 +549,10 @@
 
         def body(j, carry):
             r = get(r_ref, j)
+            if k + 1 == ITERS:
+                half = get(face_ref.at[0], j) * west_of(r) + get(face_ref.at[1], j) * south_of(r_ref, j, r)
+                image = r * get(face_ref.at[6], j) - (half + half)
+                return gathered(carry[0], r * r), gathered(carry[1], r * image)
             image = r * get(face_ref.at[6], j) - get(face_ref.at[0], j) * west_of(r) - get(face_ref.at[2], j) * east_of(r)
             image = image - get(face_ref.at[1], j) * south_of(r_ref, j, r)
             image = image - get(face_ref.at[3], j) * north_of(r_ref, j, r)

time: 29.5 us -> 29.5 us (level)
  no operation moved by 1% of the time
where the time goes in v8:
time: 29.5 us; the launch traced here: 29.3 us
  starting transfers between devices  17.4 us (59%)
  Pallas kernels  7.7 us (26%)
  waiting for transfers between devices  3.32 us (11%)
  between operations  0.8 us (3%)
    pallas_call x5, Pallas kernels, call(): pl.pallas_call(kernel, out_shape=outs, in_specs=[far if far_in else near]...  7.7 us
    all_to_all x1, starting transfers between devices, on_device(): ga = lax.all_to_all(chunks, ('ty', 'y'), 0, 0)  6.78 us
    ppermute x1, starting transfers between devices, on_device(): x2 = lax.ppermute(xp, axes, swaps(shape, 'x', 1))  4.77 us
    ppermute x1, starting transfers between devices, on_device(): y2 = lax.ppermute(y2, axes, swaps(shape, 'y', 1))  3.98 us
    ppermute x1, waiting for transfers between devices, on_device(): x2 = lax.ppermute(xp, axes, swaps(shape, 'x', 1))  2.02 us
    ppermute x1, starting transfers between devices, on_device(): gb = lax.ppermute(ga, axes, swaps(shape, 'x', 0))  1.45 us
    ppermute x1, waiting for transfers between devices, on_device(): y2 = lax.ppermute(y2, axes, swaps(shape, 'y', 1))  0.93 us
  transfers between devices with their start and end apart: 6, of which 3 were waited for; matrix products, arithmetic and copies ran while one was open for 0% of the time, Pallas kernels for 9%

profile of v8, /device:TPU:11, one launch (start us, length us, event | category | flops | bytes accessed | tf_op | source)
XLA Modules:
  0.0 29.3 jit_solution(15449946428137416930)
XLA Ops:
  0.6 2.1 %shard_map.111 = f32[16,1,6528]{2,1,0:T(1,128)} custom-call(f32[240,128]{1,0:T(8,128)} %bitcast.9, f32[240,128]{1,0:T(8,128)} %bitcast.14, f32[240,128]{1,0:T(8,128)} %bitcast.19, f32[240,128]{1,0:T(8,128)} %bitcast.23, s32[8,128]{1,0:T(8,128)} %count_ref.5, f32[8,128]{1,0:T(8,128)} %elev_hbm.1), custom_call_target="tpu_custom_call" | custom-call | flops 1048576 | bytes 2097152 | tf_op jit(solution)/shard_map/pallas_call | solution.py:770
  2.7 0.0 copy-start
  2.8 0.0 copy-start.1
  2.8 0.0 copy-start.2
  2.8 0.0 copy-start.3
  2.8 0.0 copy-start.4
  2.8 0.0 copy-start.5
  2.8 0.0 copy-start.6
  2.8 6.8 %all-to-all-start = ((f32[16,1,6528]{2,1,0:T(1,128)}), f32[16,1,6528]{2,1,0:T(1,128)S(1)}, u32[]{:S(2)}, u32[]{:S(2)}) async-start(f32[16,1,6528]{2,1,0:T(1,128)} %shard_map.111), calls=%async_computation | async-start | bytes 835584 | tf_op jit(solution)/shard_map/all_to_all | solution.py:812
  9.6 0.0 copy-done
  9.6 0.0 copy-done.1
  9.6 0.0 copy-done.2
  9.6 0.0 copy-done.3
  9.6 0.0 copy-done.4
  9.7 0.0 copy-done.5
  9.7 0.0 copy-done.6
  9.7 0.3 %shard_map.112 = (f32[296,128]{1,0:T(8,128)S(1)}, f32[296,128]{1,0:T(8,128)S(1)}, f32[72,128]{1,0:T(8,128)S(1)}) custom-call(f32[240,128]{1,0:T(8,128)S(1)} %bitcast.10, f32[240,128]{1,0:T(8,128)S(1)} %bitcast.15, f32[240,128]{1,0:T(8,128)S(1)} %bitcast.27, f32[240,128]{1,0:T(8,128)S(1)} %bitcast.20, f32[240,128]{1,0:T(8,128)S(1)} %bitcast.24, ...), custom_call_target="tpu_custom_call" | custom-call | flops 1048576 | bytes 2097152 | tf_op jit(solution)/shard_map/pallas_call | solution.py:770
  10.0 0.3 %collective-permute-start = (f32[296,128]{1,0:T(8,128)S(1)}, f32[296,128]{1,0:T(8,128)S(1)}, u32[]{:S(2)}, u32[]{:S(2)}) collective-permute-start(f32[296,128]{1,0:T(8,128)S(1)} %get-tuple-element.21), channel_id=1, source_target_pairs={{0,4},{1,5},{2,6},{3,7},{4,0},{5,1},{6,2},{7,3},{8,12},{9,13},{10,... | collective-permute-start | bytes 454664 | tf_op jit(solution)/shard_map/ppermute | solution.py:815
  10.3 4.0 %collective-permute-start.1 = (f32[296,128]{1,0:T(8,128)S(1)}, f32[296,128]{1,0:T(8,128)S(1)}, u32[]{:S(2)}, u32[]{:S(2)}) collective-permute-start(f32[296,128]{1,0:T(8,128)S(1)} %get-tuple-element.22), channel_id=1, source_target_pairs={{4,8},{5,9},{6,10},{7,11},{8,4},{9,5},{10,6},{11,7},{12,16},{13,17... | collective-permute-start | bytes 454664 | tf_op jit(solution)/shard_map/ppermute | solution.py:816
  14.3 4.8 %collective-permute-start.3 = (f32[72,128]{1,0:T(8,128)S(1)}, f32[72,128]{1,0:T(8,128)S(1)}, u32[]{:S(2)}, u32[]{:S(2)}) collective-permute-start(f32[72,128]{1,0:T(8,128)S(1)} %get-tuple-element.23), channel_id=1, source_target_pairs={{1,2},{2,1},{5,6},{6,5},{9,10},{10,9},{13,14},{14,13},{17,18},{18,... | collective-permute-start | bytes 110600 | tf_op jit(solution)/shard_map/ppermute | solution.py:814
  19.1 0.1 collective-permute-start.2
  19.2 2.0 %collective-permute-done.3.x2_ref = f32[72,128]{1,0:T(8,128)S(1)} collective-permute-done((f32[72,128]{1,0:T(8,128)S(1)}, f32[72,128]{1,0:T(8,128)S(1)}, u32[]{:S(2)}, u32[]{:S(2)}) %collective-permute-start.3) | collective-permute-done | bytes 36896 | tf_op jit(solution)/shard_map/ppermute | solution.py:814
  21.2 0.0 collective-permute-done.2.x1_ref
  21.2 1.3 %shard_map.113 = (f32[256,128]{1,0:T(8,128)S(1)}, f32[256,128]{1,0:T(8,128)S(1)}, f32[256,128]{1,0:T(8,128)S(1)}) custom-call(f32[240,128]{1,0:T(8,128)S(1)} %bitcast.11, f32[240,128]{1,0:T(8,128)S(1)} %bitcast.16, f32[240,128]{1,0:T(8,128)S(1)} %bitcast.28, f32[240,128]{1,0:T(8,128)S(1)} %bitcast.31, f32[240,128]{1,0:T(8,128)S(1)} %bitcast.21, ...), custom_call_target="tpu_custom_call" | custom-call | flops 4194304 | bytes 2097152 | tf_op jit(solution)/shard_map/pallas_call | solution.py:770
  22.5 0.0 collective-permute-done.y1_ref
  22.5 0.9 %collective-permute-done.1.y2_ref = f32[296,128]{1,0:T(8,128)S(1)} collective-permute-done((f32[296,128]{1,0:T(8,128)S(1)}, f32[296,128]{1,0:T(8,128)S(1)}, u32[]{:S(2)}, u32[]{:S(2)}) %collective-permute-start.1) | collective-permute-done | bytes 151584 | tf_op jit(solution)/shard_map/ppermute | solution.py:816
  23.4 0.0 all-to-all-done.ga_ref
  23.4 1.5 %collective-permute-start.4 = (f32[16,1,6528]{2,1,0:T(1,128)S(1)}, f32[16,1,6528]{2,1,0:T(1,128)S(1)}, u32[]{:S(2)}, u32[]{:S(2)}) collective-permute-start(f32[16,1,6528]{2,1,0:T(1,128)S(1)} %all-to-all-done.ga_ref), channel_id=1, source_target_pairs={{0,1},{1,0},{2,3},{3,2},{4,5},{5,4},{6,7},{7,6},{8,9},{9,8},{10,11... | collective-permute-start | bytes 1253384 | tf_op jit(solution)/shard_map/ppermute | solution.py:825
  24.9 1.0 %shard_map.114 = (f32[240,128]{1,0:T(8,128)}, f32[256,128]{1,0:T(8,128)S(1)}, f32[1664,128]{1,0:T(8,128)S(1)}, f32[80,128]{1,0:T(8,128)S(1)}) custom-call(f32[240,128]{1,0:T(8,128)S(1)} %bitcast.12, f32[240,128]{1,0:T(8,128)S(1)} %bitcast.17, f32[240,128]{1,0:T(8,128)S(1)} %bitcast.29, f32[240,128]{1,0:T(8,128)S(1)} %bitcast.32, s32[8,128]{1,0:T(8,128)S(1)} %copy-done.6, ...), custom_call_target="tpu_custom_call" | custom-call | flops 4194304 | bytes 2097152 | tf_op jit(solution)/shard_map/pallas_call | solution.py:770
  25.9 0.4 %collective-permute-done.4.gb_ref = f32[16,1,6528]{2,1,0:T(1,128)S(1)} collective-permute-done((f32[16,1,6528]{2,1,0:T(1,128)S(1)}, f32[16,1,6528]{2,1,0:T(1,128)S(1)}, u32[]{:S(2)}, u32[]{:S(2)}) %collective-permute-start.4) | collective-permute-done | bytes 417824 | tf_op jit(solution)/shard_map/ppermute | solution.py:825
  26.3 3.0 %shard_map.115 = (f32[240,128]{1,0:T(8,128)}, f32[240,128]{1,0:T(8,128)}, f32[8,128]{1,0:T(8,128)}) custom-call(f32[240,128]{1,0:T(8,128)S(1)} %bitcast.13, f32[240,128]{1,0:T(8,128)S(1)} %bitcast.18, f32[240,128]{1,0:T(8,128)S(1)} %bitcast.22, f32[240,128]{1,0:T(8,128)S(1)} %bitcast.26, f32[16,1,6528]{2,1,0:T(1,128)S(1)} %all-to-all-done.ga_ref, ...), custom_call_target="tpu_custom_call" | custom-call | flops 8388608 | bytes 4194304 | tf_op jit(solution)/shard_map/pallas_call | solution.py:770
Async XLA Ops:
  2.7 6.9 %copy-start = (f32[30,8,128]{2,1,0:T(8,128)S(1)}, f32[30,8,128]{2,1,0:T(8,128)}, u32[]{:S(2)}) copy-start(f32[30,8,128]{2,1,0:T(8,128)} %param.8) | copy-start | bytes 368644
  2.8 6.9 %copy-start.1 = (f32[30,8,128]{2,1,0:T(8,128)S(1)}, f32[30,8,128]{2,1,0:T(8,128)}, u32[]{:S(2)}) copy-start(f32[30,8,128]{2,1,0:T(8,128)} %param.9) | copy-start | bytes 368644
  2.8 6.9 %copy-start.2 = (f32[30,8,128]{2,1,0:T(8,128)S(1)}, f32[30,8,128]{2,1,0:T(8,128)}, u32[]{:S(2)}) copy-start(f32[30,8,128]{2,1,0:T(8,128)} %param.12) | copy-start | bytes 368644
  2.8 6.9 %copy-start.3 = (f32[30,8,128]{2,1,0:T(8,128)S(1)}, f32[30,8,128]{2,1,0:T(8,128)}, u32[]{:S(2)}) copy-start(f32[30,8,128]{2,1,0:T(8,128)} %param.13) | copy-start | bytes 368644
  2.8 6.9 %copy-start.4 = (f32[30,8,128]{2,1,0:T(8,128)S(1)}, f32[30,8,128]{2,1,0:T(8,128)}, u32[]{:S(2)}) copy-start(f32[30,8,128]{2,1,0:T(8,128)} %param.10) | copy-start | bytes 368644
  2.8 6.9 %copy-start.5 = (f32[30,8,128]{2,1,0:T(8,128)S(1)}, f32[30,8,128]{2,1,0:T(8,128)}, u32[]{:S(2)}) copy-start(f32[30,8,128]{2,1,0:T(8,128)} %param.14) | copy-start | bytes 368644
  2.8 6.8 %copy-start.6 = (s32[8,128]{1,0:T(8,128)S(1)}, s32[8,128]{1,0:T(8,128)}, u32[]{:S(2)}) copy-start(s32[8,128]{1,0:T(8,128)} %count_ref.5) | copy-start | bytes 12292
  2.8 20.6 %all-to-all-start = ((f32[16,1,6528]{2,1,0:T(1,128)}), f32[16,1,6528]{2,1,0:T(1,128)S(1)}, u32[]{:S(2)}, u32[]{:S(2)}) async-start(f32[16,1,6528]{2,1,0:T(1,128)} %shard_map.111), calls=%async_computation | async-start | bytes 835584 | tf_op jit(solution)/shard_map/all_to_all | solution.py:812
  10.0 12.5 %collective-permute-start = (f32[296,128]{1,0:T(8,128)S(1)}, f32[296,128]{1,0:T(8,128)S(1)}, u32[]{:S(2)}, u32[]{:S(2)}) collective-permute-start(f32[296,128]{1,0:T(8,128)S(1)} %get-tuple-element.21), channel_id=1, source_target_pairs={{0,4},{1,5},{2,6},{3,7},{4,0},{5,1},{6,2},{7,3},{8,12},{9,13},{10,... | collective-permute-start | bytes 454664 | tf_op jit(solution)/shard_map/ppermute | solution.py:815
  10.3 13.1 %collective-permute-start.1 = (f32[296,128]{1,0:T(8,128)S(1)}, f32[296,128]{1,0:T(8,128)S(1)}, u32[]{:S(2)}, u32[]{:S(2)}) collective-permute-start(f32[296,128]{1,0:T(8,128)S(1)} %get-tuple-element.22), channel_id=1, source_target_pairs={{4,8},{5,9},{6,10},{7,11},{8,4},{9,5},{10,6},{11,7},{12,16},{13,17... | collective-permute-start | bytes 454664 | tf_op jit(solution)/shard_map/ppermute | solution.py:816
  14.3 6.9 %collective-permute-start.3 = (f32[72,128]{1,0:T(8,128)S(1)}, f32[72,128]{1,0:T(8,128)S(1)}, u32[]{:S(2)}, u32[]{:S(2)}) collective-permute-start(f32[72,128]{1,0:T(8,128)S(1)} %get-tuple-element.23), channel_id=1, source_target_pairs={{1,2},{2,1},{5,6},{6,5},{9,10},{10,9},{13,14},{14,13},{17,18},{18,... | collective-permute-start | bytes 110600 | tf_op jit(solution)/shard_map/ppermute | solution.py:814
  19.1 2.1 %collective-permute-start.2 = (f32[72,128]{1,0:T(8,128)S(1)}, f32[72,128]{1,0:T(8,128)S(1)}, u32[]{:S(2)}, u32[]{:S(2)}) collective-permute-start(f32[72,128]{1,0:T(8,128)S(1)} %get-tuple-element.23), channel_id=1, source_target_pairs={{0,1},{1,0},{2,3},{3,2},{4,5},{5,4},{6,7},{7,6},{8,9},{9,8},{10,11... | collective-permute-start | bytes 110600 | tf_op jit(solution)/shard_map/ppermute | solution.py:813
  23.4 2.8 %collective-permute-start.4 = (f32[16,1,6528]{2,1,0:T(1,128)S(1)}, f32[16,1,6528]{2,1,0:T(1,128)S(1)}, u32[]{:S(2)}, u32[]{:S(2)}) collective-permute-start(f32[16,1,6528]{2,1,0:T(1,128)S(1)} %all-to-all-done.ga_ref), channel_id=1, source_target_pairs={{0,1},{1,0},{2,3},{3,2},{4,5},{5,4},{6,7},{7,6},{8,9},{9,8},{10,11... | collective-permute-start | bytes 1253384 | tf_op jit(solution)/shard_map/ppermute | solution.py:825

commit v9 on v7

--- a/solution.py
+++ b/solution.py
@@ -114,7 +114,7 @@
     groups = group_count(levels)
     lanes, rows = lane_ids(), row_ids()
     refs = {"u": u_ref, "v": v_ref, "su": su_ref, "sv": sv_ref}
-    for copy in copies[:4]:
+    for copy in copies:
         copy.wait()
     count = count_ref[...].astype(jnp.float32)
     zero = jnp.zeros((SUB, LANES), jnp.float32)
@@ -133,8 +133,6 @@
     col_u, col_v = ((col[0] + col[1]) + (col[2] + col[3]) for col in (col_u, col_v))
     load = elev_ref[...] + GRAVITY_DT * (at(col_u, 1) - col_u + roll_rows(col_v, -1) - col_v)
 
-    for copy in copies[4:]:
-        copy.wait()
     corners = [zero] * (len(CORNERS) // CORNERS_PER_ROW)
     for place, (name, row, column) in enumerate(CORNERS):
         n, base = place // CORNERS_PER_ROW, place % CORNERS_PER_ROW * SUB

time: 29.5 us -> 29.6 us (level)
  no operation moved by 1% of the time
where the time goes in v9:
time: 29.6 us; the launch traced here: 29.3 us
  starting transfers between devices  17.4 us (59%)
  Pallas kernels  7.73 us (26%)
  waiting for transfers between devices  3.32 us (11%)
  between operations  0.8 us (3%)
    pallas_call x5, Pallas kernels, call(): pl.pallas_call(kernel, out_shape=outs, in_specs=[far if far_in else near]...  7.73 us
    all_to_all x1, starting transfers between devices, on_device(): ga = lax.all_to_all(chunks, ('ty', 'y'), 0, 0)  6.78 us
    ppermute x1, starting transfers between devices, on_device(): x2 = lax.ppermute(xp, axes, swaps(shape, 'x', 1))  4.77 us
    ppermute x1, starting transfers between devices, on_device(): y2 = lax.ppermute(y2, axes, swaps(shape, 'y', 1))  3.98 us
    ppermute x1, waiting for transfers between devices, on_device(): x2 = lax.ppermute(xp, axes, swaps(shape, 'x', 1))  2.02 us
    ppermute x1, starting transfers between devices, on_device(): gb = lax.ppermute(ga, axes, swaps(shape, 'x', 0))  1.45 us
    ppermute x1, waiting for transfers between devices, on_device(): y2 = lax.ppermute(y2, axes, swaps(shape, 'y', 1))  0.93 us
  transfers between devices with their start and end apart: 6, of which 3 were waited for; matrix products, arithmetic and copies ran while one was open for 0% of the time, Pallas kernels for 9%

profile of v9, /device:TPU:11, one launch (start us, length us, event | category | flops | bytes accessed | tf_op | source)
XLA Modules:
  0.0 29.3 jit_solution(9710501207041543701)
XLA Ops:
  0.6 2.1 %shard_map.111 = f32[16,1,6528]{2,1,0:T(1,128)} custom-call(f32[240,128]{1,0:T(8,128)} %bitcast.9, f32[240,128]{1,0:T(8,128)} %bitcast.14, f32[240,128]{1,0:T(8,128)} %bitcast.19, f32[240,128]{1,0:T(8,128)} %bitcast.23, s32[8,128]{1,0:T(8,128)} %count_ref.5, f32[8,128]{1,0:T(8,128)} %elev_hbm.1), custom_call_target="tpu_custom_call" | custom-call | flops 1048576 | bytes 2097152 | tf_op jit(solution)/shard_map/pallas_call | solution.py:764
  2.8 0.0 copy-start
  2.8 0.0 copy-start.1
  2.8 0.0 copy-start.2
  2.8 0.0 copy-start.3
  2.8 0.0 copy-start.4
  2.8 0.0 copy-start.5
  2.8 0.0 copy-start.6
  2.8 6.8 %all-to-all-start = ((f32[16,1,6528]{2,1,0:T(1,128)}), f32[16,1,6528]{2,1,0:T(1,128)S(1)}, u32[]{:S(2)}, u32[]{:S(2)}) async-start(f32[16,1,6528]{2,1,0:T(1,128)} %shard_map.111), calls=%async_computation | async-start | bytes 835584 | tf_op jit(solution)/shard_map/all_to_all | solution.py:806
  9.6 0.0 copy-done
  9.6 0.0 copy-done.1
  9.6 0.0 copy-done.2
  9.7 0.0 copy-done.3
  9.7 0.0 copy-done.4
  9.7 0.0 copy-done.5
  9.7 0.0 copy-done.6
  9.7 0.3 %shard_map.112 = (f32[296,128]{1,0:T(8,128)S(1)}, f32[296,128]{1,0:T(8,128)S(1)}, f32[72,128]{1,0:T(8,128)S(1)}) custom-call(f32[240,128]{1,0:T(8,128)S(1)} %bitcast.10, f32[240,128]{1,0:T(8,128)S(1)} %bitcast.15, f32[240,128]{1,0:T(8,128)S(1)} %bitcast.27, f32[240,128]{1,0:T(8,128)S(1)} %bitcast.20, f32[240,128]{1,0:T(8,128)S(1)} %bitcast.24, ...), custom_call_target="tpu_custom_call" | custom-call | flops 1048576 | bytes 2097152 | tf_op jit(solution)/shard_map/pallas_call | solution.py:764
  10.0 0.3 %collective-permute-start = (f32[296,128]{1,0:T(8,128)S(1)}, f32[296,128]{1,0:T(8,128)S(1)}, u32[]{:S(2)}, u32[]{:S(2)}) collective-permute-start(f32[296,128]{1,0:T(8,128)S(1)} %get-tuple-element.21), channel_id=1, source_target_pairs={{0,4},{1,5},{2,6},{3,7},{4,0},{5,1},{6,2},{7,3},{8,12},{9,13},{10,... | collective-permute-start | bytes 454664 | tf_op jit(solution)/shard_map/ppermute | solution.py:809
  10.3 4.0 %collective-permute-start.1 = (f32[296,128]{1,0:T(8,128)S(1)}, f32[296,128]{1,0:T(8,128)S(1)}, u32[]{:S(2)}, u32[]{:S(2)}) collective-permute-start(f32[296,128]{1,0:T(8,128)S(1)} %get-tuple-element.22), channel_id=1, source_target_pairs={{4,8},{5,9},{6,10},{7,11},{8,4},{9,5},{10,6},{11,7},{12,16},{13,17... | collective-permute-start | bytes 454664 | tf_op jit(solution)/shard_map/ppermute | solution.py:810
  14.3 4.8 %collective-permute-start.3 = (f32[72,128]{1,0:T(8,128)S(1)}, f32[72,128]{1,0:T(8,128)S(1)}, u32[]{:S(2)}, u32[]{:S(2)}) collective-permute-start(f32[72,128]{1,0:T(8,128)S(1)} %get-tuple-element.23), channel_id=1, source_target_pairs={{1,2},{2,1},{5,6},{6,5},{9,10},{10,9},{13,14},{14,13},{17,18},{18,... | collective-permute-start | bytes 110600 | tf_op jit(solution)/shard_map/ppermute | solution.py:808
  19.1 0.1 collective-permute-start.2
  19.2 2.0 %collective-permute-done.3.x2_ref = f32[72,128]{1,0:T(8,128)S(1)} collective-permute-done((f32[72,128]{1,0:T(8,128)S(1)}, f32[72,128]{1,0:T(8,128)S(1)}, u32[]{:S(2)}, u32[]{:S(2)}) %collective-permute-start.3) | collective-permute-done | bytes 36896 | tf_op jit(solution)/shard_map/ppermute | solution.py:808
  21.2 0.0 collective-permute-done.2.x1_ref
  21.2 1.3 %shard_map.113 = (f32[256,128]{1,0:T(8,128)S(1)}, f32[256,128]{1,0:T(8,128)S(1)}, f32[256,128]{1,0:T(8,128)S(1)}) custom-call(f32[240,128]{1,0:T(8,128)S(1)} %bitcast.11, f32[240,128]{1,0:T(8,128)S(1)} %bitcast.16, f32[240,128]{1,0:T(8,128)S(1)} %bitcast.28, f32[240,128]{1,0:T(8,128)S(1)} %bitcast.31, f32[240,128]{1,0:T(8,128)S(1)} %bitcast.21, ...), custom_call_target="tpu_custom_call" | custom-call | flops 4194304 | bytes 2097152 | tf_op jit(solution)/shard_map/pallas_call | solution.py:764
  22.5 0.0 collective-permute-done.y1_ref
  22.5 0.9 %collective-permute-done.1.y2_ref = f32[296,128]{1,0:T(8,128)S(1)} collective-permute-done((f32[296,128]{1,0:T(8,128)S(1)}, f32[296,128]{1,0:T(8,128)S(1)}, u32[]{:S(2)}, u32[]{:S(2)}) %collective-permute-start.1) | collective-permute-done | bytes 151584 | tf_op jit(solution)/shard_map/ppermute | solution.py:810
  23.5 0.0 all-to-all-done.ga_ref
  23.5 1.5 %collective-permute-start.4 = (f32[16,1,6528]{2,1,0:T(1,128)S(1)}, f32[16,1,6528]{2,1,0:T(1,128)S(1)}, u32[]{:S(2)}, u32[]{:S(2)}) collective-permute-start(f32[16,1,6528]{2,1,0:T(1,128)S(1)} %all-to-all-done.ga_ref), channel_id=1, source_target_pairs={{0,1},{1,0},{2,3},{3,2},{4,5},{5,4},{6,7},{7,6},{8,9},{9,8},{10,11... | collective-permute-start | bytes 1253384 | tf_op jit(solution)/shard_map/ppermute | solution.py:819
  24.9 1.0 %shard_map.114 = (f32[240,128]{1,0:T(8,128)}, f32[256,128]{1,0:T(8,128)S(1)}, f32[1664,128]{1,0:T(8,128)S(1)}, f32[80,128]{1,0:T(8,128)S(1)}) custom-call(f32[240,128]{1,0:T(8,128)S(1)} %bitcast.12, f32[240,128]{1,0:T(8,128)S(1)} %bitcast.17, f32[240,128]{1,0:T(8,128)S(1)} %bitcast.29, f32[240,128]{1,0:T(8,128)S(1)} %bitcast.32, s32[8,128]{1,0:T(8,128)S(1)} %copy-done.6, ...), custom_call_target="tpu_custom_call" | custom-call | flops 4194304 | bytes 2097152 | tf_op jit(solution)/shard_map/pallas_call | solution.py:764
  25.9 0.4 %collective-permute-done.4.gb_ref = f32[16,1,6528]{2,1,0:T(1,128)S(1)} collective-permute-done((f32[16,1,6528]{2,1,0:T(1,128)S(1)}, f32[16,1,6528]{2,1,0:T(1,128)S(1)}, u32[]{:S(2)}, u32[]{:S(2)}) %collective-permute-start.4) | collective-permute-done | bytes 417824 | tf_op jit(solution)/shard_map/ppermute | solution.py:819
  26.3 3.0 %shard_map.115 = (f32[240,128]{1,0:T(8,128)}, f32[240,128]{1,0:T(8,128)}, f32[8,128]{1,0:T(8,128)}) custom-call(f32[240,128]{1,0:T(8,128)S(1)} %bitcast.13, f32[240,128]{1,0:T(8,128)S(1)} %bitcast.18, f32[240,128]{1,0:T(8,128)S(1)} %bitcast.22, f32[240,128]{1,0:T(8,128)S(1)} %bitcast.26, f32[16,1,6528]{2,1,0:T(1,128)S(1)} %all-to-all-done.ga_ref, ...), custom_call_target="tpu_custom_call" | custom-call | flops 8388608 | bytes 4194304 | tf_op jit(solution)/shard_map/pallas_call | solution.py:764
Async XLA Ops:
  2.8 6.9 %copy-start = (f32[30,8,128]{2,1,0:T(8,128)S(1)}, f32[30,8,128]{2,1,0:T(8,128)}, u32[]{:S(2)}) copy-start(f32[30,8,128]{2,1,0:T(8,128)} %param.8) | copy-start | bytes 368644
  2.8 6.9 %copy-start.1 = (f32[30,8,128]{2,1,0:T(8,128)S(1)}, f32[30,8,128]{2,1,0:T(8,128)}, u32[]{:S(2)}) copy-start(f32[30,8,128]{2,1,0:T(8,128)} %param.9) | copy-start | bytes 368644
  2.8 6.9 %copy-start.2 = (f32[30,8,128]{2,1,0:T(8,128)S(1)}, f32[30,8,128]{2,1,0:T(8,128)}, u32[]{:S(2)}) copy-start(f32[30,8,128]{2,1,0:T(8,128)} %param.12) | copy-start | bytes 368644
  2.8 6.9 %copy-start.3 = (f32[30,8,128]{2,1,0:T(8,128)S(1)}, f32[30,8,128]{2,1,0:T(8,128)}, u32[]{:S(2)}) copy-start(f32[30,8,128]{2,1,0:T(8,128)} %param.13) | copy-start | bytes 368644
  2.8 6.9 %copy-start.4 = (f32[30,8,128]{2,1,0:T(8,128)S(1)}, f32[30,8,128]{2,1,0:T(8,128)}, u32[]{:S(2)}) copy-start(f32[30,8,128]{2,1,0:T(8,128)} %param.10) | copy-start | bytes 368644
  2.8 6.9 %copy-start.5 = (f32[30,8,128]{2,1,0:T(8,128)S(1)}, f32[30,8,128]{2,1,0:T(8,128)}, u32[]{:S(2)}) copy-start(f32[30,8,128]{2,1,0:T(8,128)} %param.14) | copy-start | bytes 368644
  2.8 6.8 %copy-start.6 = (s32[8,128]{1,0:T(8,128)S(1)}, s32[8,128]{1,0:T(8,128)}, u32[]{:S(2)}) copy-start(s32[8,128]{1,0:T(8,128)} %count_ref.5) | copy-start | bytes 12292
  2.8 20.6 %all-to-all-start = ((f32[16,1,6528]{2,1,0:T(1,128)}), f32[16,1,6528]{2,1,0:T(1,128)S(1)}, u32[]{:S(2)}, u32[]{:S(2)}) async-start(f32[16,1,6528]{2,1,0:T(1,128)} %shard_map.111), calls=%async_computation | async-start | bytes 835584 | tf_op jit(solution)/shard_map/all_to_all | solution.py:806
  10.0 12.5 %collective-permute-start = (f32[296,128]{1,0:T(8,128)S(1)}, f32[296,128]{1,0:T(8,128)S(1)}, u32[]{:S(2)}, u32[]{:S(2)}) collective-permute-start(f32[296,128]{1,0:T(8,128)S(1)} %get-tuple-element.21), channel_id=1, source_target_pairs={{0,4},{1,5},{2,6},{3,7},{4,0},{5,1},{6,2},{7,3},{8,12},{9,13},{10,... | collective-permute-start | bytes 454664 | tf_op jit(solution)/shard_map/ppermute | solution.py:809
  10.3 13.1 %collective-permute-start.1 = (f32[296,128]{1,0:T(8,128)S(1)}, f32[296,128]{1,0:T(8,128)S(1)}, u32[]{:S(2)}, u32[]{:S(2)}) collective-permute-start(f32[296,128]{1,0:T(8,128)S(1)} %get-tuple-element.22), channel_id=1, source_target_pairs={{4,8},{5,9},{6,10},{7,11},{8,4},{9,5},{10,6},{11,7},{12,16},{13,17... | collective-permute-start | bytes 454664 | tf_op jit(solution)/shard_map/ppermute | solution.py:810
  14.3 6.9 %collective-permute-start.3 = (f32[72,128]{1,0:T(8,128)S(1)}, f32[72,128]{1,0:T(8,128)S(1)}, u32[]{:S(2)}, u32[]{:S(2)}) collective-permute-start(f32[72,128]{1,0:T(8,128)S(1)} %get-tuple-element.23), channel_id=1, source_target_pairs={{1,2},{2,1},{5,6},{6,5},{9,10},{10,9},{13,14},{14,13},{17,18},{18,... | collective-permute-start | bytes 110600 | tf_op jit(solution)/shard_map/ppermute | solution.py:808
  19.1 2.1 %collective-permute-start.2 = (f32[72,128]{1,0:T(8,128)S(1)}, f32[72,128]{1,0:T(8,128)S(1)}, u32[]{:S(2)}, u32[]{:S(2)}) collective-permute-start(f32[72,128]{1,0:T(8,128)S(1)} %get-tuple-element.23), channel_id=1, source_target_pairs={{0,1},{1,0},{2,3},{3,2},{4,5},{5,4},{6,7},{7,6},{8,9},{9,8},{10,11... | collective-permute-start | bytes 110600 | tf_op jit(solution)/shard_map/ppermute | solution.py:807
  23.5 2.8 %collective-permute-start.4 = (f32[16,1,6528]{2,1,0:T(1,128)S(1)}, f32[16,1,6528]{2,1,0:T(1,128)S(1)}, u32[]{:S(2)}, u32[]{:S(2)}) collective-permute-start(f32[16,1,6528]{2,1,0:T(1,128)S(1)} %all-to-all-done.ga_ref), channel_id=1, source_target_pairs={{0,1},{1,0},{2,3},{3,2},{4,5},{5,4},{6,7},{7,6},{8,9},{9,8},{10,11... | collective-permute-start | bytes 1253384 | tf_op jit(solution)/shard_map/ppermute | solution.py:819
